TPU v7x, 32 devices: a whole 2x2x4 slice. The times are simulated.
32 devices in a mesh: dp: 16 (over z, y, x), tensor: 2 (over core).
Axes of the slice: x: 2, y: 2, z: 4, core: 2. Of those that a mesh axis runs over, the one named last changes fastest.
Arguments:
- hidden_in: bfloat16 [8192, 2560], P('dp'), may hold values from -6 to 6
- adapter_ids: int32 [16, 3], P('dp'), may hold values from 0 to 7, all different within a row
- attn_gain: bfloat16 [2560], replicated, may hold values from 0.5 to 1.5
- mlp_gain: bfloat16 [2560], replicated, may hold values from 0.5 to 1.5
- w_query: bfloat16 [2560, 2560], P('dp', 'tensor'), may hold values from -0.125 to 0.125
- w_key: bfloat16 [2560, 640], P('dp', 'tensor'), may hold values from -0.125 to 0.125
- w_value: bfloat16 [2560, 640], P('dp', 'tensor'), may hold values from -0.125 to 0.125
- w_output: bfloat16 [2560, 2560], P('tensor', 'dp'), may hold values from -0.5 to 0.5
- w_gate: bfloat16 [2560, 7168], P('dp', 'tensor'), may hold values from -0.125 to 0.125
- w_up: bfloat16 [2560, 7168], P('dp', 'tensor'), may hold values from -0.125 to 0.125
- w_down: bfloat16 [7168, 2560], P('tensor', 'dp'), may hold values from -0.125 to 0.125
- in_query: bfloat16 [2560, 128], replicated, may hold values from -0.125 to 0.125
- second_query: bfloat16 [128, 2560], P(None, 'tensor'), may hold values from -0.25 to 0.25
- in_key: bfloat16 [2560, 128], replicated, may hold values from -0.125 to 0.125
- second_key: bfloat16 [128, 640], P(None, 'tensor'), may hold values from -0.25 to 0.25
- in_value: bfloat16 [2560, 128], replicated, may hold values from -0.125 to 0.125
- second_value: bfloat16 [128, 640], P(None, 'tensor'), may hold values from -0.25 to 0.25
- in_output: bfloat16 [2560, 128], P('tensor'), may hold values from -0.5 to 0.5
- second_output: bfloat16 [128, 2560], replicated, may hold values from -0.25 to 0.25
- in_gate: bfloat16 [2560, 128], replicated, may hold values from -0.125 to 0.125
- second_gate: bfloat16 [128, 7168], P(None, 'tensor'), may hold values from -0.25 to 0.25
- in_up: bfloat16 [2560, 128], replicated, may hold values from -0.125 to 0.125
- second_up: bfloat16 [128, 7168], P(None, 'tensor'), may hold values from -0.25 to 0.25
- in_down: bfloat16 [7168, 128], P('tensor'), may hold values from -0.125 to 0.125
- second_down: bfloat16 [128, 2560], replicated, may hold values from -0.25 to 0.25
- cotangent: bfloat16 [8192, 2560], P('dp'), may hold values from -6 to 6
Outputs:
- layer_output: bfloat16 [8192, 2560], P('dp')
- grad_in: bfloat16 [8192, 2560], P('dp')
- delta_in_query: float32 [2560, 128], replicated
- gradient_second_query: float32 [128, 2560], replicated
- delta_in_key: float32 [2560, 128], replicated
- gradient_second_key: float32 [128, 640], replicated
- delta_in_value: float32 [2560, 128], replicated
- gradient_second_value: float32 [128, 640], replicated
- delta_in_output: float32 [2560, 128], replicated
- gradient_second_output: float32 [128, 2560], replicated
- delta_in_gate: float32 [2560, 128], replicated
- gradient_second_gate: float32 [128, 7168], replicated
- delta_in_up: float32 [2560, 128], replicated
- gradient_second_up: float32 [128, 7168], replicated
- delta_in_down: float32 [7168, 128], replicated
- gradient_second_down: float32 [128, 2560], replicated
Inputs may be any that keep to these rules, and one draw needn't show every extreme that they name: `adapter_ids`: the 3 sequences of a group use different adapters, and every adapter is used by some sequence.
All inputs are finite; a program needn't handle non-finite values.
Results may differ from a plain program's by a relative error of at most 0.018.
Values may be sent and summed in bfloat16 or wider, within the bound.
No kernel may reach another device: no remote copies, remote signals or barrier semaphores. Data moves between devices by JAX's collectives and lax.ppermute only.
A program may use at most 256 MiB of HBM per device.

v0:
```python
import math

import jax
import jax.numpy as jnp
from jax import lax
from jax.sharding import PartitionSpec as P

HEAD_DIM = 80
RANK = 16
PROMPT = 256
CONT_LEN = 128


adapter_scale = 2.0
norm_eps = 1e-05
rope_base = 1000000.0


def rms_norm(values, gain_vec):
    return (
        values * lax.rsqrt(jnp.mean(values * values, axis=-1, keepdims=True) + norm_eps) * gain_vec
    )


def rotate(values, cos_table, sin_table):
    half_dim = values.shape[-1] // 2
    first_half = values[..., :half_dim]
    second_half = values[..., half_dim:]
    return jnp.concatenate(
        [
            first_half * cos_table - second_half * sin_table,
            second_half * cos_table + first_half * sin_table,
        ],
        axis=-1,
    )


def matrix_product(left, right):
    return jnp.dot(left, right, preferred_element_type=jnp.float32)


def product_with_transpose(left, right):
    return jnp.einsum("ij,kj->ik", left, right, preferred_element_type=jnp.float32)


def transpose_then_product(left, right):
    return jnp.einsum("ij,ik->jk", left, right, preferred_element_type=jnp.float32)


def swiglu(gate_vals, up_vals):
    return jax.nn.silu(gate_vals) * up_vals


def branch_total(base_part, low_part):
    return lax.psum((base_part, low_part), "tensor")


def branch_back(base_part, low_part):
    return lax.psum((base_part, low_part), "tensor")


def attend_scores(query_h, key_h, visible, inv_sqrt):
    scores = (
        jnp.einsum("rgd,sd->grs", query_h, key_h, preferred_element_type=jnp.float32) * inv_sqrt
    )
    return jnp.where(visible[None], scores, -1e30)


def attend_forward(query_h, key_h, value_h, visible, inv_sqrt):
    scores = attend_scores(query_h, key_h, visible, inv_sqrt)
    top_score = jnp.max(scores, axis=-1, keepdims=True)
    expo_vals = jnp.exp(scores - top_score)
    row_total = jnp.sum(expo_vals, axis=-1, keepdims=True)
    attn_prob = (expo_vals / row_total).astype(jnp.bfloat16)
    mixed = jnp.einsum("grs,sd->rgd", attn_prob, value_h, preferred_element_type=jnp.float32)
    return (mixed, top_score[..., 0] + jnp.log(row_total[..., 0]))


def attend_backward(query_h, key_h, value_h, grad_h, log_total, visible, inv_sqrt):
    scores = attend_scores(query_h, key_h, visible, inv_sqrt)
    attn_prob = jnp.exp(scores - log_total[..., None])
    gradient_value = jnp.einsum(
        "grs,rgd->sd", attn_prob.astype(jnp.bfloat16), grad_h, preferred_element_type=jnp.float32
    )
    grad_prob = jnp.einsum("rgd,sd->grs", grad_h, value_h, preferred_element_type=jnp.float32)
    row_term = jnp.sum(attn_prob * grad_prob, axis=-1, keepdims=True)
    grad_score = (attn_prob * (grad_prob - row_term)).astype(jnp.bfloat16)
    gradient_query = (
        jnp.einsum("grs,sd->rgd", grad_score, key_h, preferred_element_type=jnp.float32) * inv_sqrt
    )
    gradient_key = (
        jnp.einsum("grs,rgd->sd", grad_score, query_h, preferred_element_type=jnp.float32)
        * inv_sqrt
    )
    return (gradient_query, gradient_key, gradient_value)


def body(
    hidden_in,
    adapter_ids,
    attn_gain,
    mlp_gain,
    w_query,
    w_key,
    w_value,
    w_output,
    w_gate,
    w_up,
    w_down,
    in_query,
    second_query,
    in_key,
    second_key,
    in_value,
    second_value,
    in_output,
    second_output,
    in_gate,
    second_gate,
    in_up,
    second_up,
    in_down,
    second_down,
    cotangent,
):
    num_rows = hidden_in.shape[0]
    local_heads = w_query.shape[1] // HEAD_DIM
    local_kv = w_key.shape[1] // HEAD_DIM
    group_size = local_heads // local_kv
    rank_cols = in_query.shape[1]
    inv_sqrt = 1.0 / math.sqrt(HEAD_DIM)
    row_index = lax.iota(jnp.int32, num_rows)
    is_later = row_index >= PROMPT
    seq_of = jnp.where(is_later, 1 + (row_index - PROMPT) // CONT_LEN, 0)
    position = jnp.where(is_later, PROMPT + (row_index - PROMPT) % CONT_LEN, row_index)
    visible = (row_index[None, :] <= row_index[:, None]) & (
        (row_index[None, :] < PROMPT) | (seq_of[None, :] == seq_of[:, None])
    )
    seq_ids = lax.iota(jnp.int32, adapter_ids.shape[1])
    row_adapter = jnp.sum(
        jnp.where(seq_of[:, None] == seq_ids[None, :], adapter_ids[0][None, :], 0), axis=1
    )
    select_adapter = (
        lax.iota(jnp.int32, rank_cols)[None, :] // RANK == row_adapter[:, None]
    ).astype(jnp.float32)
    select_three = jnp.concatenate([select_adapter, select_adapter, select_adapter], axis=1)
    select_two = jnp.concatenate([select_adapter, select_adapter], axis=1)
    inv_freq = rope_base ** (-2.0 * lax.iota(jnp.float32, HEAD_DIM // 2) / HEAD_DIM)
    angles = position.astype(jnp.float32)[:, None] * inv_freq[None, :]
    cos_table = jnp.cos(angles)[:, None, :]
    sin_table = jnp.sin(angles)[:, None, :]
    attn_in = jnp.concatenate([in_query, in_key, in_value], axis=1)
    mlp_in = jnp.concatenate([in_gate, in_up], axis=1)
    attn_gain_f = attn_gain.astype(jnp.float32)
    mlp_gain_f = mlp_gain.astype(jnp.float32)
    complete_query, complete_key, complete_value, complete_gate, complete_up = (
        lax.all_gather(w_query, "dp", axis=0, tiled=True),
        lax.all_gather(w_key, "dp", axis=0, tiled=True),
        lax.all_gather(w_value, "dp", axis=0, tiled=True),
        lax.all_gather(w_gate, "dp", axis=0, tiled=True),
        lax.all_gather(w_up, "dp", axis=0, tiled=True),
    )
    full_output, full_down = (
        lax.all_gather(w_output, "dp", axis=1, tiled=True),
        lax.all_gather(w_down, "dp", axis=1, tiled=True),
    )
    hidden_state_wide = hidden_in.astype(jnp.float32)
    normalized_attention_input = rms_norm(hidden_state_wide, attn_gain_f).astype(jnp.bfloat16)
    low_attn = (matrix_product(normalized_attention_input, attn_in) * select_three).astype(
        jnp.bfloat16
    )
    reduced_query = low_attn[:, :rank_cols]
    reduced_key = low_attn[:, rank_cols : 2 * rank_cols]
    reduced_value = low_attn[:, 2 * rank_cols :]
    query_unrotated = matrix_product(
        normalized_attention_input, complete_query
    ) + adapter_scale * matrix_product(reduced_query, second_query)
    key_unrotated = matrix_product(
        normalized_attention_input, complete_key
    ) + adapter_scale * matrix_product(reduced_key, second_key)
    value_unprojected = matrix_product(
        normalized_attention_input, complete_value
    ) + adapter_scale * matrix_product(reduced_value, second_value)
    query_rot = rotate(
        query_unrotated.reshape(num_rows, local_heads, HEAD_DIM), cos_table, sin_table
    ).astype(jnp.bfloat16)
    key_rot = rotate(
        key_unrotated.reshape(num_rows, local_kv, HEAD_DIM), cos_table, sin_table
    ).astype(jnp.bfloat16)
    value_reduced_rows = value_unprojected.astype(jnp.bfloat16).reshape(
        num_rows, local_kv, HEAD_DIM
    )
    query_stack = jnp.transpose(
        query_rot.reshape(num_rows, local_kv, group_size, HEAD_DIM), (1, 0, 2, 3)
    )
    key_stack = jnp.transpose(key_rot, (1, 0, 2))
    value_stack = jnp.transpose(value_reduced_rows, (1, 0, 2))

    def forward_head(pieces):
        return attend_forward(pieces[0], pieces[1], pieces[2], visible, inv_sqrt)

    mixed_stack, log_totals = lax.map(forward_head, (query_stack, key_stack, value_stack))
    attended_values = (
        jnp.transpose(mixed_stack, (1, 0, 2, 3))
        .reshape(num_rows, local_heads * HEAD_DIM)
        .astype(jnp.bfloat16)
    )
    attention_frozen, attn_low = branch_total(
        matrix_product(attended_values, full_output), matrix_product(attended_values, in_output)
    )
    reduced_output = (attn_low * select_adapter).astype(jnp.bfloat16)
    middle_activation = (
        hidden_state_wide
        + attention_frozen
        + adapter_scale * matrix_product(reduced_output, second_output)
    )
    normalized_feedforward_input = rms_norm(middle_activation, mlp_gain_f).astype(jnp.bfloat16)
    low_mlp = (matrix_product(normalized_feedforward_input, mlp_in) * select_two).astype(
        jnp.bfloat16
    )
    reduced_gate = low_mlp[:, :rank_cols]
    reduced_up = low_mlp[:, rank_cols:]
    gate_preactivation = matrix_product(
        normalized_feedforward_input, complete_gate
    ) + adapter_scale * matrix_product(reduced_gate, second_gate)
    up_preactivation = matrix_product(
        normalized_feedforward_input, complete_up
    ) + adapter_scale * matrix_product(reduced_up, second_up)
    active_rows = swiglu(gate_preactivation, up_preactivation).astype(jnp.bfloat16)
    feedforward_frozen, mlp_low = branch_total(
        matrix_product(active_rows, full_down), matrix_product(active_rows, in_down)
    )
    reduced_down = (mlp_low * select_adapter).astype(jnp.bfloat16)
    layer_output = (
        middle_activation
        + feedforward_frozen
        + adapter_scale * matrix_product(reduced_down, second_down)
    ).astype(jnp.bfloat16)
    complete_query, complete_key, complete_value, complete_gate, complete_up = (
        lax.all_gather(w_query, "dp", axis=0, tiled=True),
        lax.all_gather(w_key, "dp", axis=0, tiled=True),
        lax.all_gather(w_value, "dp", axis=0, tiled=True),
        lax.all_gather(w_gate, "dp", axis=0, tiled=True),
        lax.all_gather(w_up, "dp", axis=0, tiled=True),
    )
    full_output, full_down = (
        lax.all_gather(w_output, "dp", axis=1, tiled=True),
        lax.all_gather(w_down, "dp", axis=1, tiled=True),
    )
    gradient_reduced_down = (
        adapter_scale * product_with_transpose(cotangent, second_down) * select_adapter
    ).astype(jnp.bfloat16)
    gradient_second_down = adapter_scale * transpose_then_product(reduced_down, cotangent)
    grad_active = product_with_transpose(cotangent, full_down) + product_with_transpose(
        gradient_reduced_down, in_down
    )
    delta_in_down = transpose_then_product(active_rows, gradient_reduced_down)
    swiglu_pull = jax.vjp(swiglu, gate_preactivation, up_preactivation)[1]
    grad_gate_f, grad_up_f = swiglu_pull(grad_active)
    gradient_gate = grad_gate_f.astype(jnp.bfloat16)
    gradient_up = grad_up_f.astype(jnp.bfloat16)
    gradient_second_gate = adapter_scale * transpose_then_product(reduced_gate, gradient_gate)
    gradient_second_up = adapter_scale * transpose_then_product(reduced_up, gradient_up)
    mlp_back_base, mlp_back_low = branch_back(
        product_with_transpose(gradient_gate, complete_gate)
        + product_with_transpose(gradient_up, complete_up),
        adapter_scale
        * jnp.concatenate(
            [
                product_with_transpose(gradient_gate, second_gate),
                product_with_transpose(gradient_up, second_up),
            ],
            axis=1,
        ),
    )
    grad_low_mlp = (mlp_back_low * select_two).astype(jnp.bfloat16)
    grad_normed_m = mlp_back_base + product_with_transpose(grad_low_mlp, mlp_in)
    delta_mlp_in = transpose_then_product(normalized_feedforward_input, grad_low_mlp)
    delta_in_gate = delta_mlp_in[:, :rank_cols]
    delta_in_up = delta_mlp_in[:, rank_cols:]

    def norm_mlp(values):
        return rms_norm(values, mlp_gain_f)

    grad_middle = (
        cotangent.astype(jnp.float32) + jax.vjp(norm_mlp, middle_activation)[1](grad_normed_m)[0]
    )
    gradient_adapter_branch = grad_middle.astype(jnp.bfloat16)
    gradient_reduced_output = (
        adapter_scale
        * product_with_transpose(gradient_adapter_branch, second_output)
        * select_adapter
    ).astype(jnp.bfloat16)
    gradient_second_output = adapter_scale * transpose_then_product(
        reduced_output, gradient_adapter_branch
    )
    grad_attended = (
        product_with_transpose(gradient_adapter_branch, full_output)
        + product_with_transpose(gradient_reduced_output, in_output)
    ).astype(jnp.bfloat16)
    delta_in_output = transpose_then_product(attended_values, gradient_reduced_output)
    grad_stack = jnp.transpose(
        grad_attended.reshape(num_rows, local_kv, group_size, HEAD_DIM), (1, 0, 2, 3)
    )

    def backward_head(pieces):
        return attend_backward(
            pieces[0], pieces[1], pieces[2], pieces[3], pieces[4], visible, inv_sqrt
        )

    grad_q_stack, grad_k_stack, grad_v_stack = lax.map(
        backward_head, (query_stack, key_stack, value_stack, grad_stack, log_totals)
    )
    grad_query_rot = jnp.transpose(grad_q_stack, (1, 0, 2, 3)).reshape(
        num_rows, local_heads, HEAD_DIM
    )
    gradient_query = (
        rotate(grad_query_rot, cos_table, -sin_table)
        .reshape(num_rows, local_heads * HEAD_DIM)
        .astype(jnp.bfloat16)
    )
    gradient_key = (
        rotate(jnp.transpose(grad_k_stack, (1, 0, 2)), cos_table, -sin_table)
        .reshape(num_rows, local_kv * HEAD_DIM)
        .astype(jnp.bfloat16)
    )
    gradient_value = (
        jnp.transpose(grad_v_stack, (1, 0, 2))
        .reshape(num_rows, local_kv * HEAD_DIM)
        .astype(jnp.bfloat16)
    )
    gradient_second_query = adapter_scale * transpose_then_product(reduced_query, gradient_query)
    gradient_second_key = adapter_scale * transpose_then_product(reduced_key, gradient_key)
    gradient_second_value = adapter_scale * transpose_then_product(reduced_value, gradient_value)
    attn_back_base, attn_back_low = branch_back(
        product_with_transpose(gradient_query, complete_query)
        + product_with_transpose(gradient_key, complete_key)
        + product_with_transpose(gradient_value, complete_value),
        adapter_scale
        * jnp.concatenate(
            [
                product_with_transpose(gradient_query, second_query),
                product_with_transpose(gradient_key, second_key),
                product_with_transpose(gradient_value, second_value),
            ],
            axis=1,
        ),
    )
    grad_low_attn = (attn_back_low * select_three).astype(jnp.bfloat16)
    grad_normed_a = attn_back_base + product_with_transpose(grad_low_attn, attn_in)
    delta_attn_in = transpose_then_product(normalized_attention_input, grad_low_attn)
    delta_in_query = delta_attn_in[:, :rank_cols]
    delta_in_key = delta_attn_in[:, rank_cols : 2 * rank_cols]
    delta_in_value = delta_attn_in[:, 2 * rank_cols :]

    def norm_attn(values):
        return rms_norm(values, attn_gain_f)

    grad_in = (grad_middle + jax.vjp(norm_attn, hidden_state_wide)[1](grad_normed_a)[0]).astype(
        jnp.bfloat16
    )
    (
        delta_in_query,
        gradient_second_query,
        delta_in_key,
        gradient_second_key,
        delta_in_value,
        gradient_second_value,
        delta_in_output,
        gradient_second_output,
        delta_in_gate,
        gradient_second_gate,
        delta_in_up,
        gradient_second_up,
        delta_in_down,
        gradient_second_down,
    ) = lax.psum(
        (
            delta_in_query,
            gradient_second_query,
            delta_in_key,
            gradient_second_key,
            delta_in_value,
            gradient_second_value,
            delta_in_output,
            gradient_second_output,
            delta_in_gate,
            gradient_second_gate,
            delta_in_up,
            gradient_second_up,
            delta_in_down,
            gradient_second_down,
        ),
        "dp",
    )
    (
        gradient_second_query,
        gradient_second_key,
        gradient_second_value,
        gradient_second_gate,
        gradient_second_up,
        delta_in_output,
        delta_in_down,
    ) = (
        lax.all_gather(
            gradient_second_query.astype(jnp.bfloat16), "tensor", axis=1, tiled=True
        ).astype(gradient_second_query.dtype),
        lax.all_gather(
            gradient_second_key.astype(jnp.bfloat16), "tensor", axis=1, tiled=True
        ).astype(gradient_second_key.dtype),
        lax.all_gather(
            gradient_second_value.astype(jnp.bfloat16), "tensor", axis=1, tiled=True
        ).astype(gradient_second_value.dtype),
        lax.all_gather(
            gradient_second_gate.astype(jnp.bfloat16), "tensor", axis=1, tiled=True
        ).astype(gradient_second_gate.dtype),
        lax.all_gather(
            gradient_second_up.astype(jnp.bfloat16), "tensor", axis=1, tiled=True
        ).astype(gradient_second_up.dtype),
        lax.all_gather(delta_in_output.astype(jnp.bfloat16), "tensor", axis=0, tiled=True).astype(
            delta_in_output.dtype
        ),
        lax.all_gather(delta_in_down.astype(jnp.bfloat16), "tensor", axis=0, tiled=True).astype(
            delta_in_down.dtype
        ),
    )
    return (
        layer_output,
        grad_in,
        delta_in_query,
        gradient_second_query,
        delta_in_key,
        gradient_second_key,
        delta_in_value,
        gradient_second_value,
        delta_in_output,
        gradient_second_output,
        delta_in_gate,
        gradient_second_gate,
        delta_in_up,
        gradient_second_up,
        delta_in_down,
        gradient_second_down,
    )


def solution(mesh):
    return jax.shard_map(
        body,
        mesh=mesh,
        in_specs=(
            P("dp", None),
            P("dp", None),
            P(),
            P(),
            P("dp", "tensor"),
            P("dp", "tensor"),
            P("dp", "tensor"),
            P("tensor", "dp"),
            P("dp", "tensor"),
            P("dp", "tensor"),
            P("tensor", "dp"),
            P(),
            P(None, "tensor"),
            P(),
            P(None, "tensor"),
            P(),
            P(None, "tensor"),
            P("tensor", None),
            P(),
            P(),
            P(None, "tensor"),
            P(),
            P(None, "tensor"),
            P("tensor", None),
            P(),
            P("dp", None),
        ),
        out_specs=(
            P("dp", None),
            P("dp", None),
            P(),
            P(),
            P(),
            P(),
            P(),
            P(),
            P(),
            P(),
            P(),
            P(),
            P(),
            P(),
            P(),
            P(),
        ),
        check_vma=False,
    )
```

profile of v0, /device:TPU:0, one launch (start us, length us, event | category | flops | bytes accessed | tf_op | source)
XLA Modules:
  0.0 1830.6 jit_solution(17379364901564966672)
XLA Ops:
  29.9 43.7 %all-gather.13.cloned.1.call-done = bf16[2560,320]{1,0:T(8,128)(2,1)} async-done(((bf16[160,320]{1,0:T(8,128)(2,1)}), bf16[2560,320]{1,0:T(8,128)(2,1)}) %all-gather.13.cloned.1.call-update) | async-done | bytes 1638416 | tf_op jit(solution)/shard_map/all_gather | solution.py:158
  78.5 56.6 %all-gather.11.cloned.1.call-done = bf16[2560,320]{1,0:T(8,128)(2,1)} async-done(((bf16[160,320]{1,0:T(8,128)(2,1)}), bf16[2560,320]{1,0:T(8,128)(2,1)}) %all-gather.11.cloned.1.call-update) | async-done | bytes 1638416 | tf_op jit(solution)/shard_map/all_gather | solution.py:159
  139.9 93.3 %all-gather.15.cloned.1.call-done = bf16[2560,1280]{1,0:T(8,128)(2,1)} async-done(((bf16[160,1280]{1,0:T(8,128)(2,1)}), bf16[2560,1280]{1,0:T(8,128)(2,1)}) %all-gather.15.cloned.1.call-update) | async-done | bytes 6553616 | tf_op jit(solution)/shard_map/all_gather | solution.py:157
  233.2 6.5 fusion.136
  249.4 26.8 %while.30 = (s32[]{:T(128)}, bf16[4,512,4,80]{1,3,2,0:T(8,128)(2,1)}, f32[4,4,512]{2,1,0:T(4,128)}, bf16[4,512,80]{1,2,0:T(8,128)(2,1)}, bf16[4,512,80]{1,2,0:T(...) while((s32[]{:T(128)}, ...), condition=%wide.region_5.6_spmd.clone.clone, body=%wide.region_2.5_spmd.clone.sunk.clone | while | flops 349173760 | bytes 14849109 | solution.py:202
  276.2 54.5 %all-gather.17.cloned.1.call-done = bf16[1280,2560]{0,1:T(8,128)(2,1)} async-done(((bf16[1280,160]{0,1:T(8,128)(2,1)}), bf16[1280,2560]{0,1:T(8,128)(2,1)}) %all-gather.17.cloned.1.call-update) | async-done | bytes 6553616 | tf_op jit(solution)/shard_map/all_gather | solution.py:164
  330.7 9.2 fusion.145
  360.4 8.1 all-reduce.12.cloned.1.call-done
  386.6 192.5 %all-gather.21.cloned.1.call-done = bf16[2560,3584]{1,0:T(8,128)(2,1)} async-done(((bf16[160,3584]{1,0:T(8,128)(2,1)}), bf16[2560,3584]{1,0:T(8,128)(2,1)}) %all-gather.21.cloned.1.call-update) | async-done | bytes 18350096 | tf_op jit(solution)/shard_map/all_gather | solution.py:161
  579.1 16.9 multiply_add_fusion
  596.0 190.9 %all-gather.19.cloned.1.call-done = bf16[2560,3584]{1,0:T(8,128)(2,1)} async-done(((bf16[160,3584]{1,0:T(8,128)(2,1)}), bf16[2560,3584]{1,0:T(8,128)(2,1)}) %all-gather.19.cloned.1.call-update) | async-done | bytes 18350096 | tf_op jit(solution)/shard_map/all_gather | solution.py:160
  786.9 16.3 multiply_add_fusion.1
  803.2 191.5 %all-gather.23.cloned.1.call-done = bf16[3584,2560]{0,1:T(8,128)(2,1)} async-done(((bf16[3584,160]{0,1:T(8,128)(2,1)}), bf16[3584,2560]{0,1:T(8,128)(2,1)}) %all-gather.23.cloned.1.call-update) | async-done | bytes 18350096 | tf_op jit(solution)/shard_map/all_gather | solution.py:165
  994.6 23.3 %multiply_convert_fusion = (bf16[512,3584]{1,0:T(8,128)(2,1)}, bf16[512,3584]{1,0:T(8,128)(2,1)}, bf16[512,3584]{1,0:T(8,128)(2,1)}) fusion(f32[512,3584]{1,0:T(8,128)} %multiply_add_fusion.1, f32[512,3584]{1,0:T(8,128)} %multiply_add_fusion, f32[512,3584]{1,0:T(8,128)} %fusion.149, bf16[512,2560]{1,0:T(8,128)(2,1)} %param.55, ...), kind=kOutput, calls=%fused_computation.81 | convolution fusion | flops 9426436096 | bytes 54001664 | tf_op jit(solution)/shard_map/ij,kj->ik/dot_general | solution.py:43
  1023.3 15.0 fusion.150
  1038.3 15.8 convolution_add_fusion.1
  1054.3 16.6 fusion.147
  1070.9 12.7 all-reduce.18.cloned.1.call-done
  1083.7 5.7 multiply_reduce_fusion
  1094.2 7.5 fusion.123
  1105.0 40.6 %while.31 = (s32[]{:T(128)}, f32[4,512,4,80]{1,3,2,0:T(8,128)}, f32[4,512,80]{1,2,0:T(8,128)}, bf16[4,512,80]{1,2,0:T(8,128)(2,1)}, bf16[4,512,80]{1,2,0:T(8,128...) while((s32[]{:T(128)}, f32[4,512,4,80]{1,3,2,0:T(8,128)}, ...), condition=%wide.region_16.17_spmd.clone.clone, body=%wide.region_14.16_spmd.clone.sunk.clone | while | flops 855840768 | bytes 35110512 | solution.py:311
  1178.6 299.8 %all-reduce.20 = (bf16[128,320]{0,1:T(8,128)(2,1)}, bf16[128,320]{0,1:T(8,128)(2,1)}, bf16[128,1280]{1,0:T(8,128)(2,1)}, bf16[1280,128]{1,0:T(8,128)(2,1)}, bf16...) all-reduce(f32[128,320]{0,1:T(8,128)S(1)} %copy-done.49, ...), channel_id=1, replica_groups=mesh['dp'=16,'tensor'=2] {'dp'}, use_global_device_ids=true, to_apply=%region_23.24 | all-reduce | flops 1785856 | bytes 10715136 | tf_op jit(solution)/shard_map/psum | solution.py:377
  1529.7 5.9 fusion.76
  1541.1 272.3 %all-reduce.14.cloned.1.call-done = (f32[2560,128]{1,0:T(8,128)}, f32[2560,128]{1,0:T(8,128)}, f32[2560,128]{1,0:T(8,128)}, f32[128,2560]{1,0:T(8,128)}, f32[256...) async-done(((f32[2560,128]{1,0:T(8,128)}, f32[2560,128]{1,0:T(8,128)}, f32[2560,128]{1,0:T(8,128)}, f32[128,2560]{1,0:T(8,128)}, f32[2560,128]{1,0:T(8,128)}, ...) | async-done | bytes 9175056 | tf_op jit(solution)/shard_map/psum | solution.py:377
  (355 shorter events, 260.4 us)
Async XLA Ops:
  7.2 375.4 %copy-start = (bf16[128,3584]{1,0:T(8,128)(2,1)S(1)}, bf16[128,3584]{1,0:T(8,128)(2,1)}, u32[]{:S(2)}) copy-start(bf16[128,3584]{1,0:T(8,128)(2,1)} %param.50) | copy-start | bytes 2752516
  7.2 66.4 %all-gather.13.cloned.1.call-start = ((), (), s32[]{:S(2)}) async-start(), calls=%async_computation.1 | async-start | bytes 2088960 | tf_op jit(solution)/shard_map/all_gather | solution.py:158
  7.9 127.2 %all-gather.11.cloned.1.call-start = ((), (), s32[]{:S(2)}) async-start(), calls=%async_computation | async-start | bytes 2088960 | tf_op jit(solution)/shard_map/all_gather | solution.py:159
  8.7 224.5 %all-gather.15.cloned.1.call-start = ((), (), s32[]{:S(2)}) async-start(), calls=%async_computation.2 | async-start | bytes 6963200 | tf_op jit(solution)/shard_map/all_gather | solution.py:157
  9.4 321.3 %all-gather.17.cloned.1.call-start = ((), (), s32[]{:S(2)}) async-start(), calls=%async_computation.3 | async-start | bytes 6963200 | tf_op jit(solution)/shard_map/all_gather | solution.py:164
  10.0 358.5 %all-reduce.12.cloned.1.call-start = ((), (), s32[]{:S(2)}) async-start(), calls=%async_computation.4 | async-start | bytes 10485760 | tf_op jit(solution)/shard_map/psum | solution.py:55
  20.0 348.5 %copy-start.60 = (s32[512]{0:T(512)}, s32[512]{0:T(512)S(1)}, u32[]{:S(2)}) copy-start(s32[512]{0:T(512)S(1)} %select_reduce_fusion) | copy-start | bytes 6148
  29.9 105.3 %copy-start.75 = (f32[512]{0:T(512)S(1)}, f32[512]{0:T(512)}, u32[]{:S(2)}) copy-start(f32[512]{0:T(512)} %fusion.118) | copy-start | bytes 6148
  276.2 63.7 %copy-start.44 = (s32[512]{0:T(512)}, s32[512]{0:T(512)S(1)}, u32[]{:S(2)}) copy-start(s32[512]{0:T(512)S(1)} %get-tuple-element.619) | copy-start | bytes 6148
  276.2 63.7 %copy-start.64 = (pred[512]{0:T(512)(128)(4,1)}, pred[512]{0:T(512)(128)(4,1)S(1)}, u32[]{:S(2)}) copy-start(pred[512]{0:T(512)(128)(4,1)S(1)} %get-tuple-element.635) | copy-start | bytes 1540
  340.0 239.1 %all-gather.21.cloned.1.call-start = ((), (), s32[]{:S(2)}) async-start(), calls=%async_computation.6 | async-start | bytes 19496960 | tf_op jit(solution)/shard_map/all_gather | solution.py:161
  340.6 446.3 %all-gather.19.cloned.1.call-start = ((), (), s32[]{:S(2)}) async-start(), calls=%async_computation.5 | async-start | bytes 19496960 | tf_op jit(solution)/shard_map/all_gather | solution.py:160
  341.3 653.3 %all-gather.23.cloned.1.call-start = ((), (), s32[]{:S(2)}) async-start(), calls=%async_computation.7 | async-start | bytes 19496960 | tf_op jit(solution)/shard_map/all_gather | solution.py:165
  342.1 741.6 %all-reduce.18.cloned.1.call-start = ((), (), s32[]{:S(2)}) async-start(), calls=%async_computation.13 | async-start | bytes 11534336 | tf_op jit(solution)/shard_map/psum | solution.py:59
  342.9 30.2 %copy-start.58 = (f32[2560]{0:T(1024)}, f32[2560]{0:T(1024)S(1)}, u32[]{:S(2)}) copy-start(f32[2560]{0:T(1024)S(1)} %convert_element_type.197) | copy-start | bytes 30724
  375.0 411.9 %copy-start.8 = (bf16[512,2560]{1,0:T(8,128)(2,1)}, bf16[512,2560]{1,0:T(8,128)(2,1)S(1)}, u32[]{:S(2)}) copy-start(bf16[512,2560]{1,0:T(8,128)(2,1)S(1)} %multiply_convert_fusion.2) | copy-start | bytes 7864324
  1054.2 445.2 %all-reduce.16.cloned.1.call-start = ((), (), s32[]{:S(2)}) async-start(), calls=%async_computation.12 | async-start | bytes 22544384 | tf_op jit(solution)/shard_map/psum | solution.py:55
  1054.3 29.4 %copy-start.18 = (f32[512,128]{1,0:T(8,128)S(1)}, f32[512,128]{1,0:T(8,128)}, u32[]{:S(2)}) copy-start(f32[512,128]{1,0:T(8,128)} %copy-done.16) | copy-start | bytes 786436
  1054.3 29.4 %copy-start.59 = (f32[2560]{0:T(1024)S(1)}, f32[2560]{0:T(1024)}, u32[]{:S(2)}) copy-start(f32[2560]{0:T(1024)} %copy-done.58) | copy-start | bytes 30724
  1163.2 355.2 %all-gather.25.cloned.1.call-start = ((), (), s32[]{:S(2)}) async-start(), calls=%async_computation.8 | async-start | bytes 2752512 | tf_op jit(solution)/shard_map/all_gather | solution.py:414
  1178.6 300.4 %copy-start.20 = (bf16[3584,128]{1,0:T(8,128)(2,1)S(1)}, bf16[3584,128]{1,0:T(8,128)(2,1)}, u32[]{:S(2)}) copy-start(bf16[3584,128]{1,0:T(8,128)(2,1)} %param.53) | copy-start | bytes 2752516
  1478.4 43.8 %all-gather.27.cloned.1.call-start = ((), (), s32[]{:S(2)}) async-start(), calls=%async_computation.9 | async-start | bytes 2752512 | tf_op jit(solution)/shard_map/all_gather | solution.py:417
  1478.9 46.9 %all-gather.29.cloned.1.call-start = ((), (), s32[]{:S(2)}) async-start(), calls=%async_computation.10 | async-start | bytes 2752512 | tf_op jit(solution)/shard_map/all_gather | solution.py:423
  1492.1 321.3 %all-reduce.14.cloned.1.call-start = ((), (), s32[]{:S(2)}) async-start(), calls=%async_computation.11 | async-start | bytes 18350080 | tf_op jit(solution)/shard_map/psum | solution.py:377
  (75 other events, 368.5 us)
Sparse Core Ops, SparseCore 0:
  10.8 62.7 all-gather.12
  76.4 58.6 all-gather.10
  137.8 95.3 all-gather.14
  235.8 94.9 all-gather.16
  340.1 28.3 all-reduce.11
  371.4 207.6 all-gather.20
  582.1 204.6 all-gather.18
  789.9 204.6 all-gather.22
  1054.3 29.3 all-reduce.17
  1163.3 45.5 all-reduce.15
  1478.5 19.7 all-gather.24
  1499.8 11.4 all-gather.26
  1512.9 11.2 all-gather.28
  1532.7 280.6 all-reduce.13
where the time goes:
time: 1840 us; the launch traced here: 1830 us
  waiting for transfers between devices  1120 us (61%)
  blocking collectives  320 us (17%)
  matrix products  285 us (15%)
  other arithmetic  53.4 us (3%)
  local copies, waits for them, and re-layouts  35.5 us (2%)
    psum x1, blocking collectives, body(): lax.psum((delta_in_query, gradient_second_query, delta_in_key, gradient_s...  300 us
    psum x1, waiting for transfers between devices, body(): lax.psum((delta_in_query, gradient_second_query, delta_in_key, gradient_s...  272 us
    all_gather x1, waiting for transfers between devices, body(): lax.all_gather(w_up, 'dp', axis=0, tiled=True)  192 us
    all_gather x1, waiting for transfers between devices, body(): lax.all_gather(w_down, 'dp', axis=1, tiled=True)  191 us
    all_gather x1, waiting for transfers between devices, body(): lax.all_gather(w_gate, 'dp', axis=0, tiled=True)  191 us
    dot_general x18, matrix products, matrix_product(): return jnp.dot(left, right, preferred_element_type=jnp.float32)  106 us
    dot_general x18, matrix products, product_with_transpose(): jnp.einsum('ij,kj->ik', left, right, preferred_element_type=jnp.float32)  101 us
    all_gather x1, waiting for transfers between devices, body(): lax.all_gather(w_query, 'dp', axis=0, tiled=True)  93.3 us
  transfers between devices with their start and end apart: 14, of which 10 were waited for; matrix products, arithmetic and copies ran while one was open for 12% of the time, Pallas kernels for 0%

commit v1 on v0

v1 whole, which is shorter than its diff:
```python
import math

import jax
import jax.numpy as jnp
from jax import lax
from jax.experimental import pallas as pl
from jax.experimental.pallas import tpu as pltpu
from jax.sharding import PartitionSpec as P

HEAD_DIM = 80
RANK = 16
PROMPT = 256
CONT_LEN = 128
WIDTH = 256

adapter_scale = 2.0
norm_eps = 1e-05
rope_base = 1000000.0

BF = jnp.bfloat16
F32 = jnp.float32

LAG = 2
STEP_FLOPS = 20_000_000_000
NORMED_AFTER = 4
EXCHANGES = ((0, 1), (2, 3), (4, 5, 6))
EXCHANGE_PRIORITY = (-40, -39, 8)
ATTN_PRIORITY = (-20, -10)
YZ_CHUNKS = ()
LAST_WIDE = 30


def matrix_product(left, right):
    return jnp.dot(left, right, preferred_element_type=F32)


def product_with_transpose(left, right):
    return lax.dot_general(left, right, (((1,), (1,)), ((), ())), preferred_element_type=F32)


def transpose_then_product(left, right):
    return lax.dot_general(left, right, (((0,), (0,)), ((), ())), preferred_element_type=F32)


def rms_norm(values, gain_vec):
    return (
        values * lax.rsqrt(jnp.mean(values * values, axis=-1, keepdims=True) + norm_eps) * gain_vec
    )


def rms_back(values, gain_vec, grad):
    scale = lax.rsqrt(jnp.mean(values * values, axis=-1, keepdims=True) + norm_eps)
    e = gain_vec * grad
    return scale * e - values * (scale * scale * scale) * jnp.mean(values * e, axis=-1, keepdims=True)


def ring_and_swaps(n):
    perms = {
        "y": [(i, i ^ 2) for i in range(n)],
        "x": [(i, i ^ 1) for i in range(n)],
        "xy": [(i, i ^ 3) for i in range(n)],
    }
    for r in range(1, n // 4):
        perms[f"z{r}"] = [(i, (i + 4 * r) % n) for i in range(n)]
    perms["z"] = perms["z1"]
    return perms


def plan_transfers(ring_size, chunks):
    plan = {}
    first, second = ATTN_PRIORITY
    plan["A0.y"] = ("y", "A0.o", first, 1)
    for r in range(ring_size):
        if r:
            plan[f"A0.b{r}"] = ("z", f"A0.b{r - 1}", first + 0.01 * r, 2)
            plan[f"A1.p{r}"] = ("z", f"A1.p{r - 1}", second + 0.01 * r, 1)
        plan[f"A1.q{r}"] = ("y", f"A1.p{r}", second + 0.01 * r, 1)
        plan[f"A0.x{r}"] = ("x", f"A0.b{r}", first + 0.01 * r, 2)
        plan[f"A1.x{r}"] = ("x", f"A1.b{r}", second + 0.01 * r, 2)
    for i, group in enumerate(exchanges_of(chunks)):
        plan[f"E{i}.e"] = ("x", f"E{i}.o", EXCHANGE_PRIORITY[min(i, 2)], (len(group) + 1) // 2)
    for j in range(chunks):
        tag = f"M{j}"
        for r in range(ring_size):
            source = (f"{tag}.p{r}" if r else tag)
            if r:
                before = f"{tag}.p{r - 1}" if r > 1 else tag
                plan[f"{tag}.p{r}"] = ("z", before, j + 0.01 * r, 1)
            plan[f"{tag}.q{r}"] = ("y", source, j + 0.01 * r, 1)
    plan["C.x"] = ("x", "C.o", LAST_WIDE, 3)
    plan["N.x"] = ("x", "N.o", -50, 3)
    return plan


def exchanges_of(chunks):
    return EXCHANGES[:2] + (tuple(range(4, chunks)),)


def schedule(plan, chunks):
    makes = {"A0.y": ["A0.b0"]}
    for i, group in enumerate(exchanges_of(chunks)):
        makes[f"E{i}.e"] = [f"M{j}" for j in group]
    ready, busy, arrivals = {}, {}, {}
    for _, source, _, _ in plan.values():
        if source.endswith(".o") and source != "N.o":
            ready[source] = 0
    ready["A1.p0"] = 0
    steps, waiting, now = [], dict(plan), 0
    while waiting:
        step = []
        if "N.o" not in ready and not any(name.startswith("A1") for name in waiting):
            ready["N.o"] = max(s for s, names in arrivals.items() if "A1.x" in str(names))
            ready["N.o"] += NORMED_AFTER
        for link in "xyz":
            able = [
                (entry[2], name)
                for name, entry in waiting.items()
                if entry[0] == link
                and busy.get(link, 0) <= now
                and ready.get(entry[1], 1 << 30) <= now
            ]
            if able:
                name = min(able)[1]
                length = waiting.pop(name)[3]
                step.append(name)
                busy[link] = now + length
                ready[name] = now + (LAG if length == 1 else length)
                arrivals.setdefault(ready[name], []).append(name)
                for made in makes.get(name, []):
                    ready[made] = ready[name]
                if name.startswith("A1") and name[3] in "pq":
                    pair = (f"A1.p{name[4:]}", f"A1.q{name[4:]}")
                    if pair[0] in ready and pair[1] in ready:
                        ready[f"A1.b{name[4:]}"] = max(ready[p] for p in pair)
        steps.append(step)
        now += 1
    return steps, arrivals


def tie(values, others, flops=STEP_FLOPS):
    def kernel(*refs):
        pass

    spec = pl.BlockSpec(memory_space=pltpu.HBM)
    n = len(values)
    return pl.pallas_call(
        kernel,
        out_shape=[jax.ShapeDtypeStruct(v.shape, v.dtype) for v in values],
        in_specs=[spec] * (n + len(others)),
        out_specs=[spec] * n,
        input_output_aliases={i: i for i in range(n)},
        cost_estimate=pl.CostEstimate(flops=flops, transcendentals=0, bytes_accessed=0),
    )(*values, *others)


def bring(blocks, place_ref, target, sems):
    total = sum(block.shape[0] for block in blocks)
    rows = total // place_ref.shape[0]
    copies = []
    for block in blocks:
        for start in range(0, block.shape[0], rows):
            i = len(copies)
            to = pl.multiple_of(place_ref[i] * rows, math.gcd(rows, 16))
            copies.append(
                pltpu.make_async_copy(
                    block.at[pl.ds(start, rows)], target.at[pl.ds(to, rows)], sems.at[i]
                )
            )
    return copies


HBM = pl.BlockSpec(memory_space=pl.ANY)
VMEM = pl.BlockSpec(memory_space=pltpu.VMEM)
SMEM = pl.BlockSpec(memory_space=pltpu.SMEM)


def nt(left, right):
    return lax.dot_general(left, right, (((1,), (1,)), ((), ())), preferred_element_type=F32)


def turn(upright, cos_ref, sin_ref, sign, row):
    half = HEAD_DIM // 2
    first, second = upright[row : row + half], upright[row + half : row + 2 * half]
    cos, sin = cos_ref[...], sin_ref[...] * sign
    return jnp.concatenate([first * cos - second * sin, second * cos + first * sin], axis=0)


def queries_and_keys(places, blocks, normed, low_query, low_key, second_query, second_key, cos, sin):
    count = len(blocks)
    tokens, width = normed.shape
    cols = blocks[0].shape[1]
    q_cols, k_cols = second_query.shape[1], second_key.shape[1]

    def kernel(place_ref, x_ref, lq_ref, lk_ref, sq_ref, sk_ref, cos_ref, sin_ref, *refs):
        parts, (q_out, k_out, w_out, w_s, sems, sem_out) = refs[:count], refs[count:]
        copies = bring(parts, place_ref, w_s, sems)
        for copy in copies:
            copy.start()
        for copy in copies:
            copy.wait()
        keep = pltpu.make_async_copy(w_s, w_out, sem_out)
        keep.start()
        x = x_ref[...]
        step = 4 * HEAD_DIM
        for start, low, second, out, shift in [
            (at, lq_ref, sq_ref, q_out, 0) for at in range(0, q_cols, step)
        ] + [(q_cols + at, lk_ref, sk_ref, k_out, q_cols) for at in range(0, k_cols, step)]:
            own = start - shift
            part = jnp.dot(x, w_s[:, start : start + step], preferred_element_type=F32)
            part += jnp.dot(low[...], second[:, own : own + step], preferred_element_type=F32)
            upright = part.T
            for row in range(0, step, HEAD_DIM):
                out[own + row : own + row + HEAD_DIM, :] = turn(
                    upright, cos_ref, sin_ref, 1.0, row
                ).astype(BF)
        keep.wait()

    return pl.pallas_call(
        kernel,
        out_shape=[
            jax.ShapeDtypeStruct((q_cols, tokens), BF),
            jax.ShapeDtypeStruct((k_cols, tokens), BF),
            jax.ShapeDtypeStruct((width, cols), BF),
        ],
        in_specs=[SMEM] + [VMEM] * 7 + [HBM] * count,
        out_specs=[VMEM, VMEM, HBM],
        scratch_shapes=[
            pltpu.VMEM((width, cols), BF),
            pltpu.SemaphoreType.DMA((places.shape[0],)),
            pltpu.SemaphoreType.DMA,
        ],
        compiler_params=pltpu.CompilerParams(vmem_limit_bytes=48 * 2**20),
        cost_estimate=pl.CostEstimate(
            flops=2 * tokens * width * cols, transcendentals=0, bytes_accessed=4 * width * cols
        ),
    )(places, normed, low_query, low_key, second_query, second_key, cos, sin, *blocks)


def seen(rows, columns, row_start, column_start):
    key = lax.broadcasted_iota(jnp.int32, (rows, columns), 0)
    query = lax.broadcasted_iota(jnp.int32, (rows, columns), 1)
    causal = key <= query
    if row_start >= PROMPT:
        causal = causal & (key // CONT_LEN == query // CONT_LEN)
    return causal


def attention(places, blocks, normed, low_value, second_value, query, key, in_output):
    count = len(blocks)
    tokens, width = normed.shape
    cols = blocks[0].shape[1]
    q_cols, k_cols = query.shape[0], key.shape[0]
    kv_heads = k_cols // HEAD_DIM
    group = q_cols // k_cols
    scale = 1.0 / math.sqrt(HEAD_DIM)

    def kernel(place_ref, x_ref, lv_ref, sv_ref, q_ref, k_ref, io_ref, *refs):
        parts = refs[:count]
        v_out, att_out, lse_out, branch_out, low_out, w_out, w_s, att_s, sems, sem_out = refs[count:]
        copies = bring(parts, place_ref, w_s, sems)
        for copy in copies:
            copy.start()
        for copy in copies:
            copy.wait()
        keep = pltpu.make_async_copy(w_s, w_out, sem_out)
        keep.start()
        value = jnp.dot(x_ref[...], w_s[:, q_cols:cols], preferred_element_type=F32)
        value += jnp.dot(lv_ref[...], sv_ref[...], preferred_element_type=F32)
        v_out[...] = value.T.astype(BF)
        seen_first = seen(PROMPT, PROMPT, 0, 0)
        seen_second = seen(tokens - PROMPT, tokens - PROMPT, PROMPT, PROMPT)

        def one_head(g, _):
            k_rows = pl.ds(pl.multiple_of(g * HEAD_DIM, 16), HEAD_DIM)
            keys = k_ref[k_rows, :].T
            values = v_out[k_rows, :]
            for h in range(group):
                rows = pl.ds(pl.multiple_of((g * group + h) * HEAD_DIM, 16), HEAD_DIM)
                head = q_ref[rows, :]
                early = jnp.dot(keys[:PROMPT], head[:, :PROMPT], preferred_element_type=F32)
                late = jnp.dot(keys, head[:, PROMPT:], preferred_element_type=F32)
                early = jnp.where(seen_first, early * scale, -1e30)
                late_prompt = late[:PROMPT] * scale
                late_own = jnp.where(seen_second, late[PROMPT:] * scale, -1e30)
                top = jnp.max(early, axis=0, keepdims=True)
                expo = jnp.exp(early - top)
                total = jnp.sum(expo, axis=0, keepdims=True)
                prob = (expo * (1.0 / total)).astype(BF)
                lse_out[g, h : h + 1, :PROMPT] = top + jnp.log(total)
                att_s[rows, :PROMPT] = jnp.dot(
                    values[:, :PROMPT], prob, preferred_element_type=F32
                ).astype(BF)
                top = jnp.maximum(
                    jnp.max(late_prompt, axis=0, keepdims=True),
                    jnp.max(late_own, axis=0, keepdims=True),
                )
                expo_p, expo_o = jnp.exp(late_prompt - top), jnp.exp(late_own - top)
                total = jnp.sum(expo_p, axis=0, keepdims=True) + jnp.sum(
                    expo_o, axis=0, keepdims=True
                )
                inverse = 1.0 / total
                prob = jnp.concatenate(
                    [(expo_p * inverse).astype(BF), (expo_o * inverse).astype(BF)], axis=0
                )
                lse_out[g, h : h + 1, PROMPT:] = top + jnp.log(total)
                att_s[rows, PROMPT:] = jnp.dot(
                    values, prob, preferred_element_type=F32
                ).astype(BF)
            return 0

        lax.fori_loop(0, kv_heads, one_head, 0)
        att_out[...] = att_s[...].T
        attended = att_out[...]
        low_out[...] = jnp.dot(attended, io_ref[...], preferred_element_type=F32)
        for at in range(0, width, 512):
            branch_out[:, at : at + 512] = nt(attended, w_s[at : at + 512, :q_cols]).astype(BF)
        keep.wait()

    return pl.pallas_call(
        kernel,
        out_shape=[
            jax.ShapeDtypeStruct((k_cols, tokens), BF),
            jax.ShapeDtypeStruct((tokens, q_cols), BF),
            jax.ShapeDtypeStruct((kv_heads, group, tokens), F32),
            jax.ShapeDtypeStruct((tokens, width), BF),
            jax.ShapeDtypeStruct((tokens, in_output.shape[1]), F32),
            jax.ShapeDtypeStruct((width, cols), BF),
        ],
        in_specs=[SMEM] + [VMEM] * 6 + [HBM] * count,
        out_specs=[VMEM] * 5 + [HBM],
        scratch_shapes=[
            pltpu.VMEM((width, cols), BF),
            pltpu.VMEM((q_cols, tokens), BF),
            pltpu.SemaphoreType.DMA((places.shape[0],)),
            pltpu.SemaphoreType.DMA,
        ],
        compiler_params=pltpu.CompilerParams(vmem_limit_bytes=48 * 2**20),
        cost_estimate=pl.CostEstimate(
            flops=4 * tokens * width * cols, transcendentals=0, bytes_accessed=4 * width * cols
        ),
    )(places, normed, low_value, second_value, query, key, in_output, *blocks)


def attention_back(
    core, halves, select, second_output, low_output, attended, in_output, full_a0, full_a1, query,
    key, value, lse, cos, sin, second_query, second_key, second_value, low_query, low_key, low_value,
):
    half_tokens, width = halves[0].shape
    tokens = 2 * half_tokens
    cols = full_a0.shape[1]
    q_cols, k_cols = query.shape[0], key.shape[0]
    rank = second_query.shape[0]
    kv_heads = k_cols // HEAD_DIM
    group = q_cols // k_cols
    scale = 1.0 / math.sqrt(HEAD_DIM)

    def kernel(
        core_ref, mine_hbm, other_hbm, sel_ref, so_ref, lo_ref, att_ref, io_ref, a0_hbm, a1_hbm, q_ref, k_ref, v_ref, lse_ref, cos_ref, sin_ref,
        sq_ref, sk_ref, sv_ref, lq_ref, lk_ref, lv_ref, back_out, low_out, second_out,
        first_out, second_o_out, a0, a1, gb_ref, glo_ref, ga_s, g_s, gw_s, sems,
    ):
        mine = core_ref[0]
        copies = [
            pltpu.make_async_copy(a1_hbm, a1, sems.at[0]),
            pltpu.make_async_copy(a0_hbm, a0, sems.at[1]),
            pltpu.make_async_copy(
                mine_hbm, gb_ref.at[pl.ds(pl.multiple_of(mine * half_tokens, 16), half_tokens)], sems.at[2]
            ),
            pltpu.make_async_copy(
                other_hbm,
                gb_ref.at[pl.ds(pl.multiple_of((1 - mine) * half_tokens, 16), half_tokens)],
                sems.at[3],
            ),
        ]
        for i in (2, 3, 0, 1):
            copies[i].start()
        for i in (2, 3):
            copies[i].wait()
        glo_ref[...] = (adapter_scale * nt(gb_ref[...], so_ref[...]) * sel_ref[...]).astype(BF)
        first_out[...] = jnp.dot(
            att_ref[...].T, glo_ref[...], preferred_element_type=F32
        ).astype(BF)
        part = jnp.dot(
            lo_ref[...].T,
            gb_ref[:, pl.ds(pl.multiple_of(mine * (width // 2), 128), width // 2)],
            preferred_element_type=F32,
        )
        for at in range(0, width // 2, rank):
            second_o_out[at : at + rank, :] = (adapter_scale * part[:, at : at + rank]).astype(BF)
        copies[0].wait()
        step = 4 * HEAD_DIM
        for at in range(0, q_cols, step):
            part = jnp.dot(gb_ref[...], a1[:, at : at + step], preferred_element_type=F32)
            part += nt(glo_ref[...], io_ref[at : at + step, :])
            ga_s[at : at + step, :] = part.astype(BF).T
        seen_first = seen(PROMPT, PROMPT, 0, 0)
        seen_second = seen(tokens - PROMPT, tokens - PROMPT, PROMPT, PROMPT)

        def one_head(g, _):
            k_rows = pl.ds(pl.multiple_of(g * HEAD_DIM, 16), HEAD_DIM)
            keys_up = k_ref[k_rows, :]
            keys = keys_up.T
            values = v_ref[k_rows, :].T
            grad_k, grad_v = [0.0, 0.0], [0.0, 0.0]
            for h in range(group):
                rows = pl.ds(pl.multiple_of((g * group + h) * HEAD_DIM, 16), HEAD_DIM)
                head, grad = q_ref[rows, :], ga_s[rows, :]
                lse_h = lse_ref[g, h : h + 1, :]
                score = jnp.dot(keys[:PROMPT], head[:, :PROMPT], preferred_element_type=F32)
                prob = jnp.where(seen_first, jnp.exp(score * scale - lse_h[:, :PROMPT]), 0.0)
                grad_prob = jnp.dot(values[:PROMPT], grad[:, :PROMPT], preferred_element_type=F32)
                row_term = jnp.sum(prob * grad_prob, axis=0, keepdims=True)
                grad_score = (prob * (grad_prob - row_term)).astype(BF)
                prob = prob.astype(BF)
                grad_q_early = jnp.dot(
                    keys_up[:, :PROMPT], grad_score, preferred_element_type=F32
                )
                grad_v[0] += nt(grad[:, :PROMPT], prob)
                grad_k[0] += nt(head[:, :PROMPT], grad_score)
                score = jnp.dot(keys, head[:, PROMPT:], preferred_element_type=F32)
                expo = jnp.exp(score * scale - lse_h[:, PROMPT:])
                prob_p = expo[:PROMPT]
                prob_o = jnp.where(seen_second, expo[PROMPT:], 0.0)
                grad_prob = jnp.dot(values, grad[:, PROMPT:], preferred_element_type=F32)
                row_term = jnp.sum(prob_p * grad_prob[:PROMPT], axis=0, keepdims=True) + jnp.sum(
                    prob_o * grad_prob[PROMPT:], axis=0, keepdims=True
                )
                score_p = (prob_p * (grad_prob[:PROMPT] - row_term)).astype(BF)
                score_o = (prob_o * (grad_prob[PROMPT:] - row_term)).astype(BF)
                grad_q_late = jnp.dot(
                    keys_up, jnp.concatenate([score_p, score_o], axis=0), preferred_element_type=F32
                )
                grad_v[0] += nt(grad[:, PROMPT:], prob_p.astype(BF))
                grad_v[1] += nt(grad[:, PROMPT:], prob_o.astype(BF))
                grad_k[0] += nt(head[:, PROMPT:], score_p)
                grad_k[1] += nt(head[:, PROMPT:], score_o)
                grad_q = jnp.concatenate([grad_q_early, grad_q_late], axis=1) * scale
                g_s[rows, :] = turn(grad_q, cos_ref, sin_ref, -1.0, 0).astype(BF)
            grad_key = jnp.concatenate(grad_k, axis=1) * scale
            g_s[pl.ds(pl.multiple_of(q_cols + g * HEAD_DIM, 16), HEAD_DIM), :] = turn(
                grad_key, cos_ref, sin_ref, -1.0, 0
            ).astype(BF)
            g_s[pl.ds(pl.multiple_of(q_cols + k_cols + g * HEAD_DIM, 16), HEAD_DIM), :] = (
                jnp.concatenate(grad_v, axis=1).astype(BF)
            )
            return 0

        lax.fori_loop(0, kv_heads, one_head, 0)
        gw_s[...] = g_s[...].T
        part = [
            jnp.dot(low[...].T, gw_s[:, at : at + size], preferred_element_type=F32)
            for at, size, low in (
                (0, q_cols, lq_ref),
                (q_cols, k_cols, lk_ref),
                (q_cols + k_cols, k_cols, lv_ref),
            )
        ]
        part = jnp.concatenate(part, axis=1).astype(BF)
        for at in range(0, q_cols + 2 * k_cols, rank):
            second_out[at : at + rank, :] = part[:, at : at + rank]
        for i, (at, size, second) in enumerate(
            ((0, q_cols, sq_ref), (q_cols, k_cols, sk_ref), (q_cols + k_cols, k_cols, sv_ref))
        ):
            low_out[:, i * rank : (i + 1) * rank] = adapter_scale * nt(
                gw_s[:, at : at + size], second[...]
            )
        copies[1].wait()
        for at in range(0, width, 512):
            rows = slice(at, at + 512)
            part = nt(gw_s[:, :cols], a0[rows, :]) + nt(gw_s[:, cols:], a1[rows, q_cols:])
            back_out[:, rows] = part.astype(BF)

    return pl.pallas_call(
        kernel,
        out_shape=[
            jax.ShapeDtypeStruct((tokens, width), BF),
            jax.ShapeDtypeStruct((tokens, 3 * rank), F32),
            jax.ShapeDtypeStruct((q_cols + 2 * k_cols, rank), BF),
            jax.ShapeDtypeStruct((q_cols, rank), BF),
            jax.ShapeDtypeStruct((width // 2, rank), BF),
        ],
        in_specs=[SMEM, HBM, HBM] + [VMEM] * 5 + [HBM] * 2 + [VMEM] * 12,
        out_specs=[VMEM] * 5,
        scratch_shapes=[
            pltpu.VMEM((width, cols), BF),
            pltpu.VMEM((width, cols), BF),
            pltpu.VMEM((tokens, width), BF),
            pltpu.VMEM((tokens, rank), BF),
            pltpu.VMEM((q_cols, tokens), BF),
            pltpu.VMEM((q_cols + 2 * k_cols, tokens), BF),
            pltpu.VMEM((tokens, q_cols + 2 * k_cols), BF),
            pltpu.SemaphoreType.DMA((4,)),
        ],
        compiler_params=pltpu.CompilerParams(vmem_limit_bytes=56 * 2**20),
        cost_estimate=pl.CostEstimate(
            flops=20 * tokens * width * cols, transcendentals=0, bytes_accessed=4 * width * cols
        ),
    )(
        core, *halves, select, second_output, low_output, attended, in_output, full_a0, full_a1, query,
        key, value, lse, cos, sin, second_query, second_key, second_value, low_query, low_key, low_value,
    )


def after_attention(
    hidden, branches, branch_lows, select, second_output, gain, mlp_in
):
    tokens, width = hidden.shape
    rank = select.shape[1]
    tile = 128

    def kernel(h_ref, b0, b1, l0, l1, sel_ref, so_ref, gain_ref, in_ref, mid_out, ext_out, low_out):
        def one(t, _):
            r = pl.ds(pl.multiple_of(t * tile, tile), tile)
            sel = sel_ref[r, :]
            low = ((l0[r, :] + l1[r, :]) * sel).astype(BF)
            low_out[r, :] = low
            middle = h_ref[r, :].astype(F32) + (b0[r, :].astype(F32) + b1[r, :].astype(F32))
            middle += adapter_scale * jnp.dot(low, so_ref[...], preferred_element_type=F32)
            mid_out[r, :] = middle
            scale = lax.rsqrt(jnp.mean(middle * middle, axis=1, keepdims=True) + norm_eps)
            normed = (middle * scale * gain_ref[...]).astype(BF)
            ext_out[r, :width] = normed
            part = jnp.dot(normed, in_ref[...], preferred_element_type=F32)
            part = (part * jnp.concatenate([sel, sel], axis=1)).astype(BF)
            ext_out[r, width:] = part * jnp.array(adapter_scale, BF)
            return 0

        lax.fori_loop(0, tokens // tile, one, 0)

    return pl.pallas_call(
        kernel,
        out_shape=[
            jax.ShapeDtypeStruct((tokens, width), F32),
            jax.ShapeDtypeStruct((tokens, width + 2 * rank), BF),
            jax.ShapeDtypeStruct((tokens, rank), BF),
        ],
        in_specs=[VMEM] * 9,
        out_specs=[VMEM] * 3,
        compiler_params=pltpu.CompilerParams(vmem_limit_bytes=40 * 2**20),
        cost_estimate=pl.CostEstimate(
            flops=6 * tokens * width * rank, transcendentals=0, bytes_accessed=14 * tokens * width
        ),
    )(hidden, *branches, *branch_lows, select, second_output, gain, mlp_in)


def after_feed_forward(core, parts, middle, cotangent, select, gain, mlp_in):
    half, wide = parts[0].shape
    tokens, width = middle.shape
    rank = select.shape[1]
    tile = 128

    def kernel(
        core_ref, p0, p1, p2, mid_hbm, cot_hbm, sel_ref, gain_ref, in_ref, mid_out, branch_out, low_out,
        mid_s, cot_s, sems,
    ):
        start = pl.multiple_of(core_ref[0] * half, 16)
        copies = [
            pltpu.make_async_copy(mid_hbm.at[pl.ds(start, half)], mid_s, sems.at[0]),
            pltpu.make_async_copy(cot_hbm.at[pl.ds(start, half)], cot_s, sems.at[1]),
        ]
        for copy in copies:
            copy.start()
        for copy in copies:
            copy.wait()

        def one(t, _):
            r = pl.ds(pl.multiple_of(t * tile, tile), tile)
            sel = sel_ref[pl.ds(pl.multiple_of(start + t * tile, tile), tile), :]
            total = p0[r, :].astype(F32) + p1[r, :].astype(F32) + p2[r, :].astype(F32)
            low = (
                adapter_scale * total[:, width:] * jnp.concatenate([sel, sel], axis=1)
            ).astype(BF)
            low_out[r, :] = low
            grad = (total[:, :width] + nt(low, in_ref[...])) * gain_ref[...]
            middle = mid_s[r, :]
            scale = lax.rsqrt(jnp.mean(middle * middle, axis=1, keepdims=True) + norm_eps)
            inner = jnp.mean(middle * grad, axis=1, keepdims=True)
            out = cot_s[r, :].astype(F32) + scale * grad - middle * (scale * scale * scale * inner)
            mid_out[r, :] = out
            branch_out[r, :] = out.astype(BF)
            return 0

        lax.fori_loop(0, half // tile, one, 0)

    return pl.pallas_call(
        kernel,
        out_shape=[
            jax.ShapeDtypeStruct((half, width), F32),
            jax.ShapeDtypeStruct((half, width), BF),
            jax.ShapeDtypeStruct((half, 2 * rank), BF),
        ],
        in_specs=[SMEM] + [VMEM] * 3 + [HBM] * 2 + [VMEM] * 3,
        out_specs=[VMEM] * 3,
        scratch_shapes=[
            pltpu.VMEM((half, width), F32),
            pltpu.VMEM((half, width), BF),
            pltpu.SemaphoreType.DMA((2,)),
        ],
        compiler_params=pltpu.CompilerParams(vmem_limit_bytes=40 * 2**20),
        cost_estimate=pl.CostEstimate(
            flops=6 * half * width * rank, transcendentals=0, bytes_accessed=20 * half * width
        ),
    )(core, *parts, middle, cotangent, select, gain, mlp_in)


def feed_forward(places, core, normed, cot, new, old, totals, last):
    sums = totals != "none"
    first = totals is None
    before = list(totals) if sums and not first else []
    n_new, n_old = len(new), len(old)
    blocks = [list(unit[-1]) for unit in new + old]
    factors = [unit[-2] for unit in new + old]
    count, per = len(blocks), len(blocks[0])
    part_rows, wide = blocks[0][0].shape
    group, n_wide = normed[0].shape
    c_wide = cot[0].shape[1]
    rank = n_wide - c_wide
    width = c_wide - rank
    rows = 2 * group
    tile = group // 2
    tiles = rows // tile
    flat = [v for unit, factor in zip(blocks, factors) for v in unit + [factor]]
    old_flat = [v for unit in old for v in unit[:2]]
    n_sums = (4 if last else 2) if sums else 0

    def kernel(place_ref, core_ref, *refs):
        it = iter(refs)

        def take(n):
            return [next(it) for _ in range(n)]

        old_ref = take(2 * n_old)
        normed_hbm, cot_hbm = take(3), take(3)
        block_hbm = [take(per + 1) for _ in range(count)]
        before_hbm = take(len(before))
        sum_hbm = take(n_sums)
        act_ref, grad_ref, own_ref = (take(n_new) for _ in range(3))
        w_s, sem_w = take(2)
        if n_new:
            normed_s, cot_s, sem_x = take(3)
        if sums:
            acc_g, acc_o, sem_t, sem_out = take(4)
            fin_g, fin_o = (normed_s, cot_s) if last else (acc_g, acc_o)
        mine = core_ref[0]

        def fetch(k):
            slot = w_s.at[k % 2]
            return bring(block_hbm[k][:per], place_ref, slot, sem_w.at[k % 2]) + [
                pltpu.make_async_copy(
                    block_hbm[k][per], slot.at[pl.ds(width, 2 * rank)], sem_w.at[k % 2, places.shape[0]]
                )
            ]

        def load_x(t):
            copies = []
            for i, (src, dst) in enumerate(((normed_hbm, normed_s), (cot_hbm, cot_s))):
                if t < 2:
                    part, to = src[0].at[pl.ds(t * tile, tile)], t * tile
                else:
                    part = src[t - 1]
                    to = group + tile * (mine if t == 2 else 1 - mine)
                    to = pl.multiple_of(to, 16)
                copies.append(pltpu.make_async_copy(part, dst.at[pl.ds(to, tile)], sem_x.at[i, t]))
            return copies

        def load_t(t):
            r = pl.ds(t * tile, tile)
            return [
                pltpu.make_async_copy(src.at[r], dst.at[r], sem_t.at[i, t])
                for i, (src, dst) in enumerate(zip(before_hbm, (acc_g, acc_o)))
            ]

        def store_t(t, to):
            r = pl.ds(t * tile, tile)
            copies = []
            for i, src in enumerate((fin_g, fin_o)):
                dst = sum_hbm[2 * i + to].at[t // 2] if last else sum_hbm[i].at[r]
                copies.append(pltpu.make_async_copy(src.at[r], dst, sem_out.at[i, t]))
            return copies

        if n_new:
            for copy in load_x(0):
                copy.start()
        for copy in fetch(0):
            copy.start()
        if n_new:
            for copy in fetch(0):
                copy.wait()
            for t in range(1, tiles):
                for copy in load_x(t):
                    copy.start()
        if before:
            for t in range(tiles):
                for copy in load_t(t):
                    copy.start()
        for k in range(count):
            if k + 1 < count:
                for copy in fetch(k + 1):
                    copy.start()
            if k or not n_new:
                for copy in fetch(k):
                    copy.wait()
            slot = k % 2
            if k < n_new:
                act, grad = act_ref[k], grad_ref[k]
                for t in range(tiles):
                    r = pl.ds(t * tile, tile)
                    if k == 0 and t < 2:
                        for copy in load_x(t):
                            copy.wait()
                    if k == 0 and t == 2:
                        for copy in load_x(2) + load_x(3):
                            copy.wait()
                    x = normed_s[r, :]
                    gate = jnp.dot(x, w_s[slot, :, 0:WIDTH], preferred_element_type=F32)
                    up = jnp.dot(x, w_s[slot, :, WIDTH : 2 * WIDTH], preferred_element_type=F32)
                    back = jnp.dot(
                        cot_s[r, :],
                        w_s[slot, :c_wide, 2 * WIDTH : 3 * WIDTH],
                        preferred_element_type=F32,
                    )
                    sig = 1.0 / (1.0 + jnp.exp(-gate))
                    silu = gate * sig
                    act[r, :] = (silu * up).astype(BF)
                    grad[r, :WIDTH] = (back * up * (sig * (1.0 + gate * (1.0 - sig)))).astype(BF)
                    grad[r, WIDTH:] = (back * silu).astype(BF)
                low = normed_s[:, width:].T
                for part in range(2):
                    second = jnp.dot(
                        low[part * rank : (part + 1) * rank],
                        grad[:, part * WIDTH : (part + 1) * WIDTH],
                        preferred_element_type=F32,
                    ).astype(BF)
                    for at in range(0, WIDTH, rank):
                        to = part * WIDTH + at
                        own_ref[k][to : to + rank, :] = second[:, at : at + rank]
                own_ref[k][2 * WIDTH :, :] = jnp.dot(
                    act[...].T, cot_s[:, width:c_wide], preferred_element_type=F32
                ).astype(BF)
            else:
                act, grad = old_ref[2 * (k - n_new)], old_ref[2 * (k - n_new) + 1]
            if not sums:
                continue
            for t in range(tiles):
                r = pl.ds(t * tile, tile)
                if before and k == 0:
                    for copy in load_t(t):
                        copy.wait()
                for acc, fin, val, lo, hi, top in (
                    (acc_g, fin_g, grad, 0, 2 * WIDTH, n_wide),
                    (acc_o, fin_o, act, 2 * WIDTH, 3 * WIDTH, c_wide),
                ):
                    for at in range(0, top, 512):
                        n = slice(at, min(at + 512, top))
                        part = nt(val[r, :], w_s[slot, n, lo:hi])
                        if k or not first:
                            part = acc[r, n] + part
                        if k == count - 1:
                            fin[r, n] = part.astype(fin.dtype)
                        else:
                            acc[r, n] = part
                if k == count - 1 and last:
                    side = mine if t % 2 == 0 else 1 - mine
                    for to in range(2):

                        @pl.when(side == to)
                        def _():
                            for copy in store_t(t, to):
                                copy.start()

                elif k == count - 1:
                    for copy in store_t(t, 0):
                        copy.start()
        if sums:
            for t in range(tiles):
                for copy in store_t(t, 0):
                    copy.wait()

    scratch = [
        pltpu.VMEM((2, n_wide, wide), BF),
        pltpu.SemaphoreType.DMA((2, places.shape[0] + 1)),
    ]
    if n_new:
        scratch += [
            pltpu.VMEM((rows, n_wide), BF),
            pltpu.VMEM((rows, c_wide), BF),
            pltpu.SemaphoreType.DMA((2, tiles)),
        ]
    out_shape = []
    if sums:
        scratch += [
            pltpu.VMEM((rows, n_wide), F32),
            pltpu.VMEM((rows, c_wide), F32),
            pltpu.SemaphoreType.DMA((2, tiles)),
            pltpu.SemaphoreType.DMA((2, tiles)),
        ]
        for columns in (n_wide, c_wide):
            if last:
                out_shape += [jax.ShapeDtypeStruct((2, tile, columns), BF)] * 2
            else:
                out_shape += [jax.ShapeDtypeStruct((rows, columns), F32)]
    out_shape += [jax.ShapeDtypeStruct((rows, WIDTH), BF)] * n_new
    out_shape += [jax.ShapeDtypeStruct((rows, 2 * WIDTH), BF)] * n_new
    out_shape += [jax.ShapeDtypeStruct((3 * WIDTH, rank), BF)] * n_new
    n_hbm = 6 + len(flat)
    at = 2 + len(old_flat) + n_hbm
    out = pl.pallas_call(
        kernel,
        out_shape=out_shape,
        in_specs=[SMEM] * 2 + [VMEM] * len(old_flat) + [HBM] * (n_hbm + len(before)),
        out_specs=[HBM] * n_sums + [VMEM] * (3 * n_new),
        scratch_shapes=scratch,
        input_output_aliases={at: 0, at + 1: 1} if before and not last else {},
        compiler_params=pltpu.CompilerParams(vmem_limit_bytes=60 * 2**20),
        cost_estimate=pl.CostEstimate(
            flops=6 * (n_new + (count if sums else 0)) * rows * width * WIDTH,
            transcendentals=n_new * rows * WIDTH,
            bytes_accessed=4 * rows * width,
        ),
    )(places, core, *old_flat, *normed, *cot, *flat, *before)
    rest = out[n_sums:]
    return tuple(out[:n_sums]), list(zip(*(rest[i * n_new : (i + 1) * n_new] for i in range(3))))


DP = ("ring", "second", "first")


def make_body(n):
    ring_size = n // 4
    perms = ring_and_swaps(n)

    def move(value, link):
        return lax.ppermute(value, DP, perms[link])

    def other_core(value):
        return lax.ppermute(value, "tensor", [(0, 1), (1, 0)])

    def take(value, start, size, axis=0):
        return lax.dynamic_slice_in_dim(value, start, size, axis)

    def body(
        hidden_in, adapter_ids, attn_gain, mlp_gain, w_query, w_key, w_value, w_output, w_gate,
        w_up, w_down, in_query, second_query, in_key, second_key, in_value, second_value,
        in_output, second_output, in_gate, second_gate, in_up, second_up, in_down, second_down,
        cotangent,
    ):
        num_rows, width = hidden_in.shape
        half_rows = num_rows // 2
        half_width = width // 2
        rank_cols = in_query.shape[1]
        units = w_gate.shape[1] // 2
        chunks = units // WIDTH
        shard = w_query.shape[0]

        ring_at, bit_y, bit_x = (lax.axis_index(name) for name in DP)
        core = lax.axis_index("tensor")
        core_at = core.astype(jnp.int32).reshape(1)
        bits = {"x": bit_x, "y": bit_y}

        def in_order(bit, value, received, axis=0):
            first = jnp.where(bit == 0, value, received)
            return jnp.concatenate([first, jnp.where(bit == 0, received, value)], axis=axis)

        def half_of(value):
            return take(value, core * half_rows, half_rows)

        def both_halves(value):
            return in_order(core, value, other_core(value))

        def cols_of_core(value):
            return take(value, core * half_width, half_width, 1)

        row_index = lax.iota(jnp.int32, num_rows)
        is_later = row_index >= PROMPT
        seq_of = jnp.where(is_later, 1 + (row_index - PROMPT) // CONT_LEN, 0)
        position = jnp.where(is_later, PROMPT + (row_index - PROMPT) % CONT_LEN, row_index)
        seq_ids = lax.iota(jnp.int32, adapter_ids.shape[1])
        row_adapter = jnp.sum(
            jnp.where(seq_of[:, None] == seq_ids[None, :], adapter_ids[0][None, :], 0), axis=1
        )
        select = (lax.iota(jnp.int32, rank_cols)[None, :] // RANK == row_adapter[:, None]).astype(F32)
        select_three = jnp.concatenate([select] * 3, axis=1)
        inv_freq = rope_base ** (-2.0 * lax.iota(F32, HEAD_DIM // 2) / HEAD_DIM)
        angles = inv_freq[:, None] * position.astype(F32)[None, :]
        cos_table, sin_table = jnp.cos(angles), jnp.sin(angles)
        attn_in = jnp.concatenate([in_query, in_key, in_value], axis=1)
        mlp_in = jnp.concatenate([in_gate, in_up], axis=1)
        attn_gain_f = attn_gain.astype(F32)
        mlp_gain_f = mlp_gain.astype(F32).reshape(1, width)
        two = jnp.array(adapter_scale, BF)

        unit_start = bit_x * units

        def half_units(start):
            return (
                take(w_gate, start, units, 1),
                take(w_up, start, units, 1),
                take(w_down, start, units, 0).T,
            )

        mine, others = half_units(unit_start), half_units(units - unit_start)

        def chunk_of(parts, j):
            return jnp.concatenate([p[:, j * WIDTH : (j + 1) * WIDTH] for p in parts], axis=1)

        factor_parts = (
            take(second_gate, unit_start, units, 1),
            take(second_up, unit_start, units, 1),
            take(in_down, unit_start, units, 0),
        )
        blank = jnp.zeros((rank_cols, WIDTH), BF)
        chunk_cols = 3 * WIDTH

        def factors_of(j):
            cols = slice(j * WIDTH, (j + 1) * WIDTH)
            gate, up, down = factor_parts
            upper = jnp.concatenate([gate[:, cols], blank, down[cols].T], axis=1)
            return jnp.concatenate(
                [upper, jnp.concatenate([blank, up[:, cols], blank], axis=1)], axis=0
            )

        grad_low_down = (
            adapter_scale * product_with_transpose(cotangent, second_down) * select
        ).astype(BF)
        cot_wide = jnp.concatenate([cotangent, grad_low_down], axis=1)

        held = {
            "A0.o": jnp.concatenate([w_query, w_key], axis=1),
            "A1.p0": jnp.concatenate([w_output.T, w_value], axis=1),
            "C.o": half_of(cot_wide),
        }
        groups = exchanges_of(chunks)
        for i, group in enumerate(groups):
            held[f"E{i}.o"] = jnp.concatenate([chunk_of(others, j) for j in group], axis=1)
        plan = plan_transfers(ring_size, chunks)
        steps, arrivals = schedule(plan, chunks)
        when = {name: s for s, names in arrivals.items() for name in names}
        last_step = len(steps) - 1

        def there(tag):
            return max(s for name, s in when.items() if name.split(".")[0] == tag)

        def pieces(tag):
            found, places = [], []
            for r in range(ring_size):
                ring = (ring_at - r + ring_size) % ring_size
                if tag[0] == "A":
                    for other in range(2):
                        found.append(held[f"{tag}.{'x' if other else 'b'}{r}"])
                        bit = 1 - bit_x if other else bit_x
                        places += [(ring * 2 + bit_y) * 2 + bit, (ring * 2 + 1 - bit_y) * 2 + bit]
                else:
                    for other in range(2):
                        name = f"{tag}.q{r}" if other else f"{tag}.p{r}" if r else tag
                        found.append(held[name])
                        pair = ring * 2 + (1 - bit_y if other else bit_y)
                        places += [pair * 2 + bit_x, pair * 2 + 1 - bit_x]
            places = jnp.stack(places).astype(jnp.int32)
            if shard % 16:
                whole = jnp.zeros((n, shard, found[0].shape[1]), BF)
                for i in range(n):
                    part = found[i // 2][(i % 2) * shard : (i % 2 + 1) * shard]
                    whole = lax.dynamic_update_slice(whole, part[None], (places[i], 0, 0))
                return [whole.reshape(n * shard, -1)], jnp.zeros((1,), jnp.int32)
            return found, places

        v = {}
        hidden_wide = hidden_in.astype(F32)
        normed_a = rms_norm(hidden_wide, attn_gain_f).astype(BF)
        low_attn = (matrix_product(normed_a, attn_in) * select_three).astype(BF)
        lows = [low_attn[:, i * rank_cols : (i + 1) * rank_cols] * two for i in range(3)]

        def start_attention():
            found, places = pieces("A0")
            v["query"], v["key"], v["a0"] = queries_and_keys(
                places, found, normed_a, lows[0], lows[1], second_query, second_key, cos_table,
                sin_table,
            )
            return [v["key"]]

        def finish_attention():
            found, places = pieces("A1")
            v["value"], v["attended"], v["lse"], branch, branch_low, v["a1"] = attention(
                places, found, normed_a, lows[2], second_value, v["query"], v["key"], in_output
            )
            v["branches"] = (branch, other_core(branch))
            v["branch_lows"] = (branch_low, other_core(branch_low))
            return [v["value"]]

        def start_feed_forward():
            v["middle"], v["normed"], v["low_output"] = after_attention(
                hidden_in, v["branches"], v["branch_lows"], select, second_output, mlp_gain_f, mlp_in
            )
            held["N.o"] = half_of(v["normed"])
            return [v["low_output"]]

        def meet_neighbour():
            v["normed_all"] = (v["normed"], held["N.x"], other_core(held["N.x"]))
            v["cot_all"] = (cot_wide, held["C.x"], other_core(held["C.x"]))
            return [v["normed_all"][2], v["cot_all"][2]]

        unit_out = {}

        def feed(new, old, totals, last):
            found = {j: pieces(f"M{j}") for j in new + old}
            sums, results = feed_forward(
                found[(new + old)[0]][1],
                core_at,
                v["normed_all"],
                v["cot_all"],
                [(factors_of(j), found[j][0]) for j in new],
                [unit_out[j][:2] + (factors_of(j), found[j][0]) for j in old],
                totals,
                last,
            )
            unit_out.update(zip(new, results))
            return sums

        def units_only(new):
            def run():
                feed(new, [], "none", False)
                return [unit_out[new[-1]][0]]

            return run

        def sums_only(old):
            def run():
                v["totals"] = feed([], old, None, False)
                return [v["totals"][0]]

            return run

        order = sorted(range(chunks), key=lambda j: there(f"M{j}"))
        events = {}

        def at_step(s, run):
            events.setdefault(min(s, last_step), []).append(run)

        at_step(there("A0"), start_attention)
        at_step(there("A1"), finish_attention)
        at_step(there("A1") + NORMED_AFTER - 1, start_feed_forward)
        begin = there("N")
        at_step(begin, meet_neighbour)
        early, later, final = order[: chunks - 3], order[chunks - 3 : chunks - 1], order[-1]
        at = begin
        for i in range(0, len(early), 2):
            pair = early[i : i + 2]
            at = max([at] + [there(f"M{j}") for j in pair])
            at_step(at, units_only(pair))
            at += 1
        at_step(max(at, last_step - 4), sums_only(early))
        for j in later:
            at_step(max(at, there(f"M{j}")), units_only([j]))

        waits = []
        for s, step in enumerate(steps):
            sources = sorted({plan[name][1] for name in step})
            if s:
                arrived = [name for name in arrivals.get(s, []) if name not in sources]
                if sources and arrived + waits:
                    tied = tie([held[k] for k in sources], [held[k] for k in arrived] + waits)
                    held.update(zip(sources, tied))
                    waits = []
            for name in step:
                held[name] = move(held[plan[name][1]], plan[name][0])
            for name in arrivals.get(s + 1, []):
                if name.endswith(".e"):
                    for i, j in enumerate(groups[int(name[1:-2])]):
                        got = held[name][:, i * chunk_cols : (i + 1) * chunk_cols]
                        held[f"M{j}"] = jnp.concatenate([chunk_of(mine, j), got], axis=0)
                elif name == "A0.y":
                    held["A0.b0"] = jnp.concatenate([held["A0.o"], held[name]], axis=0)
                elif name.startswith("A1") and name[3] in "pq":
                    pair = [f"A1.{side}{name[4:]}" for side in "pq"]
                    if f"A1.b{name[4:]}" not in held and all(p in held for p in pair):
                        if max(when.get(p, 0) for p in pair) <= s + 1:
                            held[f"A1.b{name[4:]}"] = jnp.concatenate([held[p] for p in pair], axis=0)
            for run in events.get(s, []):
                waits += run()

        totals = feed([final], later, v["totals"], True)
        grad_keep, grad_send, out_keep, out_send = totals

        def after(values, *others):
            return tie(list(values), list(others), 0)

        def exchange(value, axes, parts):
            share = value.shape[0] // parts
            return lax.all_to_all(value.reshape(parts, share, rank_cols), axes, 0, 0)

        def total(parts):
            return jnp.sum(parts.astype(F32), axis=0).astype(BF)

        grad_got = other_core(grad_send)
        grad_out = (grad_keep[1].astype(F32) + grad_got[1].astype(F32)).astype(BF)
        grad_in_parts = (grad_keep[0], grad_got[0], move(grad_out, "x"))
        out_send, *own = after([out_send] + [unit_out[j][2] for j in range(chunks)], grad_out)
        out_got = other_core(out_send)
        out_out = (out_keep[1].astype(F32) + out_got[1].astype(F32)).astype(BF)
        got_units = exchange(jnp.concatenate(own, axis=0), DP[:2], n // 2)

        grad_middle, grad_branch, grad_low_mlp = after_feed_forward(
            core_at, grad_in_parts, v["middle"], cotangent, select, mlp_gain_f, mlp_in
        )
        out_in = move(after([out_out], grad_branch)[0], "x")
        grad_branch_other = other_core(grad_branch)
        grad_low_mlp = both_halves(grad_low_mlp)
        delta_mlp = transpose_then_product(
            cols_of_core(v["normed"][:, :width]), grad_low_mlp
        ).astype(BF)
        got_mlp = exchange(
            jnp.concatenate([delta_mlp[:, :rank_cols], delta_mlp[:, rank_cols:]], axis=0), DP, n
        )

        back, back_low, seconds, first_output, second_output_blocks = attention_back(
            core_at, (grad_branch, grad_branch_other), select, second_output, v["low_output"],
            v["attended"], in_output, v["a0"], v["a1"], v["query"], v["key"], v["value"], v["lse"],
            cos_table, sin_table, second_query, second_key, second_value, *lows,
        )
        back_low, got_units, got_mlp, out_in = after([back_low, got_units, got_mlp, out_in])
        back_low = back_low + other_core(back_low)
        grad_low_attn = (back_low * select_three).astype(BF)
        delta_attn = transpose_then_product(cols_of_core(normed_a), grad_low_attn).astype(BF)

        out_sum = out_keep[0].astype(F32) + out_got[0].astype(F32) + out_in.astype(F32)
        low_down = (out_sum[:, width:] * half_of(select)).astype(BF)
        second_down_part = (
            adapter_scale * transpose_then_product(both_halves(low_down), cols_of_core(cotangent))
        ).astype(BF)
        late = jnp.concatenate(
            [seconds]
            + [delta_attn[:, i * rank_cols : (i + 1) * rank_cols] for i in range(3)]
            + [second_down_part[:, at : at + rank_cols] for at in range(0, half_width, rank_cols)]
            + [second_output_blocks, first_output],
            axis=0,
        )
        got_late = exchange(late, DP, n)
        got_units, got_mlp, back, out_sum, grad_middle = after(
            [got_units, got_mlp, back, out_sum, grad_middle], late
        )

        def join_ring(value):
            found = [value] + [move(value, f"z{r}") for r in range(1, ring_size)]
            back = jnp.stack(found[::-1] + found[::-1], axis=0)
            return take(back, ring_size - 1 - ring_at, ring_size)

        def pair(bit, value, received):
            return jnp.stack([jnp.where(bit == 0, value, received), jnp.where(bit == 0, received, value)])

        def of_core_pair(value):
            return pair(core, value, other_core(value))

        units_all = join_ring(total(got_units))
        units_all = jnp.swapaxes(pair(bit_y, units_all, move(units_all, "y")), 0, 1)
        units_all = units_all.reshape(chunks, 3 * WIDTH, rank_cols)
        units_all = of_core_pair(pair(bit_x, units_all, move(units_all, "x"))).astype(F32)

        def unit_columns(start):
            return jnp.concatenate(
                [
                    units_all[c, h, j, at : at + rank_cols]
                    for c in range(2)
                    for h in range(2)
                    for j in range(chunks)
                    for at in range(start, start + WIDTH, rank_cols)
                ],
                axis=1,
            )

        gradient_second_gate, gradient_second_up = unit_columns(0), unit_columns(WIDTH)
        delta_in_down = units_all[:, :, :, 2 * WIDTH :].reshape(-1, rank_cols)

        layer_output = both_halves(
            (
                half_of(v["middle"])
                + out_sum[:, :width]
                + adapter_scale * matrix_product(low_down, second_down)
            ).astype(BF)
        )
        back_half = half_of(back).astype(F32) + other_core(
            take(back, (1 - core) * half_rows, half_rows)
        ).astype(F32)
        grad_normed_a = back_half + product_with_transpose(half_of(grad_low_attn), attn_in)
        grad_in = both_halves(
            (grad_middle + rms_back(half_of(hidden_wide), attn_gain_f, grad_normed_a)).astype(BF)
        )

        sums = jnp.concatenate([total(got_mlp), total(got_late)], axis=0)
        cut = got_mlp.shape[1]
        sums = join_ring(sums)
        by_x, by_y, by_both = (move(sums, link) for link in ("x", "y", "xy"))
        sums = pair(bit_y, pair(bit_x, sums, by_x), pair(bit_x, by_y, by_both))
        sums = of_core_pair(jnp.transpose(sums, (2, 0, 1, 3, 4)))

        def parts_of(value, sizes):
            value = value.reshape(2, -1, rank_cols)
            at, parts = 0, []
            for size in sizes:
                parts.append(value[:, at : at + size].astype(F32))
                at += size
            return parts

        query_cols, key_cols = second_query.shape[1], second_key.shape[1]
        mlp_parts = parts_of(sums[..., :cut, :], [half_width] * 2)
        late_parts = parts_of(sums[..., cut:, :], [seconds.shape[0]] + [half_width] * 6)

        def rows(part):
            return part.reshape(-1, rank_cols)

        def columns(part):
            return jnp.concatenate(
                [part[c, at : at + rank_cols] for c in range(2) for at in range(0, part.shape[1], rank_cols)],
                axis=1,
            )

        late_seconds = columns(late_parts[0])

        def second_of(start, size):
            per_core = late_seconds.shape[1] // 2
            return jnp.concatenate(
                [late_seconds[:, c * per_core + start : c * per_core + start + size] for c in range(2)],
                axis=1,
            )

        return (
            layer_output,
            grad_in,
            rows(late_parts[1]),
            second_of(0, query_cols),
            rows(late_parts[2]),
            second_of(query_cols, key_cols),
            rows(late_parts[3]),
            second_of(query_cols + key_cols, key_cols),
            rows(late_parts[6]),
            columns(late_parts[5]),
            rows(mlp_parts[0]),
            gradient_second_gate,
            rows(mlp_parts[1]),
            gradient_second_up,
            delta_in_down,
            columns(late_parts[4]),
        )

    return body


def solution(mesh):
    n, tensor = mesh.shape["dp"], mesh.shape["tensor"]
    split = jax.sharding.Mesh(mesh.devices.reshape(n // 4, 2, 2, tensor), DP + ("tensor",))
    return jax.shard_map(
        make_body(n),
        mesh=split,
        in_specs=(
            P(DP, None), P(DP, None), P(), P(), P(DP, "tensor"), P(DP, "tensor"), P(DP, "tensor"),
            P("tensor", DP), P(DP, "tensor"), P(DP, "tensor"), P("tensor", DP), P(),
            P(None, "tensor"), P(), P(None, "tensor"), P(), P(None, "tensor"), P("tensor", None),
            P(), P(), P(None, "tensor"), P(), P(None, "tensor"), P("tensor", None), P(), P(DP, None),
        ),
        out_specs=(P(DP, None), P(DP, None)) + (P(),) * 14,
        check_vma=False,
    )
```

time: 1840 us -> 854 us (0.46)
  waiting for transfers between devices: 1120 us -> 323 us
  blocking collectives: 320 us -> 0 us
  matrix products: 285 us -> 9.79 us
  Pallas kernels: 0 us -> 209 us
  starting transfers between devices: 0.55 us -> 117 us
  local copies, waits for them, and re-layouts: 35.5 us -> 99.9 us
  other arithmetic: 53.4 us -> 82.3 us
    all_gather x10 -> x0, waiting for transfers between devices: 823 us -> none  [the longest x1 192 us: body(): lax.all_gather(w_up, 'dp', axis=0, tiled=True)]
    ppermute x0 -> x101, waiting for transfers between devices: none -> 323 us  [the longest x86 319 us: move(): return lax.ppermute(value, DP, perms[link])]
    psum x3 -> x0, blocking collectives: 311 us -> none  [the longest x1 300 us: body(): lax.psum((delta_in_query, gradient_second_query, delta_in_key, gradient_s...]
    psum x4 -> x0, waiting for transfers between devices: 293 us -> none  [the longest x1 272 us: body(): lax.psum((delta_in_query, gradient_second_query, delta_in_key, gradient_s...]
    dot_general x75 -> x7, matrix products: 285 us -> 9.79 us  [the longest x2 4.06 us: product_with_transpose(): lax.dot_general(left, right, (((1,), (1,)), ((), ())), preferred_element_...]
    pallas_call x0 -> x47, Pallas kernels: none -> 209 us  [the longest x6 124 us: feed_forward(): pl.pallas_call(kernel, out_shape=out_shape, in_specs=[SMEM] * 2 + [VMEM]...]
    ppermute x0 -> x101, starting transfers between devices: none -> 99.6 us  [the longest x86 97.5 us: move(): return lax.ppermute(value, DP, perms[link])]
    unnamed x182 -> x354, local copies, waits for them, and re-layouts: 21.8 us -> 69.8 us
  transfers between devices with their start and end apart: 14 -> 104, of which waited for: 10 -> 43; matrix products, arithmetic and copies ran while one was open for 12% -> 15% of each run, Pallas kernels for 0% -> 20%
where the time goes in v1:
time: 854 us; the launch traced here: 845 us
  waiting for transfers between devices  323 us (38%)
  Pallas kernels  209 us (24%)
  starting transfers between devices  117 us (14%)
  local copies, waits for them, and re-layouts  99.9 us (12%)
  other arithmetic  82.3 us (10%)
  matrix products  9.79 us (1%)
    ppermute x86, waiting for transfers between devices, move(): return lax.ppermute(value, DP, perms[link])  319 us
    pallas_call x6, Pallas kernels, feed_forward(): pl.pallas_call(kernel, out_shape=out_shape, in_specs=[SMEM] * 2 + [VMEM]...  124 us
    ppermute x86, starting transfers between devices, move(): return lax.ppermute(value, DP, perms[link])  97.5 us
    unnamed x354, local copies, waits for them, and re-layouts  69.8 us
    pallas_call x1, Pallas kernels, attention_back(): pl.pallas_call(kernel, out_shape=[jax.ShapeDtypeStruct((tokens, width), B...  36.7 us
    pallas_call x1, Pallas kernels, attention(): pl.pallas_call(kernel, out_shape=[jax.ShapeDtypeStruct((k_cols, tokens),...  20.4 us
    all_to_all x3, starting transfers between devices, exchange(): return lax.all_to_all(value.reshape(parts, share, rank_cols), axes, 0, 0)  17.8 us
  transfers between devices with their start and end apart: 104, of which 43 were waited for; matrix products, arithmetic and copies ran while one was open for 15% of the time, Pallas kernels for 20%

profile of v1, /device:TPU:0, one launch (start us, length us, event | category | flops | bytes accessed | tf_op | source)
XLA Modules:
  0.0 845.3 jit_solution(326996601936760156)
XLA Ops:
  99.2 12.3 %collective-permute-done.12.refs_3_.refs_16_.refs_42_ = bf16[320,768]{1,0:T(8,128)(2,1)S(1)} collective-permute-done((bf16[320,768]{1,0:T(8,128)(2,1)S(1)}, bf16[320,768]{1,0:T(8,128)(2,1)S(1)}, u32[]{:S(2)}, u32[]{:S(2)}) %collective-permute-start.12) | collective-permute-done | bytes 491552 | tf_op jit(solution)/shard_map/ppermute | solution.py:833
  122.9 13.8 %collective-permute-done.15.refs_1_ = bf16[160,1600]{1,0:T(8,128)(2,1)S(1)} collective-permute-done((bf16[160,1600]{1,0:T(8,128)(2,1)}, bf16[160,1600]{1,0:T(8,128)(2,1)S(1)}, u32[]{:S(2)}, u32[]{:S(2)}) %collective-permute-start.15) | collective-permute-done | bytes 512032 | tf_op jit(solution)/shard_map/ppermute | solution.py:833
  140.1 13.8 %shard_map.373 = (bf16[1280,512]{1,0:T(8,128)(2,1)}, bf16[320,512]{1,0:T(8,128)(2,1)S(1)}, bf16[2560,1600]{1,0:T(8,128)(2,1)}) custom-call(s32[16]{0:T(128)S(1)} %stack.134.place_ref, bf16[512,2560]{1,0:T(8,128)(2,1)} %copy-done.46, bf16[512,128]{1,0:T(8,128)(2,1)S(1)} %get-tuple-element.448.lq_ref, bf16[512,128]{1,0:T(8,128)(2,1)S(1)} %get-tuple-element.447.lk_ref, ...), custom_call_target="tpu_custom_call" | custom-call | flops 4194304000 | bytes 16384000 | tf_op jit(solution)/shard_map/pallas_call | solution.py:218
  180.4 11.0 %collective-permute-done.19.refs_2_.refs_3_ = bf16[320,1600]{1,0:T(8,128)(2,1)S(1)} collective-permute-done((bf16[320,1600]{1,0:T(8,128)(2,1)}, bf16[320,1600]{1,0:T(8,128)(2,1)S(1)}, u32[]{:S(2)}, u32[]{:S(2)}) %collective-permute-start.19) | collective-permute-done | bytes 1024032 | tf_op jit(solution)/shard_map/ppermute | solution.py:833
  212.4 14.3 %collective-permute-done.22.refs_2_.refs_5_ = bf16[320,1600]{1,0:T(8,128)(2,1)S(1)} collective-permute-done((bf16[320,1600]{1,0:T(8,128)(2,1)}, bf16[320,1600]{1,0:T(8,128)(2,1)S(1)}, u32[]{:S(2)}, u32[]{:S(2)}) %collective-permute-start.22) | collective-permute-done | bytes 1024032 | tf_op jit(solution)/shard_map/ppermute | solution.py:833
  232.8 8.7 %collective-permute-done.40.refs_4_.refs_20_.refs_28_ = bf16[320,768]{1,0:T(8,128)(2,1)S(1)} collective-permute-done((bf16[320,768]{1,0:T(8,128)(2,1)}, bf16[320,768]{1,0:T(8,128)(2,1)S(1)}, u32[]{:S(2)}, u32[]{:S(2)}) %collective-permute-start.40) | collective-permute-done | bytes 491552 | tf_op jit(solution)/shard_map/ppermute | solution.py:833
  258.7 20.4 %shard_map.378 = (bf16[320,512]{1,0:T(8,128)(2,1)S(1)}, bf16[512,1280]{1,0:T(8,128)(2,1)}, f32[4,4,512]{2,1,0:T(4,128)S(1)}, bf16[512,2560]{1,0:T(8,128)(2,1)}, ...) custom-call(s32[16]{0:T(128)S(1)} %stack.134.place_ref, bf16[512,2560]{1,0:T(8,128)(2,1)} %copy-done.46, ...), custom_call_target="tpu_custom_call" | custom-call | flops 8388608000 | bytes 16384000 | tf_op jit(solution)/shard_map/pallas_call | solution.py:319
  303.0 8.8 %shard_map.379 = (f32[512,2560]{1,0:T(8,128)}, bf16[512,2816]{1,0:T(8,128)(2,1)S(1)}, bf16[512,128]{1,0:T(8,128)(2,1)S(1)}) custom-call(bf16[512,2560]{1,0:T(8,128)(2,1)S(1)} %copy-done.2, bf16[512,2560]{1,0:T(8,128)(2,1)} %get-tuple-element.139.b0, bf16[512,2560]{1,0:T(8,128)(2,1)} %collective-permute-done.26.b1, f32[512,128]{1,0:T(8,128)} %get-tuple-element.140.l0, ...), custom_call_target="tpu_custom_call" | custom-call | flops 1006632960 | bytes 18350080 | tf_op jit(solution)/shard_map/pallas_call | solution.py:530
  332.3 10.5 %collective-permute-done.52.refs_1_ = bf16[320,768]{1,0:T(8,128)(2,1)} collective-permute-done((bf16[320,768]{1,0:T(8,128)(2,1)}, bf16[320,768]{1,0:T(8,128)(2,1)}, u32[]{:S(2)}, u32[]{:S(2)}) %collective-permute-start.52) | collective-permute-done | bytes 491552 | tf_op jit(solution)/shard_map/ppermute | solution.py:833
  358.1 18.0 %shard_map.398 = (bf16[1024,256]{1,0:T(8,128)(2,1)}, bf16[1024,256]{1,0:T(8,128)(2,1)}, bf16[1024,512]{1,0:T(8,128)(2,1)}, bf16[1024,512]{1,0:T(8,128)(2,1)}, bf...) custom-call(s32[16]{0:T(128)} %stack.147.place_ref, s32[1]{0:T(128)} %bitcast.20.core_ref, bf16[512,2816]{1,0:T(8,128)(2,1)} %copy-done.3, ...), custom_call_target="tpu_custom_call" | custom-call | flops 8053063680 | bytes 10485760 | tf_op jit(solution)/shard_map/pallas_call | solution.py:807
  378.0 18.0 %shard_map.395 = (bf16[1024,256]{1,0:T(8,128)(2,1)}, bf16[1024,256]{1,0:T(8,128)(2,1)}, bf16[1024,512]{1,0:T(8,128)(2,1)}, bf16[1024,512]{1,0:T(8,128)(2,1)}, bf...) custom-call(s32[16]{0:T(128)} %stack.147.place_ref, s32[1]{0:T(128)} %bitcast.20.core_ref, bf16[512,2816]{1,0:T(8,128)(2,1)} %copy-done.3, ...), custom_call_target="tpu_custom_call" | custom-call | flops 8053063680 | bytes 10485760 | tf_op jit(solution)/shard_map/pallas_call | solution.py:807
  398.4 28.6 %shard_map.404 = (f32[1024,2816]{1,0:T(8,128)}, f32[1024,2688]{1,0:T(8,128)}) custom-call(s32[16]{0:T(128)} %stack.147.place_ref, s32[1]{0:T(128)} %bitcast.20.core_ref, bf16[1024,256]{1,0:T(8,128)(2,1)} %get-tuple-element.177.refs_0_, bf16[1024,512]{1,0:T(8,128)(2,1)} %get-tuple-element.178.refs_1_, bf16[1024,256]{1,0:T(8,128)(2,1)} %get-tuple-element.163.refs_5_.refs_2_, ...), custom_call_target="tpu_custom_call" | custom-call | flops 16106127360 | bytes 10485760 | tf_op jit(solution)/shard_map/pallas_call | solution.py:807
  431.8 11.3 %shard_map.397 = (bf16[1024,256]{1,0:T(8,128)(2,1)}, bf16[1024,512]{1,0:T(8,128)(2,1)}, bf16[768,128]{1,0:T(8,128)(2,1)}) custom-call(s32[16]{0:T(128)} %stack.147.place_ref, s32[1]{0:T(128)} %bitcast.20.core_ref, bf16[512,2816]{1,0:T(8,128)(2,1)} %copy-done.3, bf16[256,2816]{1,0:T(8,128)(2,1)} %collective-permute-done.48.refs_2_.refs_1_.refs_9_.refs_5_, ...), custom_call_target="tpu_custom_call" | custom-call | flops 4026531840 | bytes 10485760 | tf_op jit(solution)/shard_map/pallas_call | solution.py:807
  445.5 12.2 %collective-permute-done.69.refs_11_.refs_1_.refs_33_ = bf16[320,768]{1,0:T(8,128)(2,1)} collective-permute-done((bf16[320,768]{1,0:T(8,128)(2,1)}, bf16[320,768]{1,0:T(8,128)(2,1)}, u32[]{:S(2)}, u32[]{:S(2)}) %collective-permute-start.69) | collective-permute-done | bytes 491552 | tf_op jit(solution)/shard_map/ppermute | solution.py:833
  458.1 10.1 %collective-permute-done.71.refs_13_.refs_1_.refs_35_ = bf16[320,768]{1,0:T(8,128)(2,1)} collective-permute-done((bf16[320,768]{1,0:T(8,128)(2,1)}, bf16[320,768]{1,0:T(8,128)(2,1)}, u32[]{:S(2)}, u32[]{:S(2)}) %collective-permute-start.71) | collective-permute-done | bytes 491552 | tf_op jit(solution)/shard_map/ppermute | solution.py:833
  468.6 11.3 %shard_map.403 = (bf16[1024,256]{1,0:T(8,128)(2,1)}, bf16[1024,512]{1,0:T(8,128)(2,1)}, bf16[768,128]{1,0:T(8,128)(2,1)}) custom-call(s32[16]{0:T(128)} %stack.147.place_ref, s32[1]{0:T(128)} %bitcast.20.core_ref, bf16[512,2816]{1,0:T(8,128)(2,1)} %copy-done.3, bf16[256,2816]{1,0:T(8,128)(2,1)} %collective-permute-done.48.refs_2_.refs_1_.refs_9_.refs_5_, ...), custom_call_target="tpu_custom_call" | custom-call | flops 4026531840 | bytes 10485760 | tf_op jit(solution)/shard_map/pallas_call | solution.py:807
  489.7 8.5 %collective-permute-done.75.refs_15_ = bf16[320,768]{1,0:T(8,128)(2,1)} collective-permute-done((bf16[320,768]{1,0:T(8,128)(2,1)}, bf16[320,768]{1,0:T(8,128)(2,1)}, u32[]{:S(2)}, u32[]{:S(2)}) %collective-permute-start.75) | collective-permute-done | bytes 491552 | tf_op jit(solution)/shard_map/ppermute | solution.py:833
  504.2 36.4 %shard_map.409 = (bf16[2,256,2816]{2,1,0:T(8,128)(2,1)}, bf16[2,256,2816]{2,1,0:T(8,128)(2,1)}, bf16[2,256,2688]{2,1,0:T(8,128)(2,1)}, bf16[2,256,2688]{2,1,0:T(...) custom-call(s32[16]{0:T(128)} %stack.147.place_ref, ...), custom_call_target="tpu_custom_call" | custom-call | flops 16106127360 | bytes 10485760 | tf_op jit(solution)/shard_map/pallas_call | solution.py:807
  563.8 19.3 %collective-permute-done.78.p2 = bf16[256,2816]{1,0:T(8,128)(2,1)} collective-permute-done((bf16[256,2816]{1,0:T(8,128)(2,1)}, bf16[256,2816]{1,0:T(8,128)(2,1)}, u32[]{:S(2)}, u32[]{:S(2)}) %collective-permute-start.78) | collective-permute-done | bytes 1441824 | tf_op jit(solution)/shard_map/ppermute | solution.py:833
  607.8 36.7 %shard_map.411 = (bf16[512,2560]{1,0:T(8,128)(2,1)}, f32[512,384]{1,0:T(8,128)}, bf16[1920,128]{1,0:T(8,128)(2,1)}, bf16[1280,128]{1,0:T(8,128)(2,1)}, bf16[1280,128]{1,0:T(8,128)(2,1)}) custom-call(s32[1]{0:T(128)} %bitcast.20.core_ref, bf16[256,2560]{1,0:T(8,128)(2,1)} %get-tuple-element.188.mine_hbm.refs_1_, ...), custom_call_target="tpu_custom_call" | custom-call | flops 41943040000 | bytes 16384000 | tf_op jit(solution)/shard_map/pallas_call | solution.py:473
  697.9 9.7 %collective-permute-done.98 = bf16[4,672,128]{2,1,0:T(8,128)(2,1)} collective-permute-done((bf16[4,672,128]{2,1,0:T(8,128)(2,1)}, bf16[4,672,128]{2,1,0:T(8,128)(2,1)}, u32[]{:S(2)}, u32[]{:S(2)}) %collective-permute-start.98) | collective-permute-done | bytes 688160 | tf_op jit(solution)/shard_map/ppermute | solution.py:833
  719.7 39.4 %collective-permute-done.99 = bf16[7,768,128]{2,1,0:T(8,128)(2,1)S(1)} collective-permute-done((bf16[7,768,128]{2,1,0:T(8,128)(2,1)S(1)}, bf16[7,768,128]{2,1,0:T(8,128)(2,1)S(1)}, u32[]{:S(2)}, u32[]{:S(2)}) %collective-permute-start.99) | collective-permute-done | bytes 1376288 | tf_op jit(solution)/shard_map/ppermute | solution.py:833
  776.5 13.7 %collective-permute-done.89 = bf16[760,128]{1,0:T(8,128)(2,1)S(1)} collective-permute-done((bf16[760,128]{1,0:T(8,128)(2,1)S(1)}, bf16[760,128]{1,0:T(8,128)(2,1)S(1)}, u32[]{:S(2)}, u32[]{:S(2)}) %collective-permute-start.89) | collective-permute-done | bytes 194592 | tf_op jit(solution)/shard_map/ppermute | solution.py:833
  796.7 30.0 %collective-permute-done.91 = bf16[4,760,128]{2,1,0:T(8,128)(2,1)S(1)} collective-permute-done((bf16[4,760,128]{2,1,0:T(8,128)(2,1)S(1)}, bf16[4,760,128]{2,1,0:T(8,128)(2,1)S(1)}, u32[]{:S(2)}, u32[]{:S(2)}) %collective-permute-start.91) | collective-permute-done | bytes 778272 | tf_op jit(solution)/shard_map/ppermute | solution.py:833
  (755 shorter events, 424.7 us)
Async XLA Ops:
  2.7 88.9 %collective-permute-start.14 = (bf16[160,1600]{1,0:T(8,128)(2,1)}, bf16[160,1600]{1,0:T(8,128)(2,1)}, u32[]{:S(2)}, u32[]{:S(2)}) collective-permute-start(bf16[160,1600]{1,0:T(8,128)(2,1)} %pad_maximum_fusion.37), channel_id=1, source_target_pairs={{0,4},{2,6},{4,0},{6,2},{8,12},{10,14},{12,8},{14,10},{16,20},{18,... | collective-permute-start | bytes 1536008 | tf_op jit(solution)/shard_map/ppermute | solution.py:833
  5.7 33.4 %collective-permute-start.1 = (bf16[160,1600]{1,0:T(8,128)(2,1)}, bf16[160,1600]{1,0:T(8,128)(2,1)}, u32[]{:S(2)}, u32[]{:S(2)}) collective-permute-start(bf16[160,1600]{1,0:T(8,128)(2,1)} %pad_maximum_fusion.37), channel_id=1, source_target_pairs={{0,8},{2,10},{4,12},{6,14},{8,16},{10,18},{12,20},{14,22},{16,24},... | collective-permute-start | bytes 1536008 | tf_op jit(solution)/shard_map/ppermute | solution.py:833
  16.1 61.4 %collective-permute-start.8 = (bf16[160,1536]{1,0:T(8,128)(2,1)}, bf16[160,1536]{1,0:T(8,128)(2,1)}, u32[]{:S(2)}, u32[]{:S(2)}) collective-permute-start(bf16[160,1536]{1,0:T(8,128)(2,1)} %get-tuple-element.438), channel_id=1, source_target_pairs={{0,2},{2,0},{4,6},{6,4},{8,10},{10,8},{12,14},{14,12},{16,18},{18,... | collective-permute-start | bytes 1474568 | tf_op jit(solution)/shard_map/ppermute | solution.py:833
  92.6 62.1 %collective-permute-start.28 = (bf16[320,768]{1,0:T(8,128)(2,1)}, bf16[320,768]{1,0:T(8,128)(2,1)}, u32[]{:S(2)}, u32[]{:S(2)}) collective-permute-start(bf16[320,768]{1,0:T(8,128)(2,1)} %shard_map.380.refs_6_.refs_14_), channel_id=1, source_target_pairs={{0,8},{2,10},{4,12},{6,14},{8,16},{10,18},{12,20},{14,22},{16,24},... | collective-permute-start | bytes 1474568 | tf_op jit(solution)/shard_map/ppermute | solution.py:833
  121.9 78.5 %collective-permute-start.64 = (bf16[320,768]{1,0:T(8,128)(2,1)}, bf16[320,768]{1,0:T(8,128)(2,1)}, u32[]{:S(2)}, u32[]{:S(2)}) collective-permute-start(bf16[320,768]{1,0:T(8,128)(2,1)} %shard_map.383.refs_1_), channel_id=1, source_target_pairs={{0,4},{2,6},{4,0},{6,2},{8,12},{10,14},{12,8},{14,10},{16,20},{18,... | collective-permute-start | bytes 1474568 | tf_op jit(solution)/shard_map/ppermute | solution.py:833
  231.0 48.8 %collective-permute-start.37 = (bf16[320,768]{1,0:T(8,128)(2,1)}, bf16[320,768]{1,0:T(8,128)(2,1)}, u32[]{:S(2)}, u32[]{:S(2)}) collective-permute-start(bf16[320,768]{1,0:T(8,128)(2,1)} %shard_map.385.refs_8_.refs_34_), channel_id=1, source_target_pairs={{0,4},{2,6},{4,0},{6,2},{8,12},{10,14},{12,8},{14,10},{16,20},{18,... | collective-permute-start | bytes 1474568 | tf_op jit(solution)/shard_map/ppermute | solution.py:833
  232.8 47.1 %collective-permute-start.36 = (bf16[320,768]{1,0:T(8,128)(2,1)}, bf16[320,768]{1,0:T(8,128)(2,1)}, u32[]{:S(2)}, u32[]{:S(2)}) collective-permute-start(bf16[320,768]{1,0:T(8,128)(2,1)} %shard_map.385.refs_8_.refs_34_), channel_id=1, source_target_pairs={{0,8},{2,10},{4,12},{6,14},{8,16},{10,18},{12,20},{14,22},{16,24},... | collective-permute-start | bytes 1474568 | tf_op jit(solution)/shard_map/ppermute | solution.py:833
  281.6 32.4 %collective-permute-start.55 = (bf16[320,768]{1,0:T(8,128)(2,1)}, bf16[320,768]{1,0:T(8,128)(2,1)}, u32[]{:S(2)}, u32[]{:S(2)}) collective-permute-start(bf16[320,768]{1,0:T(8,128)(2,1)} %get-tuple-element.158.refs_17_.refs_43_), channel_id=1, source_target_pairs={{0,4},{2,6},{4,0},{6,2},{8,12},{10,14},{12,8},{14,10},{16,20},{18,... | collective-permute-start | bytes 1474568 | tf_op jit(solution)/shard_map/ppermute | solution.py:833
  351.9 44.1 %collective-permute-start.53 = (bf16[320,768]{1,0:T(8,128)(2,1)}, bf16[320,768]{1,0:T(8,128)(2,1)}, u32[]{:S(2)}, u32[]{:S(2)}) collective-permute-start(bf16[320,768]{1,0:T(8,128)(2,1)} %get-tuple-element.156.refs_8_.refs_21_), channel_id=1, source_target_pairs={{0,4},{2,6},{4,0},{6,2},{8,12},{10,14},{12,8},{14,10},{16,20},{18,... | collective-permute-start | bytes 1474568 | tf_op jit(solution)/shard_map/ppermute | solution.py:833
  376.1 67.0 %collective-permute-start.68 = (bf16[320,768]{1,0:T(8,128)(2,1)}, bf16[320,768]{1,0:T(8,128)(2,1)}, u32[]{:S(2)}, u32[]{:S(2)}) collective-permute-start(bf16[320,768]{1,0:T(8,128)(2,1)} %get-tuple-element.172.refs_0_), channel_id=1, source_target_pairs={{0,8},{2,10},{4,12},{6,14},{8,16},{10,18},{12,20},{14,22},{16,24},... | collective-permute-start | bytes 1474568 | tf_op jit(solution)/shard_map/ppermute | solution.py:833
  377.0 66.1 %collective-permute-start.65 = (bf16[320,768]{1,0:T(8,128)(2,1)}, bf16[320,768]{1,0:T(8,128)(2,1)}, u32[]{:S(2)}, u32[]{:S(2)}) collective-permute-start(bf16[320,768]{1,0:T(8,128)(2,1)} %get-tuple-element.169.refs_6_.refs_28_), channel_id=1, source_target_pairs={{0,4},{2,6},{4,0},{6,2},{8,12},{10,14},{12,8},{14,10},{16,20},{18,... | collective-permute-start | bytes 1474568 | tf_op jit(solution)/shard_map/ppermute | solution.py:833
  549.2 33.9 %collective-permute-start.78 = (bf16[256,2816]{1,0:T(8,128)(2,1)}, bf16[256,2816]{1,0:T(8,128)(2,1)}, u32[]{:S(2)}, u32[]{:S(2)}) collective-permute-start(bf16[256,2816]{1,0:T(8,128)(2,1)} %fusion.3.refs_8_), channel_id=1, source_target_pairs={{0,2},{2,0},{4,6},{6,4},{8,10},{10,8},{12,14},{14,12},{16,18},{18,... | collective-permute-start | bytes 4325384 | tf_op jit(solution)/shard_map/ppermute | solution.py:833
  550.8 47.5 %collective-permute-start.81 = (bf16[2,256,2688]{2,1,0:T(8,128)(2,1)}, bf16[2,256,2688]{2,1,0:T(8,128)(2,1)}, u32[]{:S(2)}, u32[]{:S(2)}) collective-permute-start(bf16[2,256,2688]{2,1,0:T(8,128)(2,1)} %get-tuple-element.211), channel_id=1, source_target_pairs={{0,1},{1,0},{2,3},{3,2},{4,5},{5,4},{6,7},{7,6},{8,9},{9,8},{10,11... | collective-permute-start | bytes 8257544 | tf_op jit(solution)/shard_map/ppermute | solution.py:836
  557.8 44.4 %all-to-all-start = ((bf16[8,672,128]{2,1,0:T(8,128)(2,1)}), bf16[8,672,128]{2,1,0:T(8,128)(2,1)}, u32[]{:S(2)}, u32[]{:S(2)}) async-start(bf16[8,672,128]{2,1,0:T(8,128)(2,1)} %bitcast.866), calls=%async_computation | async-start | bytes 2752512 | tf_op jit(solution)/shard_map/all_to_all | solution.py:1089
  601.6 42.9 %collective-permute-start.82 = (bf16[256,2688]{1,0:T(8,128)(2,1)}, bf16[256,2688]{1,0:T(8,128)(2,1)}, u32[]{:S(2)}, u32[]{:S(2)}) collective-permute-start(bf16[256,2688]{1,0:T(8,128)(2,1)} %shard_map.413), channel_id=1, source_target_pairs={{0,2},{2,0},{4,6},{6,4},{8,10},{10,8},{12,14},{14,12},{16,18},{18,... | collective-permute-start | bytes 4128776 | tf_op jit(solution)/shard_map/ppermute | solution.py:833
  602.2 42.3 %all-to-all-start.1 = ((bf16[16,160,128]{2,1,0:T(8,128)(2,1)}), bf16[16,160,128]{2,1,0:T(8,128)(2,1)}, u32[]{:S(2)}, u32[]{:S(2)}) async-start(bf16[16,160,128]{2,1,0:T(8,128)(2,1)} %bitcast.865), calls=%async_computation.1 | async-start | bytes 1310720 | tf_op jit(solution)/shard_map/all_to_all | solution.py:1089
  671.2 41.4 %collective-permute-start.86 = (bf16[256,2560]{1,0:T(8,128)(2,1)}, bf16[256,2560]{1,0:T(8,128)(2,1)}, u32[]{:S(2)}, u32[]{:S(2)}) collective-permute-start(bf16[256,2560]{1,0:T(8,128)(2,1)} %constant_dynamic-slice_fusion.32), channel_id=1, source_target_pairs={{0,1},{1,0},{2,3},{3,2},{4,5},{5,4},{6,7},{7,6},{8,9},{9,8},{10,11... | collective-permute-start | bytes 3932168 | tf_op jit(solution)/shard_map/ppermute | solution.py:836
  686.2 76.5 %all-to-all-start.2 = ((bf16[16,600,128]{2,1,0:T(8,128)(2,1)}), bf16[16,600,128]{2,1,0:T(8,128)(2,1)}, u32[]{:S(2)}, u32[]{:S(2)}) async-start(bf16[16,600,128]{2,1,0:T(8,128)(2,1)} %bitcast.47), calls=%async_computation.2 | async-start | bytes 4915200 | tf_op jit(solution)/shard_map/all_to_all | solution.py:1089
  709.0 50.1 %collective-permute-start.99 = (bf16[7,768,128]{2,1,0:T(8,128)(2,1)S(1)}, bf16[7,768,128]{2,1,0:T(8,128)(2,1)S(1)}, u32[]{:S(2)}, u32[]{:S(2)}) collective-permute-start(bf16[7,768,128]{2,1,0:T(8,128)(2,1)S(1)} %bitcast.861), channel_id=1, source_target_pairs={{0,2},{2,0},{4,6},{6,4},{8,10},{10,8},{12,14},{14,12},{16,18},{18,... | collective-permute-start | bytes 4128776 | tf_op jit(solution)/shard_map/ppermute | solution.py:833
  717.8 43.3 %collective-permute-start.87 = (bf16[256,2560]{1,0:T(8,128)(2,1)S(1)}, bf16[256,2560]{1,0:T(8,128)(2,1)S(1)}, u32[]{:S(2)}, u32[]{:S(2)}) collective-permute-start(bf16[256,2560]{1,0:T(8,128)(2,1)S(1)} %add_convert_fusion.2), channel_id=1, source_target_pairs={{0,1},{1,0},{2,3},{3,2},{4,5},{5,4},{6,7},{7,6},{8,9},{9,8},{10,11... | collective-permute-start | bytes 3932168 | tf_op jit(solution)/shard_map/ppermute | solution.py:836
  761.0 33.1 %collective-permute-start.100 = (bf16[2,7,768,128]{3,2,1,0:T(8,128)(2,1)}, bf16[2,7,768,128]{3,2,1,0:T(8,128)(2,1)}, u32[]{:S(2)}, u32[]{:S(2)}) collective-permute-start(bf16[2,7,768,128]{3,2,1,0:T(8,128)(2,1)} %pad_maximum_fusion.1), channel_id=1, source_target_pairs={{0,1},{1,0},{2,3},{3,2},{4,5},{5,4},{6,7},{7,6},{8,9},{9,8},{10,11... | collective-permute-start | bytes 8257544 | tf_op jit(solution)/shard_map/ppermute | solution.py:836
  790.5 36.3 %collective-permute-start.93 = (bf16[4,760,128]{2,1,0:T(8,128)(2,1)S(1)}, bf16[4,760,128]{2,1,0:T(8,128)(2,1)S(1)}, u32[]{:S(2)}, u32[]{:S(2)}) collective-permute-start(bf16[4,760,128]{2,1,0:T(8,128)(2,1)S(1)} %constant_dynamic-slice_fusion.31), channel_id=1, source_target_pairs={{0,6},{2,4},{4,2},{6,0},{8,14},{10,12},{12,10},{14,8},{16,22},{18,... | collective-permute-start | bytes 2334728 | tf_op jit(solution)/shard_map/ppermute | solution.py:833
  791.7 35.5 %collective-permute-start.92 = (bf16[4,760,128]{2,1,0:T(8,128)(2,1)S(1)}, bf16[4,760,128]{2,1,0:T(8,128)(2,1)S(1)}, u32[]{:S(2)}, u32[]{:S(2)}) collective-permute-start(bf16[4,760,128]{2,1,0:T(8,128)(2,1)S(1)} %constant_dynamic-slice_fusion.31), channel_id=1, source_target_pairs={{0,4},{2,6},{4,0},{6,2},{8,12},{10,14},{12,8},{14,10},{16,20},{18,... | collective-permute-start | bytes 2334728 | tf_op jit(solution)/shard_map/ppermute | solution.py:833
  793.5 33.2 %collective-permute-start.91 = (bf16[4,760,128]{2,1,0:T(8,128)(2,1)S(1)}, bf16[4,760,128]{2,1,0:T(8,128)(2,1)S(1)}, u32[]{:S(2)}, u32[]{:S(2)}) collective-permute-start(bf16[4,760,128]{2,1,0:T(8,128)(2,1)S(1)} %constant_dynamic-slice_fusion.31), channel_id=1, source_target_pairs={{0,2},{2,0},{4,6},{6,4},{8,10},{10,8},{12,14},{14,12},{16,18},{18,... | collective-permute-start | bytes 2334728 | tf_op jit(solution)/shard_map/ppermute | solution.py:833
  (202 other events, 2315.4 us)

commit v2 on v1

--- a/solution.py
+++ b/solution.py
@@ -12,6 +12,8 @@
 PROMPT = 256
 CONT_LEN = 128
 WIDTH = 256
+ADAPTER_COLS = 128
+BLOCKS = 8
 
 adapter_scale = 2.0
 norm_eps = 1e-05
@@ -356,8 +358,7 @@
 
     def kernel(
         core_ref, mine_hbm, other_hbm, sel_ref, so_ref, lo_ref, att_ref, io_ref, a0_hbm, a1_hbm, q_ref, k_ref, v_ref, lse_ref, cos_ref, sin_ref,
-        sq_ref, sk_ref, sv_ref, lq_ref, lk_ref, lv_ref, back_out, low_out, second_out,
-        first_out, second_o_out, a0, a1, gb_ref, glo_ref, ga_s, g_s, gw_s, sems,
+        sq_ref, sk_ref, sv_ref, lq_ref, lk_ref, lv_ref, back_out, low_out, factor_out, a0, a1, gb_ref, glo_ref, ga_s, g_s, gw_s, sems,
     ):
         mine = core_ref[0]
         copies = [
@@ -377,16 +378,18 @@
         for i in (2, 3):
             copies[i].wait()
         glo_ref[...] = (adapter_scale * nt(gb_ref[...], so_ref[...]) * sel_ref[...]).astype(BF)
-        first_out[...] = jnp.dot(
+        at_second = q_cols + 2 * k_cols
+        at_first = at_second + width // 2
+        factor_out[at_first : at_first + q_cols, :] = jnp.dot(
             att_ref[...].T, glo_ref[...], preferred_element_type=F32
         ).astype(BF)
-        part = jnp.dot(
-            lo_ref[...].T,
-            gb_ref[:, pl.ds(pl.multiple_of(mine * (width // 2), 128), width // 2)],
-            preferred_element_type=F32,
-        )
-        for at in range(0, width // 2, rank):
-            second_o_out[at : at + rank, :] = (adapter_scale * part[:, at : at + rank]).astype(BF)
+        own = gb_ref[:, pl.ds(pl.multiple_of(mine * (width // 2), 128), width // 2)]
+        factor_out[at_second:at_first, :] = (
+            adapter_scale * jnp.dot(own.T, lo_ref[...], preferred_element_type=F32)
+        ).astype(BF)
+        factor_out[at_first + q_cols :, :] = jnp.zeros(
+            (4 * q_cols - at_first - q_cols, rank), BF
+        )
         copies[0].wait()
         step = 4 * HEAD_DIM
         for at in range(0, q_cols, step):
@@ -447,17 +450,14 @@
 
         lax.fori_loop(0, kv_heads, one_head, 0)
         gw_s[...] = g_s[...].T
-        part = [
-            jnp.dot(low[...].T, gw_s[:, at : at + size], preferred_element_type=F32)
-            for at, size, low in (
-                (0, q_cols, lq_ref),
-                (q_cols, k_cols, lk_ref),
-                (q_cols + k_cols, k_cols, lv_ref),
-            )
-        ]
-        part = jnp.concatenate(part, axis=1).astype(BF)
-        for at in range(0, q_cols + 2 * k_cols, rank):
-            second_out[at : at + rank, :] = part[:, at : at + rank]
+        for at, size, low in (
+            (0, q_cols, lq_ref),
+            (q_cols, k_cols, lk_ref),
+            (q_cols + k_cols, k_cols, lv_ref),
+        ):
+            factor_out[at : at + size, :] = jnp.dot(
+                g_s[at : at + size, :], low[...], preferred_element_type=F32
+            ).astype(BF)
         for i, (at, size, second) in enumerate(
             ((0, q_cols, sq_ref), (q_cols, k_cols, sk_ref), (q_cols + k_cols, k_cols, sv_ref))
         ):
@@ -475,12 +475,10 @@
         out_shape=[
             jax.ShapeDtypeStruct((tokens, width), BF),
             jax.ShapeDtypeStruct((tokens, 3 * rank), F32),
-            jax.ShapeDtypeStruct((q_cols + 2 * k_cols, rank), BF),
-            jax.ShapeDtypeStruct((q_cols, rank), BF),
-            jax.ShapeDtypeStruct((width // 2, rank), BF),
+            jax.ShapeDtypeStruct((4 * q_cols, rank), BF),
         ],
         in_specs=[SMEM, HBM, HBM] + [VMEM] * 5 + [HBM] * 2 + [VMEM] * 12,
-        out_specs=[VMEM] * 5,
+        out_specs=[VMEM] * 3,
         scratch_shapes=[
             pltpu.VMEM((width, cols), BF),
             pltpu.VMEM((width, cols), BF),
@@ -820,6 +818,200 @@
     )(places, core, *old_flat, *normed, *cot, *flat, *before)
     rest = out[n_sums:]
     return tuple(out[:n_sums]), list(zip(*(rest[i * n_new : (i + 1) * n_new] for i in range(3))))
+def adapter_columns(ids_ref):
+    sequences = ids_ref.shape[1]
+    shape = (sequences * RANK, ADAPTER_COLS)
+    row = lax.broadcasted_iota(jnp.int32, shape, 0)
+    column = lax.broadcasted_iota(jnp.int32, shape, 1)
+    start = jnp.zeros(shape, jnp.int32)
+    for i in range(sequences):
+        start = jnp.where(row // RANK == i, ids_ref[0, i] * RANK, start)
+    return (column == start + row % RANK).astype(F32).astype(BF)
+
+
+def pack(ids, factors, firsts):
+    block = factors.shape[0] // BLOCKS
+    sequences = ids.shape[1]
+    lanes = BLOCKS * sequences * RANK
+
+    def kernel(ids_ref, factor_ref, first_ref, factor_out, first_out, chosen_out):
+        chosen = adapter_columns(ids_ref)
+        chosen_out[...] = jnp.concatenate(
+            [chosen[i * RANK : (i + 1) * RANK] for i in range(sequences)], axis=1
+        )
+        parts = [
+            nt(factor_ref[i * block : (i + 1) * block, :], chosen) for i in range(BLOCKS)
+        ]
+        factor_out[...] = jnp.concatenate(parts, axis=1).astype(BF)
+        parts = []
+        for i in range(BLOCKS):
+            q, s = i // 2, i % 2
+            parts.append(
+                nt(
+                    first_ref[s * block : (s + 1) * block, q * ADAPTER_COLS : (q + 1) * ADAPTER_COLS],
+                    chosen,
+                )
+            )
+        first_out[...] = jnp.concatenate(parts, axis=1).astype(BF)
+
+    return pl.pallas_call(
+        kernel,
+        out_shape=[jax.ShapeDtypeStruct((block, lanes), BF)] * 2
+        + [jax.ShapeDtypeStruct((RANK, sequences * ADAPTER_COLS), BF)],
+        in_specs=[SMEM, VMEM, VMEM],
+        out_specs=[VMEM] * 3,
+        compiler_params=pltpu.CompilerParams(vmem_limit_bytes=32 * 2**20),
+        cost_estimate=pl.CostEstimate(flops=5_000_000_000, transcendentals=0, bytes_accessed=0),
+    )(ids, factors, firsts)
+
+
+def unpack(got):
+    groups, share, lanes = got.shape
+    share -= RANK
+    each = lanes // BLOCKS
+    sequences = each // RANK
+
+    def kernel(got_ref, out_ref, total):
+        total[...] = jnp.zeros_like(total)
+
+        def one(g, _):
+            packed = got_ref[g]
+            chosen = jnp.concatenate(
+                [
+                    packed[share:, i * ADAPTER_COLS : (i + 1) * ADAPTER_COLS]
+                    for i in range(sequences)
+                ],
+                axis=0,
+            )
+            for i in range(BLOCKS):
+                total[i] += jnp.dot(
+                    packed[:share, i * each : (i + 1) * each], chosen, preferred_element_type=F32
+                )
+            return 0
+
+        lax.fori_loop(0, groups, one, 0)
+        out_ref[...] = total[...].astype(BF)
+
+    return pl.pallas_call(
+        kernel,
+        out_shape=jax.ShapeDtypeStruct((BLOCKS, share, ADAPTER_COLS), BF),
+        in_specs=[VMEM],
+        out_specs=VMEM,
+        scratch_shapes=[pltpu.VMEM((BLOCKS, share, ADAPTER_COLS), F32)],
+        compiler_params=pltpu.CompilerParams(vmem_limit_bytes=32 * 2**20),
+        cost_estimate=pl.CostEstimate(flops=5_000_000_000, transcendentals=0, bytes_accessed=0),
+    )(got)
+
+
+def unit_results(at, parts, chunks):
+    rows = parts[0].shape[0]
+    units = chunks * WIDTH
+
+    def kernel(at_ref, *refs):
+        gate_out, up_out, down_out = refs[4:]
+        for i in range(4):
+            core = at_ref[0] if i < 2 else 1 - at_ref[0]
+            bit = at_ref[1] if i % 2 == 0 else 1 - at_ref[1]
+            start = pl.multiple_of((core * 2 + bit) * units, 128)
+            for j in range(chunks):
+                for at in range(0, WIDTH, ADAPTER_COLS):
+                    to = pl.ds(pl.multiple_of(start + j * WIDTH + at, 128), ADAPTER_COLS)
+                    row = j * 3 * WIDTH + at
+                    gate_out[:, to] = refs[i][row : row + ADAPTER_COLS, :].astype(F32)
+                    row += WIDTH
+                    up_out[:, to] = refs[i][row : row + ADAPTER_COLS, :].astype(F32)
+                row = (j * 3 + 2) * WIDTH
+                to = pl.ds(pl.multiple_of(start + j * WIDTH, 128), WIDTH)
+                down_out[to, :] = refs[i][row : row + WIDTH, :].astype(F32)
+
+    return pl.pallas_call(
+        kernel,
+        out_shape=[
+            jax.ShapeDtypeStruct((ADAPTER_COLS, 4 * units), F32),
+            jax.ShapeDtypeStruct((ADAPTER_COLS, 4 * units), F32),
+            jax.ShapeDtypeStruct((4 * units, ADAPTER_COLS), F32),
+        ],
+        in_specs=[SMEM] + [VMEM] * 4,
+        out_specs=[VMEM] * 3,
+        compiler_params=pltpu.CompilerParams(vmem_limit_bytes=48 * 2**20),
+        cost_estimate=pl.CostEstimate(flops=8_000_000_000, transcendentals=0, bytes_accessed=0),
+    )(at, *parts)
+
+
+def other_results(at, parts, share, second_cols):
+    ring, rows, cols = parts[0].shape
+    chips = 4 * ring
+    late_rows = BLOCKS * 2 * share
+    pair_rows = (rows - late_rows) // 2
+    block = chips * share
+    half = 2 * block
+    query_cols, key_cols = second_cols
+
+    def kernel(at_ref, *refs):
+        part_refs, outs = refs[:8], refs[8:19]
+        query_s, pair_s, output_s, down_s = refs[19:]
+        (
+            in_q, second_q, in_k, second_k, in_v, second_v, in_o, second_o, in_g, in_u, second_d,
+        ) = outs
+        homes = (query_s, pair_s, output_s, in_o, None)
+        for i in range(8):
+            core = at_ref[0] if i < 4 else 1 - at_ref[0]
+            bit_y = at_ref[1] if i // 2 % 2 == 0 else 1 - at_ref[1]
+            bit_x = at_ref[2] if i % 2 == 0 else 1 - at_ref[2]
+
+            def one(r, _):
+                chip = lax.rem(at_ref[3] + ring - r, ring) * 4 + bit_y * 2 + bit_x
+                found = part_refs[i][r].astype(F32)
+                for b, (home, s) in enumerate(
+                    ((query_s, 0), (query_s, 1), (pair_s, 0), (output_s, 0), (output_s, 1), (in_o, 0), (in_o, 1))
+                ):
+                    size = block if home is pair_s else half
+                    to = pl.multiple_of(core * size + s * block + chip * share, 8)
+                    home[pl.ds(to, share), :] = found[2 * b * share : (2 * b + 1) * share]
+                for b in range(BLOCKS):
+                    home, s = (in_q, in_k, in_v, down_s)[b // 2], b % 2
+                    to = pl.multiple_of(core * half + s * block + chip * share, 8)
+                    home[pl.ds(to, share), :] = found[(2 * b + 1) * share : (2 * b + 2) * share]
+                for k, home in enumerate((in_g, in_u)):
+                    to = pl.multiple_of(core * half + chip * pair_rows, 8)
+                    start = late_rows + k * pair_rows
+                    home[pl.ds(to, pair_rows), :] = found[start : start + pair_rows]
+                return 0
+
+            lax.fori_loop(0, ring, one, 0)
+        second_q[...] = query_s[...].T
+        second_o[...] = output_s[...].T
+        second_d[...] = down_s[...].T
+        both = pair_s[...].T
+        for out, start in ((second_k, 0), (second_v, key_cols)):
+            out[...] = jnp.concatenate(
+                [both[:, c * block + start : c * block + start + key_cols] for c in range(2)], axis=1
+            )
+
+    width = 2 * half
+
+    def shape(*dims):
+        return jax.ShapeDtypeStruct(dims, F32)
+
+    return pl.pallas_call(
+        kernel,
+        out_shape=[
+            shape(width, cols), shape(cols, 2 * query_cols), shape(width, cols),
+            shape(cols, 2 * key_cols), shape(width, cols), shape(cols, 2 * key_cols),
+            shape(width, cols), shape(cols, width), shape(width, cols), shape(width, cols),
+            shape(cols, width),
+        ],
+        in_specs=[SMEM] + [VMEM] * 8,
+        out_specs=[VMEM] * 11,
+        scratch_shapes=[
+            pltpu.VMEM((width, cols), F32),
+            pltpu.VMEM((half, cols), F32),
+            pltpu.VMEM((width, cols), F32),
+            pltpu.VMEM((width, cols), F32),
+        ],
+        compiler_params=pltpu.CompilerParams(vmem_limit_bytes=48 * 2**20),
+        cost_estimate=pl.CostEstimate(flops=8_000_000_000, transcendentals=0, bytes_accessed=0),
+    )(at, *parts)
 
 
 DP = ("ring", "second", "first")
@@ -1023,13 +1215,6 @@
 
             return run
 
-        def sums_only(old):
-            def run():
-                v["totals"] = feed([], old, None, False)
-                return [v["totals"][0]]
-
-            return run
-
         order = sorted(range(chunks), key=lambda j: there(f"M{j}"))
         events = {}
 
@@ -1048,7 +1233,6 @@
             at = max([at] + [there(f"M{j}") for j in pair])
             at_step(at, units_only(pair))
             at += 1
-        at_step(max(at, last_step - 4), sums_only(early))
         for j in later:
             at_step(max(at, there(f"M{j}")), units_only([j]))
 
@@ -1078,15 +1262,11 @@
             for run in events.get(s, []):
                 waits += run()
 
-        totals = feed([final], later, v["totals"], True)
+        totals = feed([final], early + later, None, True)
         grad_keep, grad_send, out_keep, out_send = totals
 
         def after(values, *others):
             return tie(list(values), list(others), 0)
-
-        def exchange(value, axes, parts):
-            share = value.shape[0] // parts
-            return lax.all_to_all(value.reshape(parts, share, rank_cols), axes, 0, 0)
 
         def total(parts):
             return jnp.sum(parts.astype(F32), axis=0).astype(BF)
@@ -1097,7 +1277,7 @@
         out_send, *own = after([out_send] + [unit_out[j][2] for j in range(chunks)], grad_out)
         out_got = other_core(out_send)
         out_out = (out_keep[1].astype(F32) + out_got[1].astype(F32)).astype(BF)
-        got_units = exchange(jnp.concatenate(own, axis=0), DP[:2], n // 2)
+        units_all = lax.psum(jnp.concatenate(own, axis=0), DP[:2])
 
         grad_middle, grad_branch, grad_low_mlp = after_feed_forward(
             core_at, grad_in_parts, v["middle"], cotangent, select, mlp_gain_f, mlp_in
@@ -1108,67 +1288,46 @@
         delta_mlp = transpose_then_product(
             cols_of_core(v["normed"][:, :width]), grad_low_mlp
         ).astype(BF)
-        got_mlp = exchange(
-            jnp.concatenate([delta_mlp[:, :rank_cols], delta_mlp[:, rank_cols:]], axis=0), DP, n
-        )
-
-        back, back_low, seconds, first_output, second_output_blocks = attention_back(
+        got_mlp = lax.all_to_all(delta_mlp.reshape(n, half_width // n, 2 * rank_cols), DP, 0, 0)
+
+        back, back_low, factors = attention_back(
             core_at, (grad_branch, grad_branch_other), select, second_output, v["low_output"],
             v["attended"], in_output, v["a0"], v["a1"], v["query"], v["key"], v["value"], v["lse"],
             cos_table, sin_table, second_query, second_key, second_value, *lows,
         )
-        back_low, got_units, got_mlp, out_in = after([back_low, got_units, got_mlp, out_in])
+        back_low, out_in = after([back_low, out_in])
         back_low = back_low + other_core(back_low)
         grad_low_attn = (back_low * select_three).astype(BF)
-        delta_attn = transpose_then_product(cols_of_core(normed_a), grad_low_attn).astype(BF)
-
         out_sum = out_keep[0].astype(F32) + out_got[0].astype(F32) + out_in.astype(F32)
         low_down = (out_sum[:, width:] * half_of(select)).astype(BF)
-        second_down_part = (
-            adapter_scale * transpose_then_product(both_halves(low_down), cols_of_core(cotangent))
-        ).astype(BF)
-        late = jnp.concatenate(
-            [seconds]
-            + [delta_attn[:, i * rank_cols : (i + 1) * rank_cols] for i in range(3)]
-            + [second_down_part[:, at : at + rank_cols] for at in range(0, half_width, rank_cols)]
-            + [second_output_blocks, first_output],
-            axis=0,
-        )
-        got_late = exchange(late, DP, n)
-        got_units, got_mlp, back, out_sum, grad_middle = after(
-            [got_units, got_mlp, back, out_sum, grad_middle], late
-        )
-
-        def join_ring(value):
-            found = [value] + [move(value, f"z{r}") for r in range(1, ring_size)]
-            back = jnp.stack(found[::-1] + found[::-1], axis=0)
-            return take(back, ring_size - 1 - ring_at, ring_size)
-
-        def pair(bit, value, received):
-            return jnp.stack([jnp.where(bit == 0, value, received), jnp.where(bit == 0, received, value)])
-
-        def of_core_pair(value):
-            return pair(core, value, other_core(value))
-
-        units_all = join_ring(total(got_units))
-        units_all = jnp.swapaxes(pair(bit_y, units_all, move(units_all, "y")), 0, 1)
-        units_all = units_all.reshape(chunks, 3 * WIDTH, rank_cols)
-        units_all = of_core_pair(pair(bit_x, units_all, move(units_all, "x"))).astype(F32)
-
-        def unit_columns(start):
-            return jnp.concatenate(
-                [
-                    units_all[c, h, j, at : at + rank_cols]
-                    for c in range(2)
-                    for h in range(2)
-                    for j in range(chunks)
-                    for at in range(start, start + WIDTH, rank_cols)
-                ],
-                axis=1,
-            )
-
-        gradient_second_gate, gradient_second_up = unit_columns(0), unit_columns(WIDTH)
-        delta_in_down = units_all[:, :, :, 2 * WIDTH :].reshape(-1, rank_cols)
+        firsts = jnp.concatenate(
+            [
+                transpose_then_product(cols_of_core(normed_a), grad_low_attn).astype(BF),
+                (
+                    adapter_scale
+                    * transpose_then_product(cols_of_core(cotangent), both_halves(low_down))
+                ).astype(BF),
+            ],
+            axis=1,
+        )
+        *packed, chosen = pack(adapter_ids, factors, firsts)
+        share = packed[0].shape[0] // n
+        packed = jnp.concatenate(
+            [part.reshape(n, share, part.shape[1]) for part in packed]
+            + [jnp.broadcast_to(chosen[None], (n,) + chosen.shape)],
+            axis=1,
+        )
+        got_late = lax.all_to_all(packed, DP, 0, 0)
+        units_all, got_mlp, back, out_sum, grad_middle = after(
+            [units_all, got_mlp, back, out_sum, grad_middle], packed
+        )
+
+        pair = (units_all, move(units_all, "x"))
+        gradient_second_gate, gradient_second_up, delta_in_down = unit_results(
+            jnp.stack([core, bit_x]).astype(jnp.int32),
+            pair + tuple(other_core(part) for part in pair),
+            chunks,
+        )
 
         layer_output = both_halves(
             (
@@ -1185,60 +1344,29 @@
             (grad_middle + rms_back(half_of(hidden_wide), attn_gain_f, grad_normed_a)).astype(BF)
         )
 
-        sums = jnp.concatenate([total(got_mlp), total(got_late)], axis=0)
-        cut = got_mlp.shape[1]
-        sums = join_ring(sums)
-        by_x, by_y, by_both = (move(sums, link) for link in ("x", "y", "xy"))
-        sums = pair(bit_y, pair(bit_x, sums, by_x), pair(bit_x, by_y, by_both))
-        sums = of_core_pair(jnp.transpose(sums, (2, 0, 1, 3, 4)))
-
-        def parts_of(value, sizes):
-            value = value.reshape(2, -1, rank_cols)
-            at, parts = 0, []
-            for size in sizes:
-                parts.append(value[:, at : at + size].astype(F32))
-                at += size
-            return parts
-
-        query_cols, key_cols = second_query.shape[1], second_key.shape[1]
-        mlp_parts = parts_of(sums[..., :cut, :], [half_width] * 2)
-        late_parts = parts_of(sums[..., cut:, :], [seconds.shape[0]] + [half_width] * 6)
-
-        def rows(part):
-            return part.reshape(-1, rank_cols)
-
-        def columns(part):
-            return jnp.concatenate(
-                [part[c, at : at + rank_cols] for c in range(2) for at in range(0, part.shape[1], rank_cols)],
-                axis=1,
-            )
-
-        late_seconds = columns(late_parts[0])
-
-        def second_of(start, size):
-            per_core = late_seconds.shape[1] // 2
-            return jnp.concatenate(
-                [late_seconds[:, c * per_core + start : c * per_core + start + size] for c in range(2)],
-                axis=1,
-            )
-
+        sums_mlp = total(got_mlp)
+        sums = jnp.concatenate(
+            [unpack(got_late).reshape(-1, rank_cols), sums_mlp[:, :rank_cols], sums_mlp[:, rank_cols:]],
+            axis=0,
+        )
+        sums = jnp.stack([sums] + [move(sums, f"z{r}") for r in range(1, ring_size)], axis=0)
+        parts = [sums] + [move(sums, link) for link in ("x", "y", "xy")]
+        parts += [other_core(part) for part in parts]
+        others = other_results(
+            jnp.stack([core, bit_y, bit_x, ring_at]).astype(jnp.int32),
+            parts,
+            share,
+            (second_query.shape[1], second_key.shape[1]),
+        )
         return (
             layer_output,
             grad_in,
-            rows(late_parts[1]),
-            second_of(0, query_cols),
-            rows(late_parts[2]),
-            second_of(query_cols, key_cols),
-            rows(late_parts[3]),
-            second_of(query_cols + key_cols, key_cols),
-            rows(late_parts[6]),
-            columns(late_parts[5]),
-            rows(mlp_parts[0]),
+            *others[:9],
             gradient_second_gate,
-            rows(mlp_parts[1]),
+            others[9],
             gradient_second_up,
             delta_in_down,
-            columns(late_parts[4]),
+            others[10],
         )
 
     return body

time: 854 us -> 819 us (0.959)
  local copies, waits for them, and re-layouts: 99.9 us -> 75.2 us
  other arithmetic: 82.3 us -> 64.4 us
  between operations: 3.74 us -> 15.8 us
  starting transfers between devices: 117 us -> 107 us
    ppermute x86 -> x82, waiting for transfers between devices: 319 us -> 263 us  [move(): return lax.ppermute(value, DP, perms[link])]
    all_to_all x3 -> x2, waiting for transfers between devices: 0.01 us -> 24.8 us  [the longest x1 24.8 us: body(): got_late = lax.all_to_all(packed, DP, 0, 0)]
    psum x0 -> x1, waiting for transfers between devices: none -> 23.6 us  [body(): units_all = lax.psum(jnp.concatenate(own, axis=0), DP[:2])]
    pallas_call x0 -> x4, Pallas kernels: none -> 20.8 us  [the longest x1 7.71 us: other_results(): pl.pallas_call(kernel, out_shape=[shape(width, cols), shape(cols, 2 * que...]
    unnamed x354 -> x273, local copies, waits for them, and re-layouts: 69.8 us -> 52.4 us
    pallas_call x6 -> x5, Pallas kernels: 124 us -> 110 us  [feed_forward(): pl.pallas_call(kernel, out_shape=out_shape, in_specs=[SMEM] * 2 + [VMEM]...]
    all_to_all x3 -> x2, starting transfers between devices: 17.8 us -> 11.1 us  [the longest x1 7.02 us: body(): lax.all_to_all(delta_mlp.reshape(n, half_width // n, 2 * rank_cols), DP,...]
    ppermute x86 -> x82, starting transfers between devices: 97.5 us -> 92.4 us  [move(): return lax.ppermute(value, DP, perms[link])]
  transfers between devices with their start and end apart: 104 -> 104, of which waited for: 43 -> 44; matrix products, arithmetic and copies ran while one was open for 15% -> 14% of each run, Pallas kernels for 20% -> 19%
where the time goes in v2:
time: 819 us; the launch traced here: 809 us
  waiting for transfers between devices  318 us (39%)
  Pallas kernels  215 us (26%)
  starting transfers between devices  107 us (13%)
  local copies, waits for them, and re-layouts  75.2 us (9%)
  other arithmetic  64.4 us (8%)
  between operations  15.8 us (2%)
  matrix products  14.1 us (2%)
    ppermute x82, waiting for transfers between devices, move(): return lax.ppermute(value, DP, perms[link])  263 us
    pallas_call x5, Pallas kernels, feed_forward(): pl.pallas_call(kernel, out_shape=out_shape, in_specs=[SMEM] * 2 + [VMEM]...  110 us
    ppermute x82, starting transfers between devices, move(): return lax.ppermute(value, DP, perms[link])  92.4 us
    unnamed x273, local copies, waits for them, and re-layouts  52.4 us
    pallas_call x1, Pallas kernels, attention_back(): pl.pallas_call(kernel, out_shape=[jax.ShapeDtypeStruct((tokens, width), B...  36.6 us
    all_to_all x1, waiting for transfers between devices, body(): got_late = lax.all_to_all(packed, DP, 0, 0)  24.8 us
    psum x1, waiting for transfers between devices, body(): units_all = lax.psum(jnp.concatenate(own, axis=0), DP[:2])  23.6 us
    pallas_call x1, Pallas kernels, attention(): pl.pallas_call(kernel, out_shape=[jax.ShapeDtypeStruct((k_cols, tokens),...  20.4 us
  transfers between devices with their start and end apart: 104, of which 44 were waited for; matrix products, arithmetic and copies ran while one was open for 14% of the time, Pallas kernels for 19%

profile of v2, /device:TPU:0, one launch (start us, length us, event | category | flops | bytes accessed | tf_op | source)
XLA Modules:
  0.0 808.9 jit_solution(8750204551146046364)
XLA Ops:
  101.3 14.2 %collective-permute-done.12.refs_3_.refs_16_.refs_55_ = bf16[320,768]{1,0:T(8,128)(2,1)S(1)} collective-permute-done((bf16[320,768]{1,0:T(8,128)(2,1)S(1)}, bf16[320,768]{1,0:T(8,128)(2,1)S(1)}, u32[]{:S(2)}, u32[]{:S(2)}) %collective-permute-start.12) | collective-permute-done | bytes 491552 | tf_op jit(solution)/shard_map/ppermute | solution.py:1025
  125.4 13.9 %collective-permute-done.15.refs_1_ = bf16[160,1600]{1,0:T(8,128)(2,1)S(1)} collective-permute-done((bf16[160,1600]{1,0:T(8,128)(2,1)}, bf16[160,1600]{1,0:T(8,128)(2,1)S(1)}, u32[]{:S(2)}, u32[]{:S(2)}) %collective-permute-start.15) | collective-permute-done | bytes 512032 | tf_op jit(solution)/shard_map/ppermute | solution.py:1025
  143.4 13.8 %shard_map.373 = (bf16[1280,512]{1,0:T(8,128)(2,1)}, bf16[320,512]{1,0:T(8,128)(2,1)S(1)}, bf16[2560,1600]{1,0:T(8,128)(2,1)}) custom-call(s32[16]{0:T(128)S(1)} %stack.96.place_ref, bf16[512,2560]{1,0:T(8,128)(2,1)} %copy-done.51, bf16[512,128]{1,0:T(8,128)(2,1)S(1)} %get-tuple-element.324.lq_ref, bf16[512,128]{1,0:T(8,128)(2,1)S(1)} %get-tuple-element.323.lk_ref, ...), custom_call_target="tpu_custom_call" | custom-call | flops 4194304000 | bytes 16384000 | tf_op jit(solution)/shard_map/pallas_call | solution.py:220
  175.8 9.9 %collective-permute-done.20.refs_1_ = bf16[320,768]{1,0:T(8,128)(2,1)} collective-permute-done((bf16[320,768]{1,0:T(8,128)(2,1)}, bf16[320,768]{1,0:T(8,128)(2,1)}, u32[]{:S(2)}, u32[]{:S(2)}) %collective-permute-start.20) | collective-permute-done | bytes 491552 | tf_op jit(solution)/shard_map/ppermute | solution.py:1025
  226.8 10.9 %collective-permute-done.25.refs_7_.refs_3_ = bf16[320,1600]{1,0:T(8,128)(2,1)S(1)} collective-permute-done((bf16[320,1600]{1,0:T(8,128)(2,1)}, bf16[320,1600]{1,0:T(8,128)(2,1)S(1)}, u32[]{:S(2)}, u32[]{:S(2)}) %collective-permute-start.25) | collective-permute-done | bytes 1024032 | tf_op jit(solution)/shard_map/ppermute | solution.py:1025
  244.0 20.4 %shard_map.378 = (bf16[320,512]{1,0:T(8,128)(2,1)S(1)}, bf16[512,1280]{1,0:T(8,128)(2,1)}, f32[4,4,512]{2,1,0:T(4,128)S(1)}, bf16[512,2560]{1,0:T(8,128)(2,1)}, ...) custom-call(s32[16]{0:T(128)S(1)} %stack.96.place_ref, bf16[512,2560]{1,0:T(8,128)(2,1)} %copy-done.51, ...), custom_call_target="tpu_custom_call" | custom-call | flops 8388608000 | bytes 16384000 | tf_op jit(solution)/shard_map/pallas_call | solution.py:321
  286.8 8.9 %shard_map.379 = (f32[512,2560]{1,0:T(8,128)}, bf16[512,2816]{1,0:T(8,128)(2,1)S(1)}, bf16[512,128]{1,0:T(8,128)(2,1)S(1)}) custom-call(bf16[512,2560]{1,0:T(8,128)(2,1)S(1)} %copy-done.2, bf16[512,2560]{1,0:T(8,128)(2,1)} %get-tuple-element.150.b0, bf16[512,2560]{1,0:T(8,128)(2,1)} %collective-permute-done.26.b1, f32[512,128]{1,0:T(8,128)} %get-tuple-element.151.l0, ...), custom_call_target="tpu_custom_call" | custom-call | flops 1006632960 | bytes 18350080 | tf_op jit(solution)/shard_map/pallas_call | solution.py:528
  308.4 10.8 %collective-permute-done.57.refs_2_.refs_7_.refs_64_ = bf16[320,768]{1,0:T(8,128)(2,1)} collective-permute-done((bf16[320,768]{1,0:T(8,128)(2,1)}, bf16[320,768]{1,0:T(8,128)(2,1)}, u32[]{:S(2)}, u32[]{:S(2)}) %collective-permute-start.57) | collective-permute-done | bytes 491552 | tf_op jit(solution)/shard_map/ppermute | solution.py:1025
  353.0 18.0 %shard_map.391 = (bf16[1024,256]{1,0:T(8,128)(2,1)}, bf16[1024,256]{1,0:T(8,128)(2,1)}, bf16[1024,512]{1,0:T(8,128)(2,1)}, bf16[1024,512]{1,0:T(8,128)(2,1)}, bf...) custom-call(s32[16]{0:T(128)} %stack.109.place_ref, s32[1]{0:T(128)} %bitcast.32.core_ref, bf16[512,2816]{1,0:T(8,128)(2,1)} %copy-done.3, ...), custom_call_target="tpu_custom_call" | custom-call | flops 8053063680 | bytes 10485760 | tf_op jit(solution)/shard_map/pallas_call | solution.py:805
  371.6 18.0 %shard_map.394 = (bf16[1024,256]{1,0:T(8,128)(2,1)}, bf16[1024,256]{1,0:T(8,128)(2,1)}, bf16[1024,512]{1,0:T(8,128)(2,1)}, bf16[1024,512]{1,0:T(8,128)(2,1)}, bf...) custom-call(s32[16]{0:T(128)} %stack.109.place_ref, s32[1]{0:T(128)} %bitcast.32.core_ref, bf16[512,2816]{1,0:T(8,128)(2,1)} %copy-done.3, ...), custom_call_target="tpu_custom_call" | custom-call | flops 8053063680 | bytes 10485760 | tf_op jit(solution)/shard_map/pallas_call | solution.py:805
  396.6 11.3 %shard_map.398 = (bf16[1024,256]{1,0:T(8,128)(2,1)}, bf16[1024,512]{1,0:T(8,128)(2,1)}, bf16[768,128]{1,0:T(8,128)(2,1)}) custom-call(s32[16]{0:T(128)} %stack.109.place_ref, s32[1]{0:T(128)} %bitcast.32.core_ref, bf16[512,2816]{1,0:T(8,128)(2,1)} %copy-done.3, bf16[256,2816]{1,0:T(8,128)(2,1)} %collective-permute-done.48.refs_1_.refs_2_.refs_13_, ...), custom_call_target="tpu_custom_call" | custom-call | flops 4026531840 | bytes 10485760 | tf_op jit(solution)/shard_map/pallas_call | solution.py:805
  417.4 7.9 collective-permute-done.69.refs_11_.refs_1_.refs_77_
  427.0 8.8 %collective-permute-done.71.refs_13_.refs_1_.refs_79_ = bf16[320,768]{1,0:T(8,128)(2,1)} collective-permute-done((bf16[320,768]{1,0:T(8,128)(2,1)}, bf16[320,768]{1,0:T(8,128)(2,1)}, u32[]{:S(2)}, u32[]{:S(2)}) %collective-permute-start.71) | collective-permute-done | bytes 491552 | tf_op jit(solution)/shard_map/ppermute | solution.py:1025
  437.5 11.3 %shard_map.403 = (bf16[1024,256]{1,0:T(8,128)(2,1)}, bf16[1024,512]{1,0:T(8,128)(2,1)}, bf16[768,128]{1,0:T(8,128)(2,1)}) custom-call(s32[16]{0:T(128)} %stack.109.place_ref, s32[1]{0:T(128)} %bitcast.32.core_ref, bf16[512,2816]{1,0:T(8,128)(2,1)} %copy-done.3, bf16[256,2816]{1,0:T(8,128)(2,1)} %collective-permute-done.48.refs_1_.refs_2_.refs_13_, ...), custom_call_target="tpu_custom_call" | custom-call | flops 4026531840 | bytes 10485760 | tf_op jit(solution)/shard_map/pallas_call | solution.py:805
  449.2 7.7 collective-permute-done.74.refs_1_.refs_21_
  458.6 8.8 %collective-permute-done.75.refs_23_ = bf16[320,768]{1,0:T(8,128)(2,1)} collective-permute-done((bf16[320,768]{1,0:T(8,128)(2,1)}, bf16[320,768]{1,0:T(8,128)(2,1)}, u32[]{:S(2)}, u32[]{:S(2)}) %collective-permute-start.75) | collective-permute-done | bytes 491552 | tf_op jit(solution)/shard_map/ppermute | solution.py:1025
  475.4 51.2 %shard_map.408 = (bf16[2,256,2816]{2,1,0:T(8,128)(2,1)}, bf16[2,256,2816]{2,1,0:T(8,128)(2,1)}, bf16[2,256,2688]{2,1,0:T(8,128)(2,1)}, bf16[2,256,2688]{2,1,0:T(...) custom-call(s32[16]{0:T(128)} %stack.109.place_ref, ...), custom_call_target="tpu_custom_call" | custom-call | flops 32212254720 | bytes 10485760 | tf_op jit(solution)/shard_map/pallas_call | solution.py:805
  543.4 30.3 %collective-permute-done.78.p2 = bf16[256,2816]{1,0:T(8,128)(2,1)S(1)} collective-permute-done((bf16[256,2816]{1,0:T(8,128)(2,1)S(1)}, bf16[256,2816]{1,0:T(8,128)(2,1)S(1)}, u32[]{:S(2)}, u32[]{:S(2)}) %collective-permute-start.78) | collective-permute-done | bytes 1441824 | tf_op jit(solution)/shard_map/ppermute | solution.py:1025
  588.7 36.6 %shard_map.411 = (bf16[512,2560]{1,0:T(8,128)(2,1)}, f32[512,384]{1,0:T(8,128)}, bf16[5120,128]{1,0:T(8,128)(2,1)}) custom-call(s32[1]{0:T(128)} %bitcast.32.core_ref, bf16[256,2560]{1,0:T(8,128)(2,1)} %get-tuple-element.213.mine_hbm.refs_1_, bf16[256,2560]{1,0:T(8,128)(2,1)} %collective-permute-done.80.other_hbm, f32[512,128]{1,0:T(8,128)} %copy-done.10, ...), custom_call_target="tpu_custom_call" | custom-call | flops 41943040000 | bytes 16384000 | tf_op jit(solution)/shard_map/pallas_call | solution.py:473
  648.5 23.6 %all-reduce.2.cloned.1.call-done.refs_0_ = bf16[5376,128]{1,0:T(8,128)(2,1)} async-done(((bf16[5376,128]{1,0:T(8,128)(2,1)}), bf16[5376,128]{1,0:T(8,128)(2,1)}) %all-reduce.2.cloned.1.call-update) | async-done | bytes 1376272 | tf_op jit(solution)/shard_map/psum | solution.py:1280
  698.3 24.8 %all-to-all-done.1.got_ref = bf16[16,96,384]{2,1,0:T(8,128)(2,1)S(1)} async-done(((bf16[16,96,384]{2,1,0:T(8,128)(2,1)}), bf16[16,96,384]{2,1,0:T(8,128)(2,1)S(1)}, u32[]{:S(2)}, u32[]{:S(2)}) %all-to-all-start.1) | async-done | bytes 1179680 | tf_op jit(solution)/shard_map/all_to_all | solution.py:1320
  751.3 15.6 %collective-permute-done.91.refs_1_ = bf16[4,800,128]{2,1,0:T(8,128)(2,1)S(1)} collective-permute-done((bf16[4,800,128]{2,1,0:T(8,128)(2,1)S(1)}, bf16[4,800,128]{2,1,0:T(8,128)(2,1)S(1)}, u32[]{:S(2)}, u32[]{:S(2)}) %collective-permute-start.91) | collective-permute-done | bytes 819232 | tf_op jit(solution)/shard_map/ppermute | solution.py:1025
  766.9 16.8 %collective-permute-done.92.refs_2_ = bf16[4,800,128]{2,1,0:T(8,128)(2,1)S(1)} collective-permute-done((bf16[4,800,128]{2,1,0:T(8,128)(2,1)S(1)}, bf16[4,800,128]{2,1,0:T(8,128)(2,1)S(1)}, u32[]{:S(2)}, u32[]{:S(2)}) %collective-permute-start.92) | collective-permute-done | bytes 819232 | tf_op jit(solution)/shard_map/ppermute | solution.py:1025
  793.9 7.7 shard_map.417
  (591 shorter events, 391.8 us)
Async XLA Ops:
  7.2 664.8 %all-reduce.2.cloned.1.call-start = ((), (), s32[]{:S(2)}) async-start(), calls=%async_computation.2 | async-start | bytes 2752512 | tf_op jit(solution)/shard_map/psum | solution.py:1280
  12.3 81.5 %collective-permute-start.14 = (bf16[160,1600]{1,0:T(8,128)(2,1)}, bf16[160,1600]{1,0:T(8,128)(2,1)}, u32[]{:S(2)}, u32[]{:S(2)}) collective-permute-start(bf16[160,1600]{1,0:T(8,128)(2,1)} %pad_maximum_fusion.33), channel_id=1, source_target_pairs={{0,4},{2,6},{4,0},{6,2},{8,12},{10,14},{12,8},{14,10},{16,20},{18,... | collective-permute-start | bytes 1536008 | tf_op jit(solution)/shard_map/ppermute | solution.py:1025
  21.7 56.1 %collective-permute-start.8 = (bf16[160,1536]{1,0:T(8,128)(2,1)}, bf16[160,1536]{1,0:T(8,128)(2,1)}, u32[]{:S(2)}, u32[]{:S(2)}) collective-permute-start(bf16[160,1536]{1,0:T(8,128)(2,1)} %get-tuple-element.314), channel_id=1, source_target_pairs={{0,2},{2,0},{4,6},{6,4},{8,10},{10,8},{12,14},{14,12},{16,18},{18,... | collective-permute-start | bytes 1474568 | tf_op jit(solution)/shard_map/ppermute | solution.py:1025
  93.9 64.1 %collective-permute-start.28 = (bf16[320,768]{1,0:T(8,128)(2,1)}, bf16[320,768]{1,0:T(8,128)(2,1)}, u32[]{:S(2)}, u32[]{:S(2)}) collective-permute-start(bf16[320,768]{1,0:T(8,128)(2,1)} %shard_map.380.refs_6_.refs_27_), channel_id=1, source_target_pairs={{0,8},{2,10},{4,12},{6,14},{8,16},{10,18},{12,20},{14,22},{16,24},... | collective-permute-start | bytes 1474568 | tf_op jit(solution)/shard_map/ppermute | solution.py:1025
  124.4 65.1 %collective-permute-start.51 = (bf16[320,768]{1,0:T(8,128)(2,1)}, bf16[320,768]{1,0:T(8,128)(2,1)}, u32[]{:S(2)}, u32[]{:S(2)}) collective-permute-start(bf16[320,768]{1,0:T(8,128)(2,1)} %shard_map.383.refs_1_), channel_id=1, source_target_pairs={{0,4},{2,6},{4,0},{6,2},{8,12},{10,14},{12,8},{14,10},{16,20},{18,... | collective-permute-start | bytes 1474568 | tf_op jit(solution)/shard_map/ppermute | solution.py:1025
  217.5 47.6 %collective-permute-start.36 = (bf16[320,768]{1,0:T(8,128)(2,1)}, bf16[320,768]{1,0:T(8,128)(2,1)}, u32[]{:S(2)}, u32[]{:S(2)}) collective-permute-start(bf16[320,768]{1,0:T(8,128)(2,1)} %shard_map.385.refs_8_.refs_47_), channel_id=1, source_target_pairs={{0,8},{2,10},{4,12},{6,14},{8,16},{10,18},{12,20},{14,22},{16,24},... | collective-permute-start | bytes 1474568 | tf_op jit(solution)/shard_map/ppermute | solution.py:1025
  218.3 46.8 %collective-permute-start.37 = (bf16[320,768]{1,0:T(8,128)(2,1)}, bf16[320,768]{1,0:T(8,128)(2,1)}, u32[]{:S(2)}, u32[]{:S(2)}) collective-permute-start(bf16[320,768]{1,0:T(8,128)(2,1)} %shard_map.385.refs_8_.refs_47_), channel_id=1, source_target_pairs={{0,4},{2,6},{4,0},{6,2},{8,12},{10,14},{12,8},{14,10},{16,20},{18,... | collective-permute-start | bytes 1474568 | tf_op jit(solution)/shard_map/ppermute | solution.py:1025
  238.7 33.5 %collective-permute-start.41 = (bf16[160,2304]{1,0:T(8,128)(2,1)}, bf16[160,2304]{1,0:T(8,128)(2,1)}, u32[]{:S(2)}, u32[]{:S(2)}) collective-permute-start(bf16[160,2304]{1,0:T(8,128)(2,1)} %get-tuple-element.158), channel_id=1, source_target_pairs={{0,2},{2,0},{4,6},{6,4},{8,10},{10,8},{12,14},{14,12},{16,18},{18,... | collective-permute-start | bytes 2211848 | tf_op jit(solution)/shard_map/ppermute | solution.py:1025
  272.2 32.5 %collective-permute-start.46 = (bf16[256,2688]{1,0:T(8,128)(2,1)}, bf16[256,2688]{1,0:T(8,128)(2,1)}, u32[]{:S(2)}, u32[]{:S(2)}) collective-permute-start(bf16[256,2688]{1,0:T(8,128)(2,1)} %get-tuple-element.162), channel_id=1, source_target_pairs={{0,2},{2,0},{4,6},{6,4},{8,10},{10,8},{12,14},{14,12},{16,18},{18,... | collective-permute-start | bytes 4128776 | tf_op jit(solution)/shard_map/ppermute | solution.py:1025
  307.4 36.6 %collective-permute-start.48 = (bf16[256,2816]{1,0:T(8,128)(2,1)}, bf16[256,2816]{1,0:T(8,128)(2,1)}, u32[]{:S(2)}, u32[]{:S(2)}) collective-permute-start(bf16[256,2816]{1,0:T(8,128)(2,1)} %get-tuple-element.164), channel_id=1, source_target_pairs={{0,2},{2,0},{4,6},{6,4},{8,10},{10,8},{12,14},{14,12},{16,18},{18,... | collective-permute-start | bytes 4325384 | tf_op jit(solution)/shard_map/ppermute | solution.py:1025
  350.8 38.8 %collective-permute-start.61 = (bf16[320,768]{1,0:T(8,128)(2,1)}, bf16[320,768]{1,0:T(8,128)(2,1)}, u32[]{:S(2)}, u32[]{:S(2)}) collective-permute-start(bf16[320,768]{1,0:T(8,128)(2,1)} %get-tuple-element.181.refs_10_.refs_67_), channel_id=1, source_target_pairs={{0,4},{2,6},{4,0},{6,2},{8,12},{10,14},{12,8},{14,10},{16,20},{18,... | collective-permute-start | bytes 1474568 | tf_op jit(solution)/shard_map/ppermute | solution.py:1025
  352.6 37.1 %collective-permute-start.64 = (bf16[320,768]{1,0:T(8,128)(2,1)}, bf16[320,768]{1,0:T(8,128)(2,1)}, u32[]{:S(2)}, u32[]{:S(2)}) collective-permute-start(bf16[320,768]{1,0:T(8,128)(2,1)} %get-tuple-element.185.refs_0_), channel_id=1, source_target_pairs={{0,8},{2,10},{4,12},{6,14},{8,16},{10,18},{12,20},{14,22},{16,24},... | collective-permute-start | bytes 1474568 | tf_op jit(solution)/shard_map/ppermute | solution.py:1025
  536.1 49.0 %collective-permute-start.81 = (bf16[2,256,2688]{2,1,0:T(8,128)(2,1)}, bf16[2,256,2688]{2,1,0:T(8,128)(2,1)}, u32[]{:S(2)}, u32[]{:S(2)}) collective-permute-start(bf16[2,256,2688]{2,1,0:T(8,128)(2,1)} %get-tuple-element.220), channel_id=1, source_target_pairs={{0,1},{1,0},{2,3},{3,2},{4,5},{5,4},{6,7},{7,6},{8,9},{9,8},{10,11... | collective-permute-start | bytes 8257544 | tf_op jit(solution)/shard_map/ppermute | solution.py:1028
  539.8 33.9 %collective-permute-start.78 = (bf16[256,2816]{1,0:T(8,128)(2,1)S(1)}, bf16[256,2816]{1,0:T(8,128)(2,1)S(1)}, u32[]{:S(2)}, u32[]{:S(2)}) collective-permute-start(bf16[256,2816]{1,0:T(8,128)(2,1)S(1)} %copy-done.41), channel_id=1, source_target_pairs={{0,2},{2,0},{4,6},{6,4},{8,10},{10,8},{12,14},{14,12},{16,18},{18,... | collective-permute-start | bytes 4325384 | tf_op jit(solution)/shard_map/ppermute | solution.py:1025
  588.2 37.1 %collective-permute-start.82 = (bf16[256,2688]{1,0:T(8,128)(2,1)}, bf16[256,2688]{1,0:T(8,128)(2,1)}, u32[]{:S(2)}, u32[]{:S(2)}) collective-permute-start(bf16[256,2688]{1,0:T(8,128)(2,1)} %shard_map.412), channel_id=1, source_target_pairs={{0,2},{2,0},{4,6},{6,4},{8,10},{10,8},{12,14},{14,12},{16,18},{18,... | collective-permute-start | bytes 4128776 | tf_op jit(solution)/shard_map/ppermute | solution.py:1025
  632.2 39.8 %all-to-all-start = ((bf16[16,80,256]{2,1,0:T(8,128)(2,1)}), bf16[16,80,256]{2,1,0:T(8,128)(2,1)}, u32[]{:S(2)}, u32[]{:S(2)}) async-start(bf16[16,80,256]{2,1,0:T(8,128)(2,1)} %bitcast.78), calls=%async_computation | async-start | bytes 1310720 | tf_op jit(solution)/shard_map/all_to_all | solution.py:1291
  677.7 52.2 %collective-permute-start.98 = (bf16[5376,128]{1,0:T(8,128)(2,1)}, bf16[5376,128]{1,0:T(8,128)(2,1)S(1)}, u32[]{:S(2)}, u32[]{:S(2)}) collective-permute-start(bf16[5376,128]{1,0:T(8,128)(2,1)} %get-tuple-element.242.refs_0_), channel_id=1, source_target_pairs={{0,2},{2,0},{4,6},{6,4},{8,10},{10,8},{12,14},{14,12},{16,18},{18,... | collective-permute-start | bytes 4128776 | tf_op jit(solution)/shard_map/ppermute | solution.py:1025
  679.2 72.0 %collective-permute-start.99 = (bf16[5376,128]{1,0:T(8,128)(2,1)}, bf16[5376,128]{1,0:T(8,128)(2,1)}, u32[]{:S(2)}, u32[]{:S(2)}) collective-permute-start(bf16[5376,128]{1,0:T(8,128)(2,1)} %get-tuple-element.242.refs_0_), channel_id=1, source_target_pairs={{0,1},{1,0},{2,3},{3,2},{4,5},{5,4},{6,7},{7,6},{8,9},{9,8},{10,11... | collective-permute-start | bytes 4128776 | tf_op jit(solution)/shard_map/ppermute | solution.py:1028
  679.4 43.8 %all-to-all-start.1 = ((bf16[16,96,384]{2,1,0:T(8,128)(2,1)}), bf16[16,96,384]{2,1,0:T(8,128)(2,1)S(1)}, u32[]{:S(2)}, u32[]{:S(2)}) async-start(bf16[16,96,384]{2,1,0:T(8,128)(2,1)} %pad_maximum_fusion.25.refs_5_), calls=%async_computation.1 | async-start | bytes 2359296 | tf_op jit(solution)/shard_map/all_to_all | solution.py:1320
  696.4 51.9 %collective-permute-start.87 = (bf16[256,2560]{1,0:T(8,128)(2,1)}, bf16[256,2560]{1,0:T(8,128)(2,1)}, u32[]{:S(2)}, u32[]{:S(2)}) collective-permute-start(bf16[256,2560]{1,0:T(8,128)(2,1)} %add_convert_fusion.2), channel_id=1, source_target_pairs={{0,1},{1,0},{2,3},{3,2},{4,5},{5,4},{6,7},{7,6},{8,9},{9,8},{10,11... | collective-permute-start | bytes 3932168 | tf_op jit(solution)/shard_map/ppermute | solution.py:1028
  737.7 48.2 %collective-permute-start.100 = (bf16[5376,128]{1,0:T(8,128)(2,1)S(1)}, bf16[5376,128]{1,0:T(8,128)(2,1)S(1)}, u32[]{:S(2)}, u32[]{:S(2)}) collective-permute-start(bf16[5376,128]{1,0:T(8,128)(2,1)S(1)} %collective-permute-done.98.refs_1_), channel_id=1, source_target_pairs={{0,1},{1,0},{2,3},{3,2},{4,5},{5,4},{6,7},{7,6},{8,9},{9,8},{10,11... | collective-permute-start | bytes 4128776 | tf_op jit(solution)/shard_map/ppermute | solution.py:1028
  747.7 36.0 %collective-permute-start.92 = (bf16[4,800,128]{2,1,0:T(8,128)(2,1)S(1)}, bf16[4,800,128]{2,1,0:T(8,128)(2,1)S(1)}, u32[]{:S(2)}, u32[]{:S(2)}) collective-permute-start(bf16[4,800,128]{2,1,0:T(8,128)(2,1)S(1)} %pad_maximum_fusion.31.refs_0_), channel_id=1, source_target_pairs={{0,4},{2,6},{4,0},{6,2},{8,12},{10,14},{12,8},{14,10},{16,20},{18,... | collective-permute-start | bytes 2457608 | tf_op jit(solution)/shard_map/ppermute | solution.py:1025
  748.4 35.4 %collective-permute-start.93 = (bf16[4,800,128]{2,1,0:T(8,128)(2,1)S(1)}, bf16[4,800,128]{2,1,0:T(8,128)(2,1)S(1)}, u32[]{:S(2)}, u32[]{:S(2)}) collective-permute-start(bf16[4,800,128]{2,1,0:T(8,128)(2,1)S(1)} %pad_maximum_fusion.31.refs_0_), channel_id=1, source_target_pairs={{0,6},{2,4},{4,2},{6,0},{8,14},{10,12},{12,10},{14,8},{16,22},{18,... | collective-permute-start | bytes 2457608 | tf_op jit(solution)/shard_map/ppermute | solution.py:1025
  751.2 41.8 %collective-permute-start.94 = (bf16[4,800,128]{2,1,0:T(8,128)(2,1)S(1)}, bf16[4,800,128]{2,1,0:T(8,128)(2,1)S(1)}, u32[]{:S(2)}, u32[]{:S(2)}) collective-permute-start(bf16[4,800,128]{2,1,0:T(8,128)(2,1)S(1)} %pad_maximum_fusion.31.refs_0_), channel_id=1, source_target_pairs={{0,1},{1,0},{2,3},{3,2},{4,5},{5,4},{6,7},{7,6},{8,9},{9,8},{10,11... | collective-permute-start | bytes 2457608 | tf_op jit(solution)/shard_map/ppermute | solution.py:1028
  (204 other events, 2197.8 us)
Sparse Core Ops, SparseCore 0:
  582.7 89.2 all-reduce.1

commit v3 on v2

--- a/solution.py
+++ b/solution.py
@@ -904,35 +904,45 @@
 
 
 def unit_results(at, parts, chunks):
-    rows = parts[0].shape[0]
+    ring, share, cols = parts[0].shape
     units = chunks * WIDTH
 
     def kernel(at_ref, *refs):
-        gate_out, up_out, down_out = refs[4:]
-        for i in range(4):
-            core = at_ref[0] if i < 2 else 1 - at_ref[0]
-            bit = at_ref[1] if i % 2 == 0 else 1 - at_ref[1]
-            start = pl.multiple_of((core * 2 + bit) * units, 128)
+        gate_out, up_out, down_out, all_s = refs[8:]
+        for i in range(8):
+            core = at_ref[0] if i < 4 else 1 - at_ref[0]
+            bit_y = at_ref[1] if i // 2 % 2 == 0 else 1 - at_ref[1]
+            bit_x = at_ref[2] if i % 2 == 0 else 1 - at_ref[2]
+
+            def one(r, _):
+                place = lax.rem(at_ref[3] + ring - r, ring) * 2 + bit_y
+                to = pl.multiple_of(place * share, 8)
+                all_s[core * 2 + bit_x, pl.ds(to, share), :] = refs[i][r].astype(F32)
+                return 0
+
+            lax.fori_loop(0, ring, one, 0)
+        for q in range(4):
             for j in range(chunks):
-                for at in range(0, WIDTH, ADAPTER_COLS):
-                    to = pl.ds(pl.multiple_of(start + j * WIDTH + at, 128), ADAPTER_COLS)
-                    row = j * 3 * WIDTH + at
-                    gate_out[:, to] = refs[i][row : row + ADAPTER_COLS, :].astype(F32)
-                    row += WIDTH
-                    up_out[:, to] = refs[i][row : row + ADAPTER_COLS, :].astype(F32)
-                row = (j * 3 + 2) * WIDTH
-                to = pl.ds(pl.multiple_of(start + j * WIDTH, 128), WIDTH)
-                down_out[to, :] = refs[i][row : row + WIDTH, :].astype(F32)
+                start = q * units + j * WIDTH
+                row = j * 3 * WIDTH
+                for at in range(0, WIDTH, cols):
+                    to = slice(start + at, start + at + cols)
+                    gate_out[:, to] = all_s[q, row + at : row + at + cols, :]
+                    at += WIDTH
+                    up_out[:, to] = all_s[q, row + at : row + at + cols, :]
+                row += 2 * WIDTH
+                down_out[start : start + WIDTH, :] = all_s[q, row : row + WIDTH, :]
 
     return pl.pallas_call(
         kernel,
         out_shape=[
-            jax.ShapeDtypeStruct((ADAPTER_COLS, 4 * units), F32),
-            jax.ShapeDtypeStruct((ADAPTER_COLS, 4 * units), F32),
-            jax.ShapeDtypeStruct((4 * units, ADAPTER_COLS), F32),
+            jax.ShapeDtypeStruct((cols, 4 * units), F32),
+            jax.ShapeDtypeStruct((cols, 4 * units), F32),
+            jax.ShapeDtypeStruct((4 * units, cols), F32),
         ],
-        in_specs=[SMEM] + [VMEM] * 4,
+        in_specs=[SMEM] + [VMEM] * 8,
         out_specs=[VMEM] * 3,
+        scratch_shapes=[pltpu.VMEM((4, 3 * units, cols), F32)],
         compiler_params=pltpu.CompilerParams(vmem_limit_bytes=48 * 2**20),
         cost_estimate=pl.CostEstimate(flops=8_000_000_000, transcendentals=0, bytes_accessed=0),
     )(at, *parts)
@@ -1277,7 +1287,8 @@
         out_send, *own = after([out_send] + [unit_out[j][2] for j in range(chunks)], grad_out)
         out_got = other_core(out_send)
         out_out = (out_keep[1].astype(F32) + out_got[1].astype(F32)).astype(BF)
-        units_all = lax.psum(jnp.concatenate(own, axis=0), DP[:2])
+        own = jnp.concatenate(own, axis=0)
+        got_units = lax.all_to_all(own.reshape(n // 2, -1, rank_cols), DP[:2], 0, 0)
 
         grad_middle, grad_branch, grad_low_mlp = after_feed_forward(
             core_at, grad_in_parts, v["middle"], cotangent, select, mlp_gain_f, mlp_in
@@ -1295,7 +1306,7 @@
             v["attended"], in_output, v["a0"], v["a1"], v["query"], v["key"], v["value"], v["lse"],
             cos_table, sin_table, second_query, second_key, second_value, *lows,
         )
-        back_low, out_in = after([back_low, out_in])
+        back_low, out_in, got_mlp, got_units = after([back_low, out_in, got_mlp, got_units])
         back_low = back_low + other_core(back_low)
         grad_low_attn = (back_low * select_three).astype(BF)
         out_sum = out_keep[0].astype(F32) + out_got[0].astype(F32) + out_in.astype(F32)
@@ -1317,16 +1328,17 @@
             + [jnp.broadcast_to(chosen[None], (n,) + chosen.shape)],
             axis=1,
         )
+        units_sum = total(got_units)
+        units_sum = jnp.stack([units_sum] + [move(units_sum, f"z{r}") for r in range(1, ring_size)])
+        packed, units_sum = after([packed, units_sum])
         got_late = lax.all_to_all(packed, DP, 0, 0)
-        units_all, got_mlp, back, out_sum, grad_middle = after(
-            [units_all, got_mlp, back, out_sum, grad_middle], packed
-        )
-
-        pair = (units_all, move(units_all, "x"))
+        got_mlp, back, out_sum, grad_middle = after([got_mlp, back, out_sum, grad_middle], packed)
+        units_parts = [units_sum] + [move(units_sum, link) for link in ("x", "y", "xy")]
+        got_late, *units_parts[1:] = after([got_late] + units_parts[1:])
+
+        device = jnp.stack([core, bit_y, bit_x, ring_at]).astype(jnp.int32)
         gradient_second_gate, gradient_second_up, delta_in_down = unit_results(
-            jnp.stack([core, bit_x]).astype(jnp.int32),
-            pair + tuple(other_core(part) for part in pair),
-            chunks,
+            device, units_parts + [other_core(part) for part in units_parts], chunks
         )
 
         layer_output = both_halves(
@@ -1353,7 +1365,7 @@
         parts = [sums] + [move(sums, link) for link in ("x", "y", "xy")]
         parts += [other_core(part) for part in parts]
         others = other_results(
-            jnp.stack([core, bit_y, bit_x, ring_at]).astype(jnp.int32),
+            device,
             parts,
             share,
             (second_query.shape[1], second_key.shape[1]),

time: 819 us -> 803 us (0.980)
  waiting for transfers between devices: 318 us -> 286 us
  starting transfers between devices: 107 us -> 129 us
  between operations: 15.8 us -> 2.24 us
    psum x1 -> x0, waiting for transfers between devices: 23.6 us -> none  [body(): units_all = lax.psum(jnp.concatenate(own, axis=0), DP[:2])]
    all_to_all x1, waiting for transfers between devices: 24.8 us -> 1.46 us  [body(): got_late = lax.all_to_all(packed, DP, 0, 0)]
    ppermute x82 -> x87, waiting for transfers between devices: 263 us -> 278 us  [move(): return lax.ppermute(value, DP, perms[link])]
    ppermute x82 -> x87, starting transfers between devices: 92.4 us -> 104 us  [move(): return lax.ppermute(value, DP, perms[link])]
    unnamed x273 -> x265, local copies, waits for them, and re-layouts: 52.4 us -> 55.5 us
  transfers between devices with their start and end apart: 104 -> 111, of which waited for: 44 -> 48; matrix products, arithmetic and copies ran while one was open for 14% -> 15% of each run, Pallas kernels for 19% -> 20%
where the time goes in v3:
time: 803 us; the launch traced here: 794 us
  waiting for transfers between devices  286 us (36%)
  Pallas kernels  217 us (27%)
  starting transfers between devices  129 us (16%)
  local copies, waits for them, and re-layouts  78.9 us (10%)
  other arithmetic  66.5 us (8%)
  matrix products  14.9 us (2%)
    ppermute x87, waiting for transfers between devices, move(): return lax.ppermute(value, DP, perms[link])  278 us
    pallas_call x5, Pallas kernels, feed_forward(): pl.pallas_call(kernel, out_shape=out_shape, in_specs=[SMEM] * 2 + [VMEM]...  110 us
    ppermute x87, starting transfers between devices, move(): return lax.ppermute(value, DP, perms[link])  104 us
    unnamed x265, local copies, waits for them, and re-layouts  55.5 us
    pallas_call x1, Pallas kernels, attention_back(): pl.pallas_call(kernel, out_shape=[jax.ShapeDtypeStruct((tokens, width), B...  36.6 us
    pallas_call x1, Pallas kernels, attention(): pl.pallas_call(kernel, out_shape=[jax.ShapeDtypeStruct((k_cols, tokens),...  20.4 us
  transfers between devices with their start and end apart: 111, of which 48 were waited for; matrix products, arithmetic and copies ran while one was open for 15% of the time, Pallas kernels for 20%

profile of v3, /device:TPU:0, one launch (start us, length us, event | category | flops | bytes accessed | tf_op | source)
XLA Modules:
  0.0 794.3 jit_solution(11745864674370613582)
XLA Ops:
  94.7 14.2 %collective-permute-done.12.refs_3_.refs_16_.refs_55_ = bf16[320,768]{1,0:T(8,128)(2,1)S(1)} collective-permute-done((bf16[320,768]{1,0:T(8,128)(2,1)S(1)}, bf16[320,768]{1,0:T(8,128)(2,1)S(1)}, u32[]{:S(2)}, u32[]{:S(2)}) %collective-permute-start.12) | collective-permute-done | bytes 491552 | tf_op jit(solution)/shard_map/ppermute | solution.py:1035
  118.8 13.9 %collective-permute-done.15.refs_1_ = bf16[160,1600]{1,0:T(8,128)(2,1)S(1)} collective-permute-done((bf16[160,1600]{1,0:T(8,128)(2,1)}, bf16[160,1600]{1,0:T(8,128)(2,1)S(1)}, u32[]{:S(2)}, u32[]{:S(2)}) %collective-permute-start.15) | collective-permute-done | bytes 512032 | tf_op jit(solution)/shard_map/ppermute | solution.py:1035
  136.8 13.8 %shard_map.373 = (bf16[1280,512]{1,0:T(8,128)(2,1)}, bf16[320,512]{1,0:T(8,128)(2,1)S(1)}, bf16[2560,1600]{1,0:T(8,128)(2,1)}) custom-call(s32[16]{0:T(128)S(1)} %stack.104.place_ref, bf16[512,2560]{1,0:T(8,128)(2,1)} %copy-done.52, bf16[512,128]{1,0:T(8,128)(2,1)S(1)} %get-tuple-element.338.lq_ref, bf16[512,128]{1,0:T(8,128)(2,1)S(1)} %get-tuple-element.337.lk_ref, ...), custom_call_target="tpu_custom_call" | custom-call | flops 4194304000 | bytes 16384000 | tf_op jit(solution)/shard_map/pallas_call | solution.py:220
  169.2 9.9 %collective-permute-done.20.refs_1_ = bf16[320,768]{1,0:T(8,128)(2,1)} collective-permute-done((bf16[320,768]{1,0:T(8,128)(2,1)}, bf16[320,768]{1,0:T(8,128)(2,1)}, u32[]{:S(2)}, u32[]{:S(2)}) %collective-permute-start.20) | collective-permute-done | bytes 491552 | tf_op jit(solution)/shard_map/ppermute | solution.py:1035
  220.1 10.9 %collective-permute-done.25.refs_7_.refs_3_ = bf16[320,1600]{1,0:T(8,128)(2,1)S(1)} collective-permute-done((bf16[320,1600]{1,0:T(8,128)(2,1)}, bf16[320,1600]{1,0:T(8,128)(2,1)S(1)}, u32[]{:S(2)}, u32[]{:S(2)}) %collective-permute-start.25) | collective-permute-done | bytes 1024032 | tf_op jit(solution)/shard_map/ppermute | solution.py:1035
  237.3 20.4 %shard_map.378 = (bf16[320,512]{1,0:T(8,128)(2,1)S(1)}, bf16[512,1280]{1,0:T(8,128)(2,1)}, f32[4,4,512]{2,1,0:T(4,128)S(1)}, bf16[512,2560]{1,0:T(8,128)(2,1)}, ...) custom-call(s32[16]{0:T(128)S(1)} %stack.104.place_ref, bf16[512,2560]{1,0:T(8,128)(2,1)} %copy-done.52, ...), custom_call_target="tpu_custom_call" | custom-call | flops 8388608000 | bytes 16384000 | tf_op jit(solution)/shard_map/pallas_call | solution.py:321
  280.1 8.8 %shard_map.379 = (f32[512,2560]{1,0:T(8,128)}, bf16[512,2816]{1,0:T(8,128)(2,1)S(1)}, bf16[512,128]{1,0:T(8,128)(2,1)S(1)}) custom-call(bf16[512,2560]{1,0:T(8,128)(2,1)S(1)} %copy-done.2, bf16[512,2560]{1,0:T(8,128)(2,1)} %get-tuple-element.157.b0, bf16[512,2560]{1,0:T(8,128)(2,1)} %collective-permute-done.26.b1, f32[512,128]{1,0:T(8,128)} %get-tuple-element.158.l0, ...), custom_call_target="tpu_custom_call" | custom-call | flops 1006632960 | bytes 18350080 | tf_op jit(solution)/shard_map/pallas_call | solution.py:528
  301.7 10.8 %collective-permute-done.57.refs_2_.refs_7_.refs_64_ = bf16[320,768]{1,0:T(8,128)(2,1)} collective-permute-done((bf16[320,768]{1,0:T(8,128)(2,1)}, bf16[320,768]{1,0:T(8,128)(2,1)}, u32[]{:S(2)}, u32[]{:S(2)}) %collective-permute-start.57) | collective-permute-done | bytes 491552 | tf_op jit(solution)/shard_map/ppermute | solution.py:1035
  346.3 18.0 %shard_map.391 = (bf16[1024,256]{1,0:T(8,128)(2,1)}, bf16[1024,256]{1,0:T(8,128)(2,1)}, bf16[1024,512]{1,0:T(8,128)(2,1)}, bf16[1024,512]{1,0:T(8,128)(2,1)}, bf...) custom-call(s32[16]{0:T(128)} %stack.117.place_ref, s32[1]{0:T(128)} %bitcast.20.core_ref, bf16[512,2816]{1,0:T(8,128)(2,1)} %copy-done.3, ...), custom_call_target="tpu_custom_call" | custom-call | flops 8053063680 | bytes 10485760 | tf_op jit(solution)/shard_map/pallas_call | solution.py:805
  364.9 18.0 %shard_map.394 = (bf16[1024,256]{1,0:T(8,128)(2,1)}, bf16[1024,256]{1,0:T(8,128)(2,1)}, bf16[1024,512]{1,0:T(8,128)(2,1)}, bf16[1024,512]{1,0:T(8,128)(2,1)}, bf...) custom-call(s32[16]{0:T(128)} %stack.117.place_ref, s32[1]{0:T(128)} %bitcast.20.core_ref, bf16[512,2816]{1,0:T(8,128)(2,1)} %copy-done.3, ...), custom_call_target="tpu_custom_call" | custom-call | flops 8053063680 | bytes 10485760 | tf_op jit(solution)/shard_map/pallas_call | solution.py:805
  389.9 11.3 %shard_map.398 = (bf16[1024,256]{1,0:T(8,128)(2,1)}, bf16[1024,512]{1,0:T(8,128)(2,1)}, bf16[768,128]{1,0:T(8,128)(2,1)}) custom-call(s32[16]{0:T(128)} %stack.117.place_ref, s32[1]{0:T(128)} %bitcast.20.core_ref, bf16[512,2816]{1,0:T(8,128)(2,1)} %copy-done.3, bf16[256,2816]{1,0:T(8,128)(2,1)} %collective-permute-done.48.refs_1_.refs_2_.refs_13_, ...), custom_call_target="tpu_custom_call" | custom-call | flops 4026531840 | bytes 10485760 | tf_op jit(solution)/shard_map/pallas_call | solution.py:805
  410.6 7.9 %collective-permute-done.69.refs_11_.refs_1_.refs_77_ = bf16[320,768]{1,0:T(8,128)(2,1)} collective-permute-done((bf16[320,768]{1,0:T(8,128)(2,1)}, bf16[320,768]{1,0:T(8,128)(2,1)}, u32[]{:S(2)}, u32[]{:S(2)}) %collective-permute-start.69) | collective-permute-done | bytes 491552 | tf_op jit(solution)/shard_map/ppermute | solution.py:1035
  420.3 8.8 %collective-permute-done.71.refs_13_.refs_1_.refs_79_ = bf16[320,768]{1,0:T(8,128)(2,1)} collective-permute-done((bf16[320,768]{1,0:T(8,128)(2,1)}, bf16[320,768]{1,0:T(8,128)(2,1)}, u32[]{:S(2)}, u32[]{:S(2)}) %collective-permute-start.71) | collective-permute-done | bytes 491552 | tf_op jit(solution)/shard_map/ppermute | solution.py:1035
  430.8 11.3 %shard_map.403 = (bf16[1024,256]{1,0:T(8,128)(2,1)}, bf16[1024,512]{1,0:T(8,128)(2,1)}, bf16[768,128]{1,0:T(8,128)(2,1)}) custom-call(s32[16]{0:T(128)} %stack.117.place_ref, s32[1]{0:T(128)} %bitcast.20.core_ref, bf16[512,2816]{1,0:T(8,128)(2,1)} %copy-done.3, bf16[256,2816]{1,0:T(8,128)(2,1)} %collective-permute-done.48.refs_1_.refs_2_.refs_13_, ...), custom_call_target="tpu_custom_call" | custom-call | flops 4026531840 | bytes 10485760 | tf_op jit(solution)/shard_map/pallas_call | solution.py:805
  442.5 7.7 collective-permute-done.74.refs_1_.refs_21_
  451.9 8.8 %collective-permute-done.75.refs_23_ = bf16[320,768]{1,0:T(8,128)(2,1)} collective-permute-done((bf16[320,768]{1,0:T(8,128)(2,1)}, bf16[320,768]{1,0:T(8,128)(2,1)}, u32[]{:S(2)}, u32[]{:S(2)}) %collective-permute-start.75) | collective-permute-done | bytes 491552 | tf_op jit(solution)/shard_map/ppermute | solution.py:1035
  468.7 51.3 %shard_map.408 = (bf16[2,256,2816]{2,1,0:T(8,128)(2,1)}, bf16[2,256,2816]{2,1,0:T(8,128)(2,1)}, bf16[2,256,2688]{2,1,0:T(8,128)(2,1)}, bf16[2,256,2688]{2,1,0:T(...) custom-call(s32[16]{0:T(128)} %stack.117.place_ref, ...), custom_call_target="tpu_custom_call" | custom-call | flops 32212254720 | bytes 10485760 | tf_op jit(solution)/shard_map/pallas_call | solution.py:805
  544.9 18.5 %collective-permute-done.78.p2 = bf16[256,2816]{1,0:T(8,128)(2,1)} collective-permute-done((bf16[256,2816]{1,0:T(8,128)(2,1)}, bf16[256,2816]{1,0:T(8,128)(2,1)}, u32[]{:S(2)}, u32[]{:S(2)}) %collective-permute-start.78) | collective-permute-done | bytes 1441824 | tf_op jit(solution)/shard_map/ppermute | solution.py:1035
  586.9 36.6 %shard_map.410 = (bf16[512,2560]{1,0:T(8,128)(2,1)}, f32[512,384]{1,0:T(8,128)}, bf16[5120,128]{1,0:T(8,128)(2,1)}) custom-call(s32[1]{0:T(128)} %bitcast.20.core_ref, bf16[256,2560]{1,0:T(8,128)(2,1)} %get-tuple-element.204.mine_hbm.refs_1_, bf16[256,2560]{1,0:T(8,128)(2,1)} %collective-permute-done.79.other_hbm, f32[512,128]{1,0:T(8,128)} %copy-done.10, ...), custom_call_target="tpu_custom_call" | custom-call | flops 41943040000 | bytes 16384000 | tf_op jit(solution)/shard_map/pallas_call | solution.py:473
  663.5 8.7 %all-to-all-start.2 = ((bf16[16,96,384]{2,1,0:T(8,128)(2,1)}), bf16[16,96,384]{2,1,0:T(8,128)(2,1)S(1)}, u32[]{:S(2)}, u32[]{:S(2)}) async-start(bf16[16,96,384]{2,1,0:T(8,128)(2,1)} %get-tuple-element.238.refs_4_), calls=%async_computation.2 | async-start | bytes 2359296 | tf_op jit(solution)/shard_map/all_to_all | solution.py:1334
  686.2 18.5 %collective-permute-done.92.refs_2_ = bf16[4,672,128]{2,1,0:T(8,128)(2,1)S(1)} collective-permute-done((bf16[4,672,128]{2,1,0:T(8,128)(2,1)}, bf16[4,672,128]{2,1,0:T(8,128)(2,1)S(1)}, u32[]{:S(2)}, u32[]{:S(2)}) %collective-permute-start.92) | collective-permute-done | bytes 688160 | tf_op jit(solution)/shard_map/ppermute | solution.py:1035
  741.9 15.6 %collective-permute-done.97.refs_1_ = bf16[4,800,128]{2,1,0:T(8,128)(2,1)S(1)} collective-permute-done((bf16[4,800,128]{2,1,0:T(8,128)(2,1)S(1)}, bf16[4,800,128]{2,1,0:T(8,128)(2,1)S(1)}, u32[]{:S(2)}, u32[]{:S(2)}) %collective-permute-start.97) | collective-permute-done | bytes 819232 | tf_op jit(solution)/shard_map/ppermute | solution.py:1035
  757.5 18.5 %collective-permute-done.98.refs_2_ = bf16[4,800,128]{2,1,0:T(8,128)(2,1)S(1)} collective-permute-done((bf16[4,800,128]{2,1,0:T(8,128)(2,1)S(1)}, bf16[4,800,128]{2,1,0:T(8,128)(2,1)S(1)}, u32[]{:S(2)}, u32[]{:S(2)}) %collective-permute-start.98) | collective-permute-done | bytes 819232 | tf_op jit(solution)/shard_map/ppermute | solution.py:1035
  786.3 7.7 shard_map.419
  (599 shorter events, 422.0 us)
Async XLA Ops:
  5.8 81.5 %collective-permute-start.14 = (bf16[160,1600]{1,0:T(8,128)(2,1)}, bf16[160,1600]{1,0:T(8,128)(2,1)}, u32[]{:S(2)}, u32[]{:S(2)}) collective-permute-start(bf16[160,1600]{1,0:T(8,128)(2,1)} %pad_maximum_fusion.34), channel_id=1, source_target_pairs={{0,4},{2,6},{4,0},{6,2},{8,12},{10,14},{12,8},{14,10},{16,20},{18,... | collective-permute-start | bytes 1536008 | tf_op jit(solution)/shard_map/ppermute | solution.py:1035
  15.1 56.1 %collective-permute-start.8 = (bf16[160,1536]{1,0:T(8,128)(2,1)}, bf16[160,1536]{1,0:T(8,128)(2,1)}, u32[]{:S(2)}, u32[]{:S(2)}) collective-permute-start(bf16[160,1536]{1,0:T(8,128)(2,1)} %get-tuple-element.328), channel_id=1, source_target_pairs={{0,2},{2,0},{4,6},{6,4},{8,10},{10,8},{12,14},{14,12},{16,18},{18,... | collective-permute-start | bytes 1474568 | tf_op jit(solution)/shard_map/ppermute | solution.py:1035
  87.3 64.1 %collective-permute-start.28 = (bf16[320,768]{1,0:T(8,128)(2,1)}, bf16[320,768]{1,0:T(8,128)(2,1)}, u32[]{:S(2)}, u32[]{:S(2)}) collective-permute-start(bf16[320,768]{1,0:T(8,128)(2,1)} %shard_map.380.refs_6_.refs_27_), channel_id=1, source_target_pairs={{0,8},{2,10},{4,12},{6,14},{8,16},{10,18},{12,20},{14,22},{16,24},... | collective-permute-start | bytes 1474568 | tf_op jit(solution)/shard_map/ppermute | solution.py:1035
  117.8 65.0 %collective-permute-start.51 = (bf16[320,768]{1,0:T(8,128)(2,1)}, bf16[320,768]{1,0:T(8,128)(2,1)}, u32[]{:S(2)}, u32[]{:S(2)}) collective-permute-start(bf16[320,768]{1,0:T(8,128)(2,1)} %shard_map.383.refs_1_), channel_id=1, source_target_pairs={{0,4},{2,6},{4,0},{6,2},{8,12},{10,14},{12,8},{14,10},{16,20},{18,... | collective-permute-start | bytes 1474568 | tf_op jit(solution)/shard_map/ppermute | solution.py:1035
  210.9 47.6 %collective-permute-start.36 = (bf16[320,768]{1,0:T(8,128)(2,1)}, bf16[320,768]{1,0:T(8,128)(2,1)}, u32[]{:S(2)}, u32[]{:S(2)}) collective-permute-start(bf16[320,768]{1,0:T(8,128)(2,1)} %shard_map.385.refs_8_.refs_47_), channel_id=1, source_target_pairs={{0,8},{2,10},{4,12},{6,14},{8,16},{10,18},{12,20},{14,22},{16,24},... | collective-permute-start | bytes 1474568 | tf_op jit(solution)/shard_map/ppermute | solution.py:1035
  211.8 46.7 %collective-permute-start.37 = (bf16[320,768]{1,0:T(8,128)(2,1)}, bf16[320,768]{1,0:T(8,128)(2,1)}, u32[]{:S(2)}, u32[]{:S(2)}) collective-permute-start(bf16[320,768]{1,0:T(8,128)(2,1)} %shard_map.385.refs_8_.refs_47_), channel_id=1, source_target_pairs={{0,4},{2,6},{4,0},{6,2},{8,12},{10,14},{12,8},{14,10},{16,20},{18,... | collective-permute-start | bytes 1474568 | tf_op jit(solution)/shard_map/ppermute | solution.py:1035
  300.8 36.7 %collective-permute-start.48 = (bf16[256,2816]{1,0:T(8,128)(2,1)}, bf16[256,2816]{1,0:T(8,128)(2,1)}, u32[]{:S(2)}, u32[]{:S(2)}) collective-permute-start(bf16[256,2816]{1,0:T(8,128)(2,1)} %get-tuple-element.171), channel_id=1, source_target_pairs={{0,2},{2,0},{4,6},{6,4},{8,10},{10,8},{12,14},{14,12},{16,18},{18,... | collective-permute-start | bytes 4325384 | tf_op jit(solution)/shard_map/ppermute | solution.py:1035
  344.2 38.8 %collective-permute-start.61 = (bf16[320,768]{1,0:T(8,128)(2,1)}, bf16[320,768]{1,0:T(8,128)(2,1)}, u32[]{:S(2)}, u32[]{:S(2)}) collective-permute-start(bf16[320,768]{1,0:T(8,128)(2,1)} %get-tuple-element.188.refs_10_.refs_67_), channel_id=1, source_target_pairs={{0,4},{2,6},{4,0},{6,2},{8,12},{10,14},{12,8},{14,10},{16,20},{18,... | collective-permute-start | bytes 1474568 | tf_op jit(solution)/shard_map/ppermute | solution.py:1035
  345.9 37.0 %collective-permute-start.64 = (bf16[320,768]{1,0:T(8,128)(2,1)}, bf16[320,768]{1,0:T(8,128)(2,1)}, u32[]{:S(2)}, u32[]{:S(2)}) collective-permute-start(bf16[320,768]{1,0:T(8,128)(2,1)} %get-tuple-element.192.refs_0_), channel_id=1, source_target_pairs={{0,8},{2,10},{4,12},{6,14},{8,16},{10,18},{12,20},{14,22},{16,24},... | collective-permute-start | bytes 1474568 | tf_op jit(solution)/shard_map/ppermute | solution.py:1035
  529.4 33.9 %collective-permute-start.78 = (bf16[256,2816]{1,0:T(8,128)(2,1)}, bf16[256,2816]{1,0:T(8,128)(2,1)}, u32[]{:S(2)}, u32[]{:S(2)}) collective-permute-start(bf16[256,2816]{1,0:T(8,128)(2,1)} %fusion.1.refs_8_), channel_id=1, source_target_pairs={{0,2},{2,0},{4,6},{6,4},{8,10},{10,8},{12,14},{14,12},{16,18},{18,... | collective-permute-start | bytes 4325384 | tf_op jit(solution)/shard_map/ppermute | solution.py:1035
  530.6 45.8 %collective-permute-start.80 = (bf16[2,256,2688]{2,1,0:T(8,128)(2,1)}, bf16[2,256,2688]{2,1,0:T(8,128)(2,1)}, u32[]{:S(2)}, u32[]{:S(2)}) collective-permute-start(bf16[2,256,2688]{2,1,0:T(8,128)(2,1)} %get-tuple-element.219), channel_id=1, source_target_pairs={{0,1},{1,0},{2,3},{3,2},{4,5},{5,4},{6,7},{7,6},{8,9},{9,8},{10,11... | collective-permute-start | bytes 8257544 | tf_op jit(solution)/shard_map/ppermute | solution.py:1038
  535.7 43.8 %all-to-all-start.1 = ((bf16[8,672,128]{2,1,0:T(8,128)(2,1)}), bf16[8,672,128]{2,1,0:T(8,128)(2,1)}, u32[]{:S(2)}, u32[]{:S(2)}) async-start(bf16[8,672,128]{2,1,0:T(8,128)(2,1)} %bitcast.81), calls=%async_computation.1 | async-start | bytes 2752512 | tf_op jit(solution)/shard_map/all_to_all | solution.py:1291
  579.2 44.3 %collective-permute-start.81 = (bf16[256,2688]{1,0:T(8,128)(2,1)}, bf16[256,2688]{1,0:T(8,128)(2,1)}, u32[]{:S(2)}, u32[]{:S(2)}) collective-permute-start(bf16[256,2688]{1,0:T(8,128)(2,1)} %shard_map.412), channel_id=1, source_target_pairs={{0,2},{2,0},{4,6},{6,4},{8,10},{10,8},{12,14},{14,12},{16,18},{18,... | collective-permute-start | bytes 4128776 | tf_op jit(solution)/shard_map/ppermute | solution.py:1035
  579.5 44.0 %all-to-all-start = ((bf16[16,80,256]{2,1,0:T(8,128)(2,1)}), bf16[16,80,256]{2,1,0:T(8,128)(2,1)}, u32[]{:S(2)}, u32[]{:S(2)}) async-start(bf16[16,80,256]{2,1,0:T(8,128)(2,1)} %bitcast.85), calls=%async_computation | async-start | bytes 1310720 | tf_op jit(solution)/shard_map/all_to_all | solution.py:1302
  661.7 43.0 %collective-permute-start.92 = (bf16[4,672,128]{2,1,0:T(8,128)(2,1)}, bf16[4,672,128]{2,1,0:T(8,128)(2,1)S(1)}, u32[]{:S(2)}, u32[]{:S(2)}) collective-permute-start(bf16[4,672,128]{2,1,0:T(8,128)(2,1)} %get-tuple-element.242.refs_0_), channel_id=1, source_target_pairs={{0,4},{2,6},{4,0},{6,2},{8,12},{10,14},{12,8},{14,10},{16,20},{18,... | collective-permute-start | bytes 2064392 | tf_op jit(solution)/shard_map/ppermute | solution.py:1035
  663.1 42.6 %collective-permute-start.93 = (bf16[4,672,128]{2,1,0:T(8,128)(2,1)}, bf16[4,672,128]{2,1,0:T(8,128)(2,1)}, u32[]{:S(2)}, u32[]{:S(2)}) collective-permute-start(bf16[4,672,128]{2,1,0:T(8,128)(2,1)} %get-tuple-element.242.refs_0_), channel_id=1, source_target_pairs={{0,6},{2,4},{4,2},{6,0},{8,14},{10,12},{12,10},{14,8},{16,22},{18,... | collective-permute-start | bytes 2064392 | tf_op jit(solution)/shard_map/ppermute | solution.py:1035
  663.5 43.7 %all-to-all-start.2 = ((bf16[16,96,384]{2,1,0:T(8,128)(2,1)}), bf16[16,96,384]{2,1,0:T(8,128)(2,1)S(1)}, u32[]{:S(2)}, u32[]{:S(2)}) async-start(bf16[16,96,384]{2,1,0:T(8,128)(2,1)} %get-tuple-element.238.refs_4_), calls=%async_computation.2 | async-start | bytes 2359296 | tf_op jit(solution)/shard_map/all_to_all | solution.py:1334
  672.2 64.2 %collective-permute-start.104 = (bf16[4,672,128]{2,1,0:T(8,128)(2,1)}, bf16[4,672,128]{2,1,0:T(8,128)(2,1)}, u32[]{:S(2)}, u32[]{:S(2)}) collective-permute-start(bf16[4,672,128]{2,1,0:T(8,128)(2,1)} %get-tuple-element.242.refs_0_), channel_id=1, source_target_pairs={{0,1},{1,0},{2,3},{3,2},{4,5},{5,4},{6,7},{7,6},{8,9},{9,8},{10,11... | collective-permute-start | bytes 2064392 | tf_op jit(solution)/shard_map/ppermute | solution.py:1038
  677.8 40.2 %collective-permute-start.88 = (bf16[256,2560]{1,0:T(8,128)(2,1)}, bf16[256,2560]{1,0:T(8,128)(2,1)}, u32[]{:S(2)}, u32[]{:S(2)}) collective-permute-start(bf16[256,2560]{1,0:T(8,128)(2,1)} %add_convert_fusion.3), channel_id=1, source_target_pairs={{0,1},{1,0},{2,3},{3,2},{4,5},{5,4},{6,7},{7,6},{8,9},{9,8},{10,11... | collective-permute-start | bytes 3932168 | tf_op jit(solution)/shard_map/ppermute | solution.py:1038
  685.7 52.4 %collective-permute-start.90 = (bf16[256,2560]{1,0:T(8,128)(2,1)}, bf16[256,2560]{1,0:T(8,128)(2,1)}, u32[]{:S(2)}, u32[]{:S(2)}) collective-permute-start(bf16[256,2560]{1,0:T(8,128)(2,1)} %add_convert_fusion.2), channel_id=1, source_target_pairs={{0,1},{1,0},{2,3},{3,2},{4,5},{5,4},{6,7},{7,6},{8,9},{9,8},{10,11... | collective-permute-start | bytes 3932168 | tf_op jit(solution)/shard_map/ppermute | solution.py:1038
  736.3 42.0 %collective-permute-start.107 = (bf16[4,672,128]{2,1,0:T(8,128)(2,1)}, bf16[4,672,128]{2,1,0:T(8,128)(2,1)S(1)}, u32[]{:S(2)}, u32[]{:S(2)}) collective-permute-start(bf16[4,672,128]{2,1,0:T(8,128)(2,1)} %get-tuple-element.256.refs_3_), channel_id=1, source_target_pairs={{0,1},{1,0},{2,3},{3,2},{4,5},{5,4},{6,7},{7,6},{8,9},{9,8},{10,11... | collective-permute-start | bytes 2064392 | tf_op jit(solution)/shard_map/ppermute | solution.py:1038
  738.1 37.9 %collective-permute-start.98 = (bf16[4,800,128]{2,1,0:T(8,128)(2,1)S(1)}, bf16[4,800,128]{2,1,0:T(8,128)(2,1)S(1)}, u32[]{:S(2)}, u32[]{:S(2)}) collective-permute-start(bf16[4,800,128]{2,1,0:T(8,128)(2,1)S(1)} %pad_maximum_fusion.31.refs_0_), channel_id=1, source_target_pairs={{0,4},{2,6},{4,0},{6,2},{8,12},{10,14},{12,8},{14,10},{16,20},{18,... | collective-permute-start | bytes 2457608 | tf_op jit(solution)/shard_map/ppermute | solution.py:1035
  739.0 37.0 %collective-permute-start.99 = (bf16[4,800,128]{2,1,0:T(8,128)(2,1)S(1)}, bf16[4,800,128]{2,1,0:T(8,128)(2,1)S(1)}, u32[]{:S(2)}, u32[]{:S(2)}) collective-permute-start(bf16[4,800,128]{2,1,0:T(8,128)(2,1)S(1)} %pad_maximum_fusion.31.refs_0_), channel_id=1, source_target_pairs={{0,6},{2,4},{4,2},{6,0},{8,14},{10,12},{12,10},{14,8},{16,22},{18,... | collective-permute-start | bytes 2457608 | tf_op jit(solution)/shard_map/ppermute | solution.py:1035
  741.8 43.6 %collective-permute-start.100 = (bf16[4,800,128]{2,1,0:T(8,128)(2,1)S(1)}, bf16[4,800,128]{2,1,0:T(8,128)(2,1)S(1)}, u32[]{:S(2)}, u32[]{:S(2)}) collective-permute-start(bf16[4,800,128]{2,1,0:T(8,128)(2,1)S(1)} %pad_maximum_fusion.31.refs_0_), channel_id=1, source_target_pairs={{0,1},{1,0},{2,3},{3,2},{4,5},{5,4},{6,7},{7,6},{8,9},{9,8},{10,11... | collective-permute-start | bytes 2457608 | tf_op jit(solution)/shard_map/ppermute | solution.py:1038
  (207 other events, 2353.2 us)

commit v4 on v3

--- a/solution.py
+++ b/solution.py
@@ -30,6 +30,8 @@
 ATTN_PRIORITY = (-20, -10)
 YZ_CHUNKS = ()
 LAST_WIDE = 30
+CHUNK_PRIORITY = (0, 1, 2, 3, 4, 5, 6)
+BY_RING_FROM = (9, 9, 9, 9, 3, 3, 3)
 
 
 def matrix_product(left, right):
@@ -87,8 +89,11 @@
             source = (f"{tag}.p{r}" if r else tag)
             if r:
                 before = f"{tag}.p{r - 1}" if r > 1 else tag
-                plan[f"{tag}.p{r}"] = ("z", before, j + 0.01 * r, 1)
-            plan[f"{tag}.q{r}"] = ("y", source, j + 0.01 * r, 1)
+                plan[f"{tag}.p{r}"] = ("z", before, CHUNK_PRIORITY[min(j, 6)] + 0.01 * r, 1)
+            link = "y"
+            if r >= BY_RING_FROM[min(j, 6)]:
+                link, source = "z", f"{tag}.q{r - 1}"
+            plan[f"{tag}.q{r}"] = (link, source, CHUNK_PRIORITY[min(j, 6)] + 0.01 * r, 1)
     plan["C.x"] = ("x", "C.o", LAST_WIDE, 3)
     plan["N.x"] = ("x", "N.o", -50, 3)
     return plan
@@ -903,9 +908,9 @@
     )(got)
 
 
-def unit_results(at, parts, chunks):
+def unit_results(at, parts, order):
     ring, share, cols = parts[0].shape
-    units = chunks * WIDTH
+    units = len(order) * WIDTH
 
     def kernel(at_ref, *refs):
         gate_out, up_out, down_out, all_s = refs[8:]
@@ -922,9 +927,9 @@
 
             lax.fori_loop(0, ring, one, 0)
         for q in range(4):
-            for j in range(chunks):
+            for i, j in enumerate(order):
                 start = q * units + j * WIDTH
-                row = j * 3 * WIDTH
+                row = i * 3 * WIDTH
                 for at in range(0, WIDTH, cols):
                     to = slice(start + at, start + at + cols)
                     gate_out[:, to] = all_s[q, row + at : row + at + cols, :]
@@ -1203,7 +1208,7 @@
 
         unit_out = {}
 
-        def feed(new, old, totals, last):
+        def feed(new, old, totals, last, core_at=core_at):
             found = {j: pieces(f"M{j}") for j in new + old}
             sums, results = feed_forward(
                 found[(new + old)[0]][1],
@@ -1272,7 +1277,8 @@
             for run in events.get(s, []):
                 waits += run()
 
-        totals = feed([final], early + later, None, True)
+        own = jnp.concatenate([unit_out[j][2] for j in order[:-1]], axis=0)
+        totals = feed([final], early + later, None, True, tie([core_at], [own], 0)[0])
         grad_keep, grad_send, out_keep, out_send = totals
 
         def after(values, *others):
@@ -1281,13 +1287,15 @@
         def total(parts):
             return jnp.sum(parts.astype(F32), axis=0).astype(BF)
 
+        own = jnp.concatenate([own, unit_out[final][2]], axis=0)
         grad_got = other_core(grad_send)
         grad_out = (grad_keep[1].astype(F32) + grad_got[1].astype(F32)).astype(BF)
-        grad_in_parts = (grad_keep[0], grad_got[0], move(grad_out, "x"))
-        out_send, *own = after([out_send] + [unit_out[j][2] for j in range(chunks)], grad_out)
+        grad_own = tie([grad_keep[0]], [grad_out])[0]
+        own = after([own], grad_own)[0]
+        grad_in_parts = (grad_own, grad_got[0], move(grad_out, "x"))
+        out_send = after([out_send], grad_out)[0]
         out_got = other_core(out_send)
         out_out = (out_keep[1].astype(F32) + out_got[1].astype(F32)).astype(BF)
-        own = jnp.concatenate(own, axis=0)
         got_units = lax.all_to_all(own.reshape(n // 2, -1, rank_cols), DP[:2], 0, 0)
 
         grad_middle, grad_branch, grad_low_mlp = after_feed_forward(
@@ -1301,12 +1309,14 @@
         ).astype(BF)
         got_mlp = lax.all_to_all(delta_mlp.reshape(n, half_width // n, 2 * rank_cols), DP, 0, 0)
 
+        units_sum = [total(got_units)]
+        units_sum += [move(units_sum[0], f"z{r}") for r in range(1, ring_size)]
         back, back_low, factors = attention_back(
             core_at, (grad_branch, grad_branch_other), select, second_output, v["low_output"],
             v["attended"], in_output, v["a0"], v["a1"], v["query"], v["key"], v["value"], v["lse"],
             cos_table, sin_table, second_query, second_key, second_value, *lows,
         )
-        back_low, out_in, got_mlp, got_units = after([back_low, out_in, got_mlp, got_units])
+        back_low, out_in, got_mlp, *units_sum = after([back_low, out_in, got_mlp] + units_sum)
         back_low = back_low + other_core(back_low)
         grad_low_attn = (back_low * select_three).astype(BF)
         out_sum = out_keep[0].astype(F32) + out_got[0].astype(F32) + out_in.astype(F32)
@@ -1328,17 +1338,18 @@
             + [jnp.broadcast_to(chosen[None], (n,) + chosen.shape)],
             axis=1,
         )
-        units_sum = total(got_units)
-        units_sum = jnp.stack([units_sum] + [move(units_sum, f"z{r}") for r in range(1, ring_size)])
-        packed, units_sum = after([packed, units_sum])
+        units_sum = jnp.stack(units_sum)
         got_late = lax.all_to_all(packed, DP, 0, 0)
-        got_mlp, back, out_sum, grad_middle = after([got_mlp, back, out_sum, grad_middle], packed)
         units_parts = [units_sum] + [move(units_sum, link) for link in ("x", "y", "xy")]
         got_late, *units_parts[1:] = after([got_late] + units_parts[1:])
+        late = unpack(got_late)
+        back, out_sum, grad_middle, hidden_half = after(
+            [back, out_sum, grad_middle, half_of(hidden_in)], late
+        )
 
         device = jnp.stack([core, bit_y, bit_x, ring_at]).astype(jnp.int32)
         gradient_second_gate, gradient_second_up, delta_in_down = unit_results(
-            device, units_parts + [other_core(part) for part in units_parts], chunks
+            device, units_parts + [other_core(part) for part in units_parts], order
         )
 
         layer_output = both_halves(
@@ -1353,12 +1364,12 @@
         ).astype(F32)
         grad_normed_a = back_half + product_with_transpose(half_of(grad_low_attn), attn_in)
         grad_in = both_halves(
-            (grad_middle + rms_back(half_of(hidden_wide), attn_gain_f, grad_normed_a)).astype(BF)
+            (grad_middle + rms_back(hidden_half.astype(F32), attn_gain_f, grad_normed_a)).astype(BF)
         )
 
         sums_mlp = total(got_mlp)
         sums = jnp.concatenate(
-            [unpack(got_late).reshape(-1, rank_cols), sums_mlp[:, :rank_cols], sums_mlp[:, rank_cols:]],
+            [late.reshape(-1, rank_cols), sums_mlp[:, :rank_cols], sums_mlp[:, rank_cols:]],
             axis=0,
         )
         sums = jnp.stack([sums] + [move(sums, f"z{r}") for r in range(1, ring_size)], axis=0)

time: 803 us -> 792 us (0.986)
  starting transfers between devices: 129 us -> 111 us
  local copies, waits for them, and re-layouts: 78.9 us -> 92.4 us
  other arithmetic: 66.5 us -> 54 us
  waiting for transfers between devices: 286 us -> 295 us
    unnamed x265 -> x337, local copies, waits for them, and re-layouts: 55.5 us -> 68.9 us
    ppermute x87, waiting for transfers between devices: 278 us -> 290 us  [move(): return lax.ppermute(value, DP, perms[link])]
    ppermute x87, starting transfers between devices: 104 us -> 93.1 us  [move(): return lax.ppermute(value, DP, perms[link])]
  transfers between devices with their start and end apart: 111 -> 111, of which waited for: 48 -> 45; matrix products, arithmetic and copies ran while one was open for 15% -> 13% of each run, Pallas kernels for 20% -> 21%
where the time goes in v4:
time: 792 us; the launch traced here: 783 us
  waiting for transfers between devices  295 us (37%)
  Pallas kernels  217 us (27%)
  starting transfers between devices  111 us (14%)
  local copies, waits for them, and re-layouts  92.4 us (12%)
  other arithmetic  54 us (7%)
  matrix products  11.6 us (1%)
    ppermute x87, waiting for transfers between devices, move(): return lax.ppermute(value, DP, perms[link])  290 us
    pallas_call x5, Pallas kernels, feed_forward(): pl.pallas_call(kernel, out_shape=out_shape, in_specs=[SMEM] * 2 + [VMEM]...  111 us
    ppermute x87, starting transfers between devices, move(): return lax.ppermute(value, DP, perms[link])  93.1 us
    unnamed x337, local copies, waits for them, and re-layouts  68.9 us
    pallas_call x1, Pallas kernels, attention_back(): pl.pallas_call(kernel, out_shape=[jax.ShapeDtypeStruct((tokens, width), B...  36.6 us
    pallas_call x1, Pallas kernels, attention(): pl.pallas_call(kernel, out_shape=[jax.ShapeDtypeStruct((k_cols, tokens),...  20.3 us
  transfers between devices with their start and end apart: 111, of which 45 were waited for; matrix products, arithmetic and copies ran while one was open for 13% of the time, Pallas kernels for 21%

profile of v4, /device:TPU:0, one launch (start us, length us, event | category | flops | bytes accessed | tf_op | source)
XLA Modules:
  0.0 783.1 jit_solution(14490377161048428758)
XLA Ops:
  94.6 14.0 %collective-permute-done.12.refs_3_.refs_16_.refs_55_ = bf16[320,768]{1,0:T(8,128)(2,1)S(1)} collective-permute-done((bf16[320,768]{1,0:T(8,128)(2,1)S(1)}, bf16[320,768]{1,0:T(8,128)(2,1)S(1)}, u32[]{:S(2)}, u32[]{:S(2)}) %collective-permute-start.12) | collective-permute-done | bytes 491552 | tf_op jit(solution)/shard_map/ppermute | solution.py:1040
  118.8 14.0 %collective-permute-done.15.refs_1_ = bf16[160,1600]{1,0:T(8,128)(2,1)S(1)} collective-permute-done((bf16[160,1600]{1,0:T(8,128)(2,1)}, bf16[160,1600]{1,0:T(8,128)(2,1)S(1)}, u32[]{:S(2)}, u32[]{:S(2)}) %collective-permute-start.15) | collective-permute-done | bytes 512032 | tf_op jit(solution)/shard_map/ppermute | solution.py:1040
  136.9 13.8 %shard_map.373 = (bf16[1280,512]{1,0:T(8,128)(2,1)}, bf16[320,512]{1,0:T(8,128)(2,1)S(1)}, bf16[2560,1600]{1,0:T(8,128)(2,1)}) custom-call(s32[16]{0:T(128)S(1)} %stack.104.place_ref, bf16[512,2560]{1,0:T(8,128)(2,1)} %copy-done.63, bf16[512,128]{1,0:T(8,128)(2,1)S(1)} %get-tuple-element.324.lq_ref, bf16[512,128]{1,0:T(8,128)(2,1)S(1)} %get-tuple-element.323.lk_ref, ...), custom_call_target="tpu_custom_call" | custom-call | flops 4194304000 | bytes 16384000 | tf_op jit(solution)/shard_map/pallas_call | solution.py:225
  170.1 9.1 %collective-permute-done.20.refs_1_ = bf16[320,768]{1,0:T(8,128)(2,1)} collective-permute-done((bf16[320,768]{1,0:T(8,128)(2,1)}, bf16[320,768]{1,0:T(8,128)(2,1)}, u32[]{:S(2)}, u32[]{:S(2)}) %collective-permute-start.20) | collective-permute-done | bytes 491552 | tf_op jit(solution)/shard_map/ppermute | solution.py:1040
  213.2 7.1 collective-permute-done.39.refs_1_
  220.3 10.1 %collective-permute-done.25.refs_7_.refs_3_ = bf16[320,1600]{1,0:T(8,128)(2,1)S(1)} collective-permute-done((bf16[320,1600]{1,0:T(8,128)(2,1)}, bf16[320,1600]{1,0:T(8,128)(2,1)S(1)}, u32[]{:S(2)}, u32[]{:S(2)}) %collective-permute-start.25) | collective-permute-done | bytes 1024032 | tf_op jit(solution)/shard_map/ppermute | solution.py:1040
  238.8 20.3 %shard_map.378 = (bf16[320,512]{1,0:T(8,128)(2,1)S(1)}, bf16[512,1280]{1,0:T(8,128)(2,1)}, f32[4,4,512]{2,1,0:T(4,128)S(1)}, bf16[512,2560]{1,0:T(8,128)(2,1)}, ...) custom-call(s32[16]{0:T(128)S(1)} %stack.104.place_ref, bf16[512,2560]{1,0:T(8,128)(2,1)} %copy-done.63, ...), custom_call_target="tpu_custom_call" | custom-call | flops 8388608000 | bytes 16384000 | tf_op jit(solution)/shard_map/pallas_call | solution.py:326
  280.9 8.9 %shard_map.379 = (f32[512,2560]{1,0:T(8,128)}, bf16[512,2816]{1,0:T(8,128)(2,1)S(1)}, bf16[512,128]{1,0:T(8,128)(2,1)S(1)}) custom-call(bf16[512,2560]{1,0:T(8,128)(2,1)S(1)} %copy-done.4, bf16[512,2560]{1,0:T(8,128)(2,1)} %get-tuple-element.150.b0, bf16[512,2560]{1,0:T(8,128)(2,1)} %collective-permute-done.26.b1, f32[512,128]{1,0:T(8,128)S(1)} %get-tuple-element.151.l0, ...), custom_call_target="tpu_custom_call" | custom-call | flops 1006632960 | bytes 18350080 | tf_op jit(solution)/shard_map/pallas_call | solution.py:533
  303.0 10.8 %collective-permute-done.57.refs_2_.refs_7_.refs_64_ = bf16[320,768]{1,0:T(8,128)(2,1)S(1)} collective-permute-done((bf16[320,768]{1,0:T(8,128)(2,1)}, bf16[320,768]{1,0:T(8,128)(2,1)S(1)}, u32[]{:S(2)}, u32[]{:S(2)}) %collective-permute-start.57) | collective-permute-done | bytes 491552 | tf_op jit(solution)/shard_map/ppermute | solution.py:1040
  349.0 18.0 %shard_map.391 = (bf16[1024,256]{1,0:T(8,128)(2,1)}, bf16[1024,256]{1,0:T(8,128)(2,1)}, bf16[1024,512]{1,0:T(8,128)(2,1)}, bf16[1024,512]{1,0:T(8,128)(2,1)}, bf...) custom-call(s32[16]{0:T(128)} %stack.117.place_ref, s32[1]{0:T(128)} %bitcast.20.core_ref, bf16[512,2816]{1,0:T(8,128)(2,1)} %copy-done.1, ...), custom_call_target="tpu_custom_call" | custom-call | flops 8053063680 | bytes 10485760 | tf_op jit(solution)/shard_map/pallas_call | solution.py:810
  367.6 18.0 %shard_map.394 = (bf16[1024,256]{1,0:T(8,128)(2,1)}, bf16[1024,256]{1,0:T(8,128)(2,1)}, bf16[1024,512]{1,0:T(8,128)(2,1)}, bf16[1024,512]{1,0:T(8,128)(2,1)}, bf...) custom-call(s32[16]{0:T(128)} %stack.117.place_ref, s32[1]{0:T(128)} %bitcast.20.core_ref, bf16[512,2816]{1,0:T(8,128)(2,1)} %copy-done.1, ...), custom_call_target="tpu_custom_call" | custom-call | flops 8053063680 | bytes 10485760 | tf_op jit(solution)/shard_map/pallas_call | solution.py:810
  389.6 9.0 %collective-permute-done.64.refs_13_.refs_3_.refs_70_ = bf16[320,768]{1,0:T(8,128)(2,1)S(1)} collective-permute-done((bf16[320,768]{1,0:T(8,128)(2,1)}, bf16[320,768]{1,0:T(8,128)(2,1)S(1)}, u32[]{:S(2)}, u32[]{:S(2)}) %collective-permute-start.64) | collective-permute-done | bytes 491552 | tf_op jit(solution)/shard_map/ppermute | solution.py:1040
  405.1 11.3 %shard_map.398 = (bf16[1024,256]{1,0:T(8,128)(2,1)}, bf16[1024,512]{1,0:T(8,128)(2,1)}, bf16[768,128]{1,0:T(8,128)(2,1)}) custom-call(s32[16]{0:T(128)} %stack.117.place_ref, s32[1]{0:T(128)} %bitcast.20.core_ref, bf16[512,2816]{1,0:T(8,128)(2,1)} %copy-done.1, bf16[256,2816]{1,0:T(8,128)(2,1)} %collective-permute-done.48.refs_1_.refs_2_.refs_13_, ...), custom_call_target="tpu_custom_call" | custom-call | flops 4026531840 | bytes 10485760 | tf_op jit(solution)/shard_map/pallas_call | solution.py:810
  427.5 12.2 %collective-permute-done.70.refs_13_.refs_79_ = bf16[320,768]{1,0:T(8,128)(2,1)} collective-permute-done((bf16[320,768]{1,0:T(8,128)(2,1)}, bf16[320,768]{1,0:T(8,128)(2,1)}, u32[]{:S(2)}, u32[]{:S(2)}) %collective-permute-start.70) | collective-permute-done | bytes 491552 | tf_op jit(solution)/shard_map/ppermute | solution.py:1040
  439.7 11.3 %shard_map.403 = (bf16[1024,256]{1,0:T(8,128)(2,1)}, bf16[1024,512]{1,0:T(8,128)(2,1)}, bf16[768,128]{1,0:T(8,128)(2,1)}) custom-call(s32[16]{0:T(128)} %stack.117.place_ref, s32[1]{0:T(128)} %bitcast.20.core_ref, bf16[512,2816]{1,0:T(8,128)(2,1)} %copy-done.1, bf16[256,2816]{1,0:T(8,128)(2,1)} %collective-permute-done.48.refs_1_.refs_2_.refs_13_, ...), custom_call_target="tpu_custom_call" | custom-call | flops 4026531840 | bytes 10485760 | tf_op jit(solution)/shard_map/pallas_call | solution.py:810
  462.9 52.1 %shard_map.407 = (bf16[2,256,2816]{2,1,0:T(8,128)(2,1)}, bf16[2,256,2816]{2,1,0:T(8,128)(2,1)}, bf16[2,256,2688]{2,1,0:T(8,128)(2,1)}, bf16[2,256,2688]{2,1,0:T(...) custom-call(s32[16]{0:T(128)} %stack.117.place_ref, ...), custom_call_target="tpu_custom_call" | custom-call | flops 32212254720 | bytes 10485760 | tf_op jit(solution)/shard_map/pallas_call | solution.py:810
  529.2 31.9 %collective-permute-done.78.p2 = bf16[256,2816]{1,0:T(8,128)(2,1)S(1)} collective-permute-done((bf16[256,2816]{1,0:T(8,128)(2,1)S(1)}, bf16[256,2816]{1,0:T(8,128)(2,1)S(1)}, u32[]{:S(2)}, u32[]{:S(2)}) %collective-permute-start.78) | collective-permute-done | bytes 1441824 | tf_op jit(solution)/shard_map/ppermute | solution.py:1040
  593.8 36.6 %shard_map.410 = (bf16[512,2560]{1,0:T(8,128)(2,1)}, f32[512,384]{1,0:T(8,128)}, bf16[5120,128]{1,0:T(8,128)(2,1)}) custom-call(s32[1]{0:T(128)} %bitcast.20.core_ref, bf16[256,2560]{1,0:T(8,128)(2,1)} %get-tuple-element.203.mine_hbm.refs_1_, bf16[256,2560]{1,0:T(8,128)(2,1)} %collective-permute-done.79.other_hbm, f32[512,128]{1,0:T(8,128)} %copy-done.15, ...), custom_call_target="tpu_custom_call" | custom-call | flops 41943040000 | bytes 16384000 | tf_op jit(solution)/shard_map/pallas_call | solution.py:478
  651.6 26.0 %collective-permute-done.88.refs_1_ = bf16[4,672,128]{2,1,0:T(8,128)(2,1)S(1)} collective-permute-done((bf16[4,672,128]{2,1,0:T(8,128)(2,1)S(1)}, bf16[4,672,128]{2,1,0:T(8,128)(2,1)S(1)}, u32[]{:S(2)}, u32[]{:S(2)}) %collective-permute-start.88) | collective-permute-done | bytes 688160 | tf_op jit(solution)/shard_map/ppermute | solution.py:1040
  677.7 15.2 %collective-permute-done.90.refs_3_ = bf16[4,672,128]{2,1,0:T(8,128)(2,1)} collective-permute-done((bf16[4,672,128]{2,1,0:T(8,128)(2,1)S(1)}, bf16[4,672,128]{2,1,0:T(8,128)(2,1)}, u32[]{:S(2)}, u32[]{:S(2)}) %collective-permute-start.90) | collective-permute-done | bytes 688160 | tf_op jit(solution)/shard_map/ppermute | solution.py:1040
  729.5 7.5 shard_map.420
  737.0 7.5 collective-permute-done.97.refs_1_
  744.5 17.4 %collective-permute-done.98.refs_2_ = bf16[4,800,128]{2,1,0:T(8,128)(2,1)S(1)} collective-permute-done((bf16[4,800,128]{2,1,0:T(8,128)(2,1)S(1)}, bf16[4,800,128]{2,1,0:T(8,128)(2,1)S(1)}, u32[]{:S(2)}, u32[]{:S(2)}) %collective-permute-start.98) | collective-permute-done | bytes 819232 | tf_op jit(solution)/shard_map/ppermute | solution.py:1040
  773.1 7.7 shard_map.419
  (671 shorter events, 390.5 us)
Async XLA Ops:
  5.7 81.5 %collective-permute-start.14 = (bf16[160,1600]{1,0:T(8,128)(2,1)}, bf16[160,1600]{1,0:T(8,128)(2,1)}, u32[]{:S(2)}, u32[]{:S(2)}) collective-permute-start(bf16[160,1600]{1,0:T(8,128)(2,1)} %pad_maximum_fusion.34), channel_id=1, source_target_pairs={{0,4},{2,6},{4,0},{6,2},{8,12},{10,14},{12,8},{14,10},{16,20},{18,... | collective-permute-start | bytes 1536008 | tf_op jit(solution)/shard_map/ppermute | solution.py:1040
  15.3 56.0 %collective-permute-start.8 = (bf16[160,1536]{1,0:T(8,128)(2,1)}, bf16[160,1536]{1,0:T(8,128)(2,1)}, u32[]{:S(2)}, u32[]{:S(2)}) collective-permute-start(bf16[160,1536]{1,0:T(8,128)(2,1)} %get-tuple-element.314), channel_id=1, source_target_pairs={{0,2},{2,0},{4,6},{6,4},{8,10},{10,8},{12,14},{14,12},{16,18},{18,... | collective-permute-start | bytes 1474568 | tf_op jit(solution)/shard_map/ppermute | solution.py:1040
  87.3 64.2 %collective-permute-start.28 = (bf16[320,768]{1,0:T(8,128)(2,1)}, bf16[320,768]{1,0:T(8,128)(2,1)}, u32[]{:S(2)}, u32[]{:S(2)}) collective-permute-start(bf16[320,768]{1,0:T(8,128)(2,1)} %shard_map.380.refs_6_.refs_27_), channel_id=1, source_target_pairs={{0,8},{2,10},{4,12},{6,14},{8,16},{10,18},{12,20},{14,22},{16,24},... | collective-permute-start | bytes 1474568 | tf_op jit(solution)/shard_map/ppermute | solution.py:1040
  117.8 65.2 %collective-permute-start.51 = (bf16[320,768]{1,0:T(8,128)(2,1)}, bf16[320,768]{1,0:T(8,128)(2,1)}, u32[]{:S(2)}, u32[]{:S(2)}) collective-permute-start(bf16[320,768]{1,0:T(8,128)(2,1)} %shard_map.383.refs_1_), channel_id=1, source_target_pairs={{0,4},{2,6},{4,0},{6,2},{8,12},{10,14},{12,8},{14,10},{16,20},{18,... | collective-permute-start | bytes 1474568 | tf_op jit(solution)/shard_map/ppermute | solution.py:1040
  211.1 48.7 %collective-permute-start.36 = (bf16[320,768]{1,0:T(8,128)(2,1)}, bf16[320,768]{1,0:T(8,128)(2,1)}, u32[]{:S(2)}, u32[]{:S(2)}) collective-permute-start(bf16[320,768]{1,0:T(8,128)(2,1)} %shard_map.385.refs_8_.refs_47_), channel_id=1, source_target_pairs={{0,8},{2,10},{4,12},{6,14},{8,16},{10,18},{12,20},{14,22},{16,24},... | collective-permute-start | bytes 1474568 | tf_op jit(solution)/shard_map/ppermute | solution.py:1040
  212.5 47.3 %collective-permute-start.37 = (bf16[320,768]{1,0:T(8,128)(2,1)}, bf16[320,768]{1,0:T(8,128)(2,1)}, u32[]{:S(2)}, u32[]{:S(2)}) collective-permute-start(bf16[320,768]{1,0:T(8,128)(2,1)} %shard_map.385.refs_8_.refs_47_), channel_id=1, source_target_pairs={{0,4},{2,6},{4,0},{6,2},{8,12},{10,14},{12,8},{14,10},{16,20},{18,... | collective-permute-start | bytes 1474568 | tf_op jit(solution)/shard_map/ppermute | solution.py:1040
  231.4 35.5 %collective-permute-start.41 = (bf16[160,2304]{1,0:T(8,128)(2,1)}, bf16[160,2304]{1,0:T(8,128)(2,1)}, u32[]{:S(2)}, u32[]{:S(2)}) collective-permute-start(bf16[160,2304]{1,0:T(8,128)(2,1)} %get-tuple-element.158), channel_id=1, source_target_pairs={{0,2},{2,0},{4,6},{6,4},{8,10},{10,8},{12,14},{14,12},{16,18},{18,... | collective-permute-start | bytes 2211848 | tf_op jit(solution)/shard_map/ppermute | solution.py:1040
  302.4 36.4 %collective-permute-start.48 = (bf16[256,2816]{1,0:T(8,128)(2,1)}, bf16[256,2816]{1,0:T(8,128)(2,1)}, u32[]{:S(2)}, u32[]{:S(2)}) collective-permute-start(bf16[256,2816]{1,0:T(8,128)(2,1)} %get-tuple-element.164), channel_id=1, source_target_pairs={{0,2},{2,0},{4,6},{6,4},{8,10},{10,8},{12,14},{14,12},{16,18},{18,... | collective-permute-start | bytes 4325384 | tf_op jit(solution)/shard_map/ppermute | solution.py:1040
  345.5 40.1 %collective-permute-start.61 = (bf16[320,768]{1,0:T(8,128)(2,1)}, bf16[320,768]{1,0:T(8,128)(2,1)}, u32[]{:S(2)}, u32[]{:S(2)}) collective-permute-start(bf16[320,768]{1,0:T(8,128)(2,1)} %get-tuple-element.177.refs_10_.refs_67_), channel_id=1, source_target_pairs={{0,4},{2,6},{4,0},{6,2},{8,12},{10,14},{12,8},{14,10},{16,20},{18,... | collective-permute-start | bytes 1474568 | tf_op jit(solution)/shard_map/ppermute | solution.py:1040
  347.3 38.3 %collective-permute-start.62 = (bf16[320,768]{1,0:T(8,128)(2,1)}, bf16[320,768]{1,0:T(8,128)(2,1)}, u32[]{:S(2)}, u32[]{:S(2)}) collective-permute-start(bf16[320,768]{1,0:T(8,128)(2,1)} %get-tuple-element.178.refs_1_), channel_id=1, source_target_pairs={{0,8},{2,10},{4,12},{6,14},{8,16},{10,18},{12,20},{14,22},{16,24},... | collective-permute-start | bytes 1474568 | tf_op jit(solution)/shard_map/ppermute | solution.py:1040
  522.6 66.6 %collective-permute-start.80 = (bf16[2,256,2688]{2,1,0:T(8,128)(2,1)}, bf16[2,256,2688]{2,1,0:T(8,128)(2,1)}, u32[]{:S(2)}, u32[]{:S(2)}) collective-permute-start(bf16[2,256,2688]{2,1,0:T(8,128)(2,1)} %shard_map.411), channel_id=1, source_target_pairs={{0,1},{1,0},{2,3},{3,2},{4,5},{5,4},{6,7},{7,6},{8,9},{9,8},{10,11... | collective-permute-start | bytes 8257544 | tf_op jit(solution)/shard_map/ppermute | solution.py:1043
  522.7 53.4 %all-to-all-start.1 = ((bf16[8,672,128]{2,1,0:T(8,128)(2,1)}), bf16[8,672,128]{2,1,0:T(8,128)(2,1)}, u32[]{:S(2)}, u32[]{:S(2)}) async-start(bf16[8,672,128]{2,1,0:T(8,128)(2,1)} %bitcast.81), calls=%async_computation.1 | async-start | bytes 2752512 | tf_op jit(solution)/shard_map/all_to_all | solution.py:1299
  576.1 54.4 %all-to-all-start = ((bf16[16,80,256]{2,1,0:T(8,128)(2,1)}), bf16[16,80,256]{2,1,0:T(8,128)(2,1)S(1)}, u32[]{:S(2)}, u32[]{:S(2)}) async-start(bf16[16,80,256]{2,1,0:T(8,128)(2,1)} %bitcast.45), calls=%async_computation | async-start | bytes 1310720 | tf_op jit(solution)/shard_map/all_to_all | solution.py:1310
  583.4 47.0 %collective-permute-start.83 = (bf16[672,128]{1,0:T(8,128)(2,1)S(1)}, bf16[672,128]{1,0:T(8,128)(2,1)S(1)}, u32[]{:S(2)}, u32[]{:S(2)}) collective-permute-start(bf16[672,128]{1,0:T(8,128)(2,1)S(1)} %reduce_sum.62.refs_3_), channel_id=1, source_target_pairs={{0,8},{2,10},{4,12},{6,14},{8,16},{10,18},{12,20},{14,22},{16,24},... | collective-permute-start | bytes 516104 | tf_op jit(solution)/shard_map/ppermute | solution.py:1040
  585.4 45.1 %collective-permute-start.84 = (bf16[672,128]{1,0:T(8,128)(2,1)S(1)}, bf16[672,128]{1,0:T(8,128)(2,1)S(1)}, u32[]{:S(2)}, u32[]{:S(2)}) collective-permute-start(bf16[672,128]{1,0:T(8,128)(2,1)S(1)} %reduce_sum.62.refs_3_), channel_id=1, source_target_pairs={{0,16},{2,18},{4,20},{6,22},{8,24},{10,26},{12,28},{14,30},{16,0},... | collective-permute-start | bytes 516104 | tf_op jit(solution)/shard_map/ppermute | solution.py:1040
  587.7 42.7 %collective-permute-start.85 = (bf16[672,128]{1,0:T(8,128)(2,1)S(1)}, bf16[672,128]{1,0:T(8,128)(2,1)S(1)}, u32[]{:S(2)}, u32[]{:S(2)}) collective-permute-start(bf16[672,128]{1,0:T(8,128)(2,1)S(1)} %reduce_sum.62.refs_3_), channel_id=1, source_target_pairs={{0,24},{2,26},{4,28},{6,30},{8,0},{10,2},{12,4},{14,6},{16,8},{18,... | collective-permute-start | bytes 516104 | tf_op jit(solution)/shard_map/ppermute | solution.py:1040
  592.3 38.1 %collective-permute-start.81 = (bf16[256,2688]{1,0:T(8,128)(2,1)}, bf16[256,2688]{1,0:T(8,128)(2,1)S(1)}, u32[]{:S(2)}, u32[]{:S(2)}) collective-permute-start(bf16[256,2688]{1,0:T(8,128)(2,1)} %shard_map.412), channel_id=1, source_target_pairs={{0,2},{2,0},{4,6},{6,4},{8,10},{10,8},{12,14},{14,12},{16,18},{18,... | collective-permute-start | bytes 4128776 | tf_op jit(solution)/shard_map/ppermute | solution.py:1040
  642.9 50.0 %all-to-all-start.2 = ((bf16[16,96,384]{2,1,0:T(8,128)(2,1)}), bf16[16,96,384]{2,1,0:T(8,128)(2,1)S(1)}, u32[]{:S(2)}, u32[]{:S(2)}) async-start(bf16[16,96,384]{2,1,0:T(8,128)(2,1)} %pad_maximum_fusion.25), calls=%async_computation.2 | async-start | bytes 2359296 | tf_op jit(solution)/shard_map/all_to_all | solution.py:1342
  650.2 42.7 %collective-permute-start.90 = (bf16[4,672,128]{2,1,0:T(8,128)(2,1)S(1)}, bf16[4,672,128]{2,1,0:T(8,128)(2,1)}, u32[]{:S(2)}, u32[]{:S(2)}) collective-permute-start(bf16[4,672,128]{2,1,0:T(8,128)(2,1)S(1)} %pad_maximum_fusion.33.refs_0_), channel_id=1, source_target_pairs={{0,6},{2,4},{4,2},{6,0},{8,14},{10,12},{12,10},{14,8},{16,22},{18,... | collective-permute-start | bytes 2064392 | tf_op jit(solution)/shard_map/ppermute | solution.py:1040
  650.4 73.0 %collective-permute-start.104 = (bf16[4,672,128]{2,1,0:T(8,128)(2,1)S(1)}, bf16[4,672,128]{2,1,0:T(8,128)(2,1)}, u32[]{:S(2)}, u32[]{:S(2)}) collective-permute-start(bf16[4,672,128]{2,1,0:T(8,128)(2,1)S(1)} %pad_maximum_fusion.33.refs_0_), channel_id=1, source_target_pairs={{0,1},{1,0},{2,3},{3,2},{4,5},{5,4},{6,7},{7,6},{8,9},{9,8},{10,11... | collective-permute-start | bytes 2064392 | tf_op jit(solution)/shard_map/ppermute | solution.py:1043
  722.3 40.2 %collective-permute-start.92 = (bf16[256,2560]{1,0:T(8,128)(2,1)}, bf16[256,2560]{1,0:T(8,128)(2,1)}, u32[]{:S(2)}, u32[]{:S(2)}) collective-permute-start(bf16[256,2560]{1,0:T(8,128)(2,1)} %constant_dynamic-slice_fusion.29), channel_id=1, source_target_pairs={{0,1},{1,0},{2,3},{3,2},{4,5},{5,4},{6,7},{7,6},{8,9},{9,8},{10,11... | collective-permute-start | bytes 3932168 | tf_op jit(solution)/shard_map/ppermute | solution.py:1043
  724.0 37.9 %collective-permute-start.98 = (bf16[4,800,128]{2,1,0:T(8,128)(2,1)S(1)}, bf16[4,800,128]{2,1,0:T(8,128)(2,1)S(1)}, u32[]{:S(2)}, u32[]{:S(2)}) collective-permute-start(bf16[4,800,128]{2,1,0:T(8,128)(2,1)S(1)} %pad_maximum_fusion.31.refs_0_), channel_id=1, source_target_pairs={{0,4},{2,6},{4,0},{6,2},{8,12},{10,14},{12,8},{14,10},{16,20},{18,... | collective-permute-start | bytes 2457608 | tf_op jit(solution)/shard_map/ppermute | solution.py:1040
  724.6 37.4 %collective-permute-start.99 = (bf16[4,800,128]{2,1,0:T(8,128)(2,1)S(1)}, bf16[4,800,128]{2,1,0:T(8,128)(2,1)S(1)}, u32[]{:S(2)}, u32[]{:S(2)}) collective-permute-start(bf16[4,800,128]{2,1,0:T(8,128)(2,1)S(1)} %pad_maximum_fusion.31.refs_0_), channel_id=1, source_target_pairs={{0,6},{2,4},{4,2},{6,0},{8,14},{10,12},{12,10},{14,8},{16,22},{18,... | collective-permute-start | bytes 2457608 | tf_op jit(solution)/shard_map/ppermute | solution.py:1040
  729.4 39.1 %collective-permute-start.91 = (bf16[256,2560]{1,0:T(8,128)(2,1)S(1)}, bf16[256,2560]{1,0:T(8,128)(2,1)}, u32[]{:S(2)}, u32[]{:S(2)}) collective-permute-start(bf16[256,2560]{1,0:T(8,128)(2,1)S(1)} %add_convert_fusion.2), channel_id=1, source_target_pairs={{0,1},{1,0},{2,3},{3,2},{4,5},{5,4},{6,7},{7,6},{8,9},{9,8},{10,11... | collective-permute-start | bytes 3932168 | tf_op jit(solution)/shard_map/ppermute | solution.py:1043
  (243 other events, 2557.8 us)
